TPU v7x, 128 devices: a whole 4x4x4 slice. The times are simulated.
128 devices in a mesh: gx: 8 (over y, x_lo), gz: 16 (over x_hi, z, core).
Axes of the slice: x: 4 (x_hi: 2, x_lo: 2; x = x_hi * 2 + x_lo), y: 4, z: 4, core: 2. Of those that a mesh axis runs over, the one named last changes fastest.
Arguments:
- flow: float32 [4, 512, 1024, 128], P(None, 'gx', 'gz'), may hold values from -16 to 16
- dy_matrix: float32 [128, 128], replicated, may hold values from -0.5 to 0.5
Outputs:
- moments: float32 [40, 512, 128], P(None, 'gx')
All inputs are finite; a program needn't handle non-finite values.
Results may differ from a plain program's by a relative error of at most 0.00012.
Values sent between devices are 32-bit elements; how exact they have to be, the bound alone decides.
No kernel may reach another device: no remote copies, remote signals or barrier semaphores. Data moves between devices by JAX's collectives and lax.ppermute only.
A program may use at most 128 MiB of HBM per device.

v0:
```python
import jax
import jax.numpy as jnp
from jax import lax
from jax.sharding import PartitionSpec as P

coeffs = (0.8, -0.2, 4.0 / 105.0, -1.0 / 280.0)
pair_list = ((0, 0), (0, 1), (0, 2), (1, 1), (1, 2), (2, 2))
triple_list = (
    (0, 0, 0),
    (0, 0, 1),
    (0, 0, 2),
    (0, 1, 1),
    (0, 1, 2),
    (0, 2, 2),
    (1, 1, 1),
    (1, 1, 2),
    (1, 2, 2),
    (2, 2, 2),
)


def extended(value, sides, width, wrap):
    for axis, dim in sides:
        size, length = (lax.axis_size(axis), value.shape[dim])
        up = [(i, (i + 1) % size) for i in range(size if wrap else size - 1)]
        down = [(j, i) for i, j in up]
        last = lax.slice_in_dim(value, length - width, length, axis=dim)
        first = lax.slice_in_dim(value, 0, width, axis=dim)
        before = lax.ppermute(last, axis, up)
        after = lax.ppermute(first, axis, down)
        value = jnp.concatenate([before, value, after], axis=dim)
    return value


def centered(padded, along, length):
    result = jnp.zeros_like(lax.slice_in_dim(padded, 4, 4 + length, axis=along))
    for offset in range(1, 5):
        upper = lax.slice_in_dim(padded, 4 + offset, 4 + offset + length, axis=along)
        lower = lax.slice_in_dim(padded, 4 - offset, 4 - offset + length, axis=along)
        result = result + coeffs[offset - 1] * (upper - lower)
    return result


def moment_sums(fluct, slopes):
    term_list = []
    for left_c, right_c in pair_list:
        term_list.append(fluct[left_c] * fluct[right_c])
    for first_c, second_c, third_c in triple_list:
        term_list.append(fluct[first_c] * fluct[second_c] * fluct[third_c])
    for comp_c in range(3):
        term_list.append(fluct[3] * fluct[comp_c])
    for left_c, right_c in pair_list:
        term_list.append(fluct[3] * (slopes[left_c][right_c] + slopes[right_c][left_c]))
    for left_c, right_c in pair_list:
        term_list.append(
            slopes[left_c][0] * slopes[right_c][0]
            + slopes[left_c][1] * slopes[right_c][1]
            + slopes[left_c][2] * slopes[right_c][2]
        )
    for left_c, right_c in pair_list:
        term_list.append(-(fluct[left_c] * slopes[3][right_c] + fluct[right_c] * slopes[3][left_c]))
    return jnp.stack([jnp.sum(entry_term, axis=1) for entry_term in term_list])


def shards(flow, dy_matrix):
    local_x = flow.shape[1]
    local_z = flow.shape[2]
    span_total = local_z * lax.axis_size("gz")
    averages = lax.psum(jnp.sum(flow, axis=2), "gz") / span_total
    fluct = flow - averages[:, :, None, :]
    x_padded = extended(fluct, (("gx", 1),), 4, False)
    at_inlet = lax.axis_index("gx") == 0
    at_outlet = lax.axis_index("gx") == lax.axis_size("gx") - 1
    left_rim = jnp.where(at_inlet, jnp.flip(fluct[:, :4], axis=1), x_padded[:, :4])
    right_rim = jnp.where(
        at_outlet, jnp.flip(fluct[:, local_x - 4 :], axis=1), x_padded[:, local_x + 4 :]
    )
    x_padded = jnp.concatenate([left_rim, fluct, right_rim], axis=1)
    z_padded = extended(fluct, (("gz", 2),), 4, True)
    slope_x = centered(x_padded, 1, local_x)
    slope_z = centered(z_padded, 2, local_z)
    slope_y = jnp.dot(fluct, dy_matrix.T, precision=lax.Precision.HIGHEST)
    slopes = [(slope_x[comp_c], slope_y[comp_c], slope_z[comp_c]) for comp_c in range(4)]
    local_sums = moment_sums(fluct, slopes)
    merged = lax.psum(local_sums, "gz")
    return jnp.concatenate([averages[:3], merged / span_total], axis=0)


def solution(mesh):
    in_specs = (P(None, "gx", "gz", None), P())
    out_specs = P(None, "gx", None)
    return jax.shard_map(shards, mesh=mesh, in_specs=in_specs, out_specs=out_specs, check_vma=False)
```

profile of v0, /device:TPU:9, one launch (start us, length us, event | category | flops | bytes accessed | tf_op | source)
XLA Modules:
  0.0 436.6 jit_solution(10589142643841623337)
XLA Ops:
  6.5 0.0 copy-start
  6.5 0.0 all-reduce.3.cloned.1.call-start
  6.5 5.4 %reduce_sum.342 = f32[4,64,128]{2,1,0:T(8,128)} reduce(f32[4,64,64,128]{3,2,1,0:T(8,128)} %param.2, f32[]{:T(128)} %constant.10.clone.1), dimensions={2}, to_apply=%region_0.0 | reduce | flops 2064384 | bytes 8519684 | tf_op jit(solution)/shard_map/reduce_sum | solution.py:69
  11.9 0.0 all-reduce.3.cloned.1.call-update
  12.0 0.0 all-reduce.5.cloned.1.call-start
  12.0 139.1 %all-reduce.3.cloned.1.call-done = f32[4,64,128]{2,1,0:T(8,128)} async-done(((f32[4,64,128]{2,1,0:T(8,128)}), f32[4,64,128]{2,1,0:T(8,128)}) %all-reduce.3.cloned.1.call-update) | async-done | bytes 131088 | tf_op jit(solution)/shard_map/psum | solution.py:69
  151.1 0.9 broadcast_multiply_fusion.1
  152.0 0.0 copy-start.4
  152.0 4.6 %broadcast_subtract_fusion = f32[4,64,64,128]{3,2,1,0:T(8,128)S(1)} fusion(f32[4,64,64,128]{3,2,1,0:T(8,128)} %param.2, f32[4,64,128]{2,1,0:T(8,128)S(1)} %broadcast_multiply_fusion.1), kind=kLoop, calls=%fused_computation.58 | loop fusion | flops 2097152 | bytes 16908288 | tf_op jit(solution)/shard_map/sub | solution.py:70
  156.6 0.0 copy-start.1
  156.6 0.1 fusion.50
  156.7 0.2 fusion.51
  156.9 2.2 collective-permute-start
  159.1 3.1 collective-permute-start.1
  162.2 1.2 collective-permute-start.2
  163.4 0.6 collective-permute-start.3
  164.0 0.0 copy-done
  164.0 8.9 %fusion.47 = f32[4,64,64,128]{3,2,1,0:T(8,128)} fusion(f32[4,64,64,128]{3,2,1,0:T(8,128)S(1)} %broadcast_subtract_fusion, f32[128,128]{1,0:T(8,128)S(1)} %copy-done), kind=kOutput, calls=%fused_computation.156 | convolution fusion | flops 3221225472 | bytes 16842752 | tf_op jit(solution)/shard_map/dot_general | solution.py:82
  172.9 0.0 copy-done.1
  172.9 0.0 collective-permute-done
  172.9 0.1 reverse_select_fusion.1
  173.0 10.0 %collective-permute-done.1 = f32[4,4,64,128]{3,2,1,0:T(8,128)S(1)} collective-permute-done((f32[4,4,64,128]{3,2,1,0:T(8,128)S(1)}, f32[4,4,64,128]{3,2,1,0:T(8,128)S(1)}, u32[]{:S(2)}, u32[]{:S(2)}) %collective-permute-start.1) | collective-permute-done | bytes 524320 | tf_op jit(solution)/shard_map/ppermute | solution.py:29
  182.9 0.1 reverse_select_fusion
  183.0 0.0 collective-permute-done.2
  183.0 0.0 collective-permute-done.3
  183.0 70.9 %fusion.19 = (f32[4,64,64,128]{3,2,1,0:T(8,128)}, f32[4,64,64,128]{3,2,1,0:T(8,128)}) fusion(f32[4,4,64,128]{3,2,1,0:T(8,128)S(1)} %reverse_select_fusion, f32[4,4,64,128]{3,2,1,0:T(8,128)S(1)} %reverse_select_fusion.1, f32[4,64,64,128]{3,2,1,0:T(8,128)} %copy-done.1, f32[4,64,4,128]{3,2,1,0:T(4,128)S(1)} %collective-permute-done.3, ...), kind=kLoop, calls=%fused_computation.37 | loop fusion | flops 79691776 | bytes 27262976 | tf_op jit(solution)/shard_map/add | solution.py:40
  253.9 0.0 copy-start.2
  253.9 0.0 slice-start
  253.9 0.0 slice-start.2
  253.9 10.8 %add_reduce_fusion.4 = (f32[64,128]{1,0:T(8,128)S(1)}, f32[64,128]{1,0:T(8,128)S(1)}, f32[64,128]{1,0:T(8,128)S(1)}, f32[64,128]{1,0:T(8,128)S(1)}, f32[64,128]{1,0:T(8,128)S(1)}, /*index=5*/f32[64,128]{1,0:T(8,128)S(1)}) fusion(f32[4,64,64,128]{3,2,1,0:T(8,128)} %get-tuple-element.65, f32[4,64,64,128]{3,2,1,0:T(8,128)} %fusion.47, ...), kind=kLoop, calls=%fused_computation.100 | loop fusion | flops 18825216 | bytes 19070976 | tf_op jit(solution)/shard_map/reduce_sum | solution.py:62
  264.7 0.0 copy-done.2
  264.7 0.0 slice-start.1
  264.7 0.0 slice-start.3
  264.7 11.1 %add_reduce_fusion = (f32[64,128]{1,0:T(8,128)S(1)}, f32[64,128]{1,0:T(8,128)S(1)}, f32[64,128]{1,0:T(8,128)S(1)}, f32[64,128]{1,0:T(8,128)S(1)}, f32[64,128]{1,...) fusion(f32[4,64,64,128]{3,2,1,0:T(8,128)} %fusion.47, ...), kind=kLoop, calls=%fused_computation.96 | loop fusion | flops 23977984 | bytes 25722880 | tf_op jit(solution)/shard_map/reduce_sum | solution.py:62
  275.9 0.0 slice-done
  275.9 0.0 slice-done.2
  275.9 0.0 slice-done.1
  275.9 0.0 slice-done.3
  275.9 5.4 %add_reduce_fusion.2 = (f32[64,128]{1,0:T(8,128)S(1)}, f32[64,128]{1,0:T(8,128)S(1)}, f32[64,128]{1,0:T(8,128)S(1)}, f32[64,128]{1,0:T(8,128)S(1)}, f32[64,128]{...) fusion(f32[4,64,64,128]{3,2,1,0:T(8,128)S(1)} %copy-done.2, ...), kind=kLoop, calls=%fused_computation.98 | loop fusion | flops 18759680 | bytes 21430272 | tf_op jit(solution)/shard_map/reduce_sum | solution.py:62
  281.8 0.0 copy-start.3
  281.8 1.0 copy-done.3
  282.8 0.0 all-reduce.5.cloned.1.call-update
  282.9 0.0 copy-done.4
  282.9 0.0 slice-start.4
  282.9 144.3 %all-reduce.5.cloned.1.call-done = f32[37,64,128]{2,1,0:T(8,128)} async-done(((f32[37,64,128]{2,1,0:T(8,128)}), f32[37,64,128]{2,1,0:T(8,128)}) %all-reduce.5.cloned.1.call-update) | async-done | bytes 1212432 | tf_op jit(solution)/shard_map/psum | solution.py:85
  427.2 1.4 broadcast_multiply_fusion
  428.6 0.0 slice-done.4
  428.6 1.1 pad_maximum_fusion.4
  (39 shorter events, 0.2 us)
Async XLA Ops:
  6.5 157.5 %copy-start = (f32[128,128]{1,0:T(8,128)S(1)}, f32[128,128]{1,0:T(8,128)}, u32[]{:S(2)}) copy-start(f32[128,128]{1,0:T(8,128)} %param.3) | copy-start | bytes 196612
  6.5 144.6 %all-reduce.3.cloned.1.call-start = ((), (), s32[]{:S(2)}) async-start(), calls=%async_computation | async-start | bytes 262144 | tf_op jit(solution)/shard_map/psum | solution.py:69
  12.0 415.2 %all-reduce.5.cloned.1.call-start = ((), (), s32[]{:S(2)}) async-start(), calls=%async_computation.1 | async-start | bytes 2424832 | tf_op jit(solution)/shard_map/psum | solution.py:85
  152.0 130.8 %copy-start.4 = (f32[4,64,128]{2,1,0:T(8,128)}, f32[4,64,128]{2,1,0:T(8,128)S(1)}, u32[]{:S(2)}) copy-start(f32[4,64,128]{2,1,0:T(8,128)S(1)} %broadcast_multiply_fusion.1) | copy-start | bytes 393220
  156.6 16.3 %copy-start.1 = (f32[4,64,64,128]{3,2,1,0:T(8,128)}, f32[4,64,64,128]{3,2,1,0:T(8,128)S(1)}, u32[]{:S(2)}) copy-start(f32[4,64,64,128]{3,2,1,0:T(8,128)S(1)} %broadcast_subtract_fusion) | copy-start | bytes 25165828
  156.9 16.0 %collective-permute-start = (f32[4,4,64,128]{3,2,1,0:T(8,128)S(1)}, f32[4,4,64,128]{3,2,1,0:T(8,128)S(1)}, u32[]{:S(2)}, u32[]{:S(2)}) collective-permute-start(f32[4,4,64,128]{3,2,1,0:T(8,128)S(1)} %get-tuple-element.66), channel_id=1, source_target_pairs={{16,0},{32,16},{48,32},{64,48},{80,64},{96,80},{112,96},{17,1},{33... | collective-permute-start | bytes 1572872 | tf_op jit(solution)/shard_map/ppermute | solution.py:30
  159.1 23.8 %collective-permute-start.1 = (f32[4,4,64,128]{3,2,1,0:T(8,128)S(1)}, f32[4,4,64,128]{3,2,1,0:T(8,128)S(1)}, u32[]{:S(2)}, u32[]{:S(2)}) collective-permute-start(f32[4,4,64,128]{3,2,1,0:T(8,128)S(1)} %get-tuple-element.67), channel_id=1, source_target_pairs={{0,16},{16,32},{32,48},{48,64},{64,80},{80,96},{96,112},{1,17},{17... | collective-permute-start | bytes 1572872 | tf_op jit(solution)/shard_map/ppermute | solution.py:29
  162.2 20.8 %collective-permute-start.2 = (f32[4,64,4,128]{3,2,1,0:T(4,128)S(1)}, f32[4,64,4,128]{3,2,1,0:T(4,128)S(1)}, u32[]{:S(2)}, u32[]{:S(2)}) collective-permute-start(f32[4,64,4,128]{3,2,1,0:T(4,128)S(1)} %get-tuple-element.68), channel_id=1, source_target_pairs={{1,0},{2,1},{3,2},{4,3},{5,4},{6,5},{7,6},{8,7},{9,8},{10,9},{11,1... | collective-permute-start | bytes 1572872 | tf_op jit(solution)/shard_map/ppermute | solution.py:30
  163.4 19.6 %collective-permute-start.3 = (f32[4,64,4,128]{3,2,1,0:T(4,128)S(1)}, f32[4,64,4,128]{3,2,1,0:T(4,128)S(1)}, u32[]{:S(2)}, u32[]{:S(2)}) collective-permute-start(f32[4,64,4,128]{3,2,1,0:T(4,128)S(1)} %get-tuple-element.69), channel_id=1, source_target_pairs={{0,1},{1,2},{2,3},{3,4},{4,5},{5,6},{6,7},{7,8},{8,9},{9,10},{10,1... | collective-permute-start | bytes 1572872 | tf_op jit(solution)/shard_map/ppermute | solution.py:29
  253.9 10.8 %copy-start.2 = (f32[4,64,64,128]{3,2,1,0:T(8,128)S(1)}, f32[4,64,64,128]{3,2,1,0:T(8,128)}, u32[]{:S(2)}) copy-start(f32[4,64,64,128]{3,2,1,0:T(8,128)} %get-tuple-element.64) | copy-start | bytes 25165828
  253.9 22.0 %slice-start = ((s8[8388608]{0:T(1024)(128)(4,1)}), s8[4194304]{0:T(1024)(128)(4,1)S(1)}, s32[]{:S(2)}) async-start(s8[8388608]{0:T(1024)(128)(4,1)} %bitcast.238), calls=%async_computation.2 | async-start | bytes 8388608
  253.9 22.0 %slice-start.2 = ((s8[8388608]{0:T(1024)(128)(4,1)}), s8[4194304]{0:T(1024)(128)(4,1)S(1)}, s32[]{:S(2)}) async-start(s8[8388608]{0:T(1024)(128)(4,1)} %bitcast.240), calls=%async_computation.4 | async-start | bytes 8388608
  264.7 11.2 %slice-start.1 = ((s8[8388608]{0:T(1024)(128)(4,1)}), s8[4194304]{0:T(1024)(128)(4,1)S(1)}, s32[]{:S(2)}) async-start(s8[8388608]{0:T(1024)(128)(4,1)} %bitcast.238), calls=%async_computation.3 | async-start | bytes 8388608
  264.7 11.2 %slice-start.3 = ((s8[8388608]{0:T(1024)(128)(4,1)}), s8[4194304]{0:T(1024)(128)(4,1)S(1)}, s32[]{:S(2)}) async-start(s8[8388608]{0:T(1024)(128)(4,1)} %bitcast.240), calls=%async_computation.5 | async-start | bytes 8388608
  281.8 1.0 copy-start.3
  282.9 145.7 %slice-start.4 = ((f32[4,64,128]{2,1,0:T(8,128)}), f32[3,64,128]{2,1,0:T(8,128)S(1)}, s32[]{:S(2)}) async-start(f32[4,64,128]{2,1,0:T(8,128)} %copy-done.4), calls=%async_computation.6 | async-start | bytes 196608 | tf_op jit(solution)/shard_map/slice | solution.py:86
Sparse Core Ops, SparseCore 0:
  12.1 138.9 all-reduce.2
  283.0 144.1 all-reduce.4
where the time goes:
time: 440 us; the launch traced here: 437 us
  waiting for transfers between devices  293 us (67%)
  other arithmetic  112 us (25%)
  between operations  13.9 us (3%)
  matrix products  8.87 us (2%)
  starting transfers between devices  7.14 us (2%)
    psum x1, waiting for transfers between devices, shards(): merged = lax.psum(local_sums, 'gz')  144 us
    psum x1, waiting for transfers between devices, shards(): averages = lax.psum(jnp.sum(flow, axis=2), 'gz') / span_total  139 us
    add x1, other arithmetic, centered(): result = result + coeffs[offset - 1] * (upper - lower)  70.9 us
    reduce_sum x3, other arithmetic, moment_sums(): return jnp.stack([jnp.sum(entry_term, axis=1) for entry_term in term_list])  27.3 us
    ppermute x2, waiting for transfers between devices, extended(): before = lax.ppermute(last, axis, up)  9.97 us
    dot_general x1, matrix products, shards(): slope_y = jnp.dot(fluct, dy_matrix.T, precision=lax.Precision.HIGHEST)  8.87 us
  transfers between devices with their start and end apart: 6, of which 3 were waited for; matrix products, arithmetic and copies ran while one was open for 2% of the time, Pallas kernels for 0%

commit v1 on v0

v1 whole, which is shorter than its diff:
```python
import functools

import jax
import jax.numpy as jnp
from jax import lax
from jax.experimental import pallas as pl
from jax.experimental.pallas import tpu as pltpu
from jax.sharding import Mesh, PartitionSpec as P

F32 = jnp.float32
BF16 = jnp.bfloat16
lead = 4.0 / 5.0
ratios = (1.0, -0.25, 1.0 / 21.0, -1.0 / 224.0)
pairs = ((0, 0), (0, 1), (0, 2), (1, 1), (1, 2), (2, 2))
triples = (
    (0, 0, 0), (0, 0, 1), (0, 0, 2), (0, 1, 1), (0, 1, 2),
    (0, 2, 2), (1, 1, 1), (1, 1, 2), (1, 2, 2), (2, 2, 2),
)
MEAN, DXM, ZSUM, UU, UUU, PU, PG, GG, UG = 0, 4, 8, 11, 17, 27, 30, 36, 42
STATE = 47
OUT = 40
NBASE = 19
NSLOPE = 22
GXA, ZA, CA = "gx", ("xh", "z", "c"), "c"


def combine(left, right, count, dmat, put):
    half = [0.5 * (left(MEAN + c) - right(MEAN + c)) for c in range(4)]
    gx = [0.5 * (left(DXM + c) - right(DXM + c)) for c in range(4)]
    gy = [
        jnp.dot(h, dmat, precision=lax.Precision.HIGHEST, preferred_element_type=F32) for h in half
    ]
    dz = [half[3] * (left(ZSUM + c) - right(ZSUM + c)) for c in range(3)]
    both = float(2 * count)
    nh = [both * h for h in half]
    for c in range(4):
        put(MEAN + c, 0.5 * (left(MEAN + c) + right(MEAN + c)))
        put(DXM + c, 0.5 * (left(DXM + c) + right(DXM + c)))
    for c in range(3):
        put(ZSUM + c, left(ZSUM + c) + right(ZSUM + c))
    gap = {}
    for k, (i, j) in enumerate(pairs):
        a, b = left(UU + k), right(UU + k)
        gap[i, j] = gap[j, i] = a - b
        put(UU + k, (a + b) + nh[i] * half[j])
    for k, (i, j, l) in enumerate(triples):
        fix = half[i] * gap[j, l] + half[j] * gap[i, l] + half[l] * gap[i, j]
        put(UUU + k, (left(UUU + k) + right(UUU + k)) + fix)
    for c in range(3):
        put(PU + c, (left(PU + c) + right(PU + c)) + nh[3] * half[c])
    fixes = (
        2.0 * nh[3] * gx[0],
        nh[3] * (gy[0] + gx[1]),
        dz[0] + nh[3] * gx[2],
        2.0 * nh[3] * gy[1],
        dz[1] + nh[3] * gy[2],
        2.0 * dz[2],
    )
    for k in range(6):
        put(PG + k, (left(PG + k) + right(PG + k)) + fixes[k])
    for k, (i, j) in enumerate(pairs):
        fix = both * (gx[i] * gx[j] + gy[i] * gy[j])
        put(GG + k, (left(GG + k) + right(GG + k)) + fix)
    fixes = (
        -2.0 * nh[0] * gx[3],
        -(nh[0] * gy[3] + nh[1] * gx[3]),
        dz[0] - nh[2] * gx[3],
        -2.0 * nh[1] * gy[3],
        dz[1] - nh[2] * gy[3],
    )
    for k in range(5):
        put(UG + k, (left(UG + k) + right(UG + k)) + fixes[k])


def base_kernel(flow, mean, base, acc):
    rows, depth = flow.shape[1], flow.shape[2]

    def one(x, _):
        centre = []
        for c in range(4):
            m = jnp.sum(flow[c, x], axis=0, keepdims=True) * (1.0 / depth)
            mean[c, pl.ds(x, 1), :] = m
            centre.append(m)
        total = [None] * NBASE

        def add(k, v):
            total[k] = v if total[k] is None else total[k] + v

        for b in range(depth // 8):
            f = [flow[c, x, pl.ds(8 * b, 8), :] - centre[c] for c in range(4)]
            prod = {}
            for k, (i, j) in enumerate(pairs):
                prod[i, j] = f[i] * f[j]
                add(k, prod[i, j])
            for k, (i, j, l) in enumerate(triples):
                add(6 + k, prod[i, j] * f[l])
            for c in range(3):
                add(16 + c, f[3] * f[c])
        for k in range(NBASE):
            acc[pl.ds(pl.multiple_of(k * 8 * rows + 8 * x, 8), 8), :] = total[k]
        return 0

    lax.fori_loop(0, rows, one, 0)
    for k in range(NBASE):
        base[k] = sum(acc[pl.ds(k * 8 * rows + s, rows, stride=8), :] for s in range(8))


def base_moments(flow):
    _, lx, lz, ny = flow.shape
    step = 8
    return pl.pallas_call(
        base_kernel,
        grid=(lx // step,),
        in_specs=[pl.BlockSpec((4, step, lz, ny), lambda i: (0, i, 0, 0))],
        out_specs=[
            pl.BlockSpec((4, step, ny), lambda i: (0, i, 0)),
            pl.BlockSpec((NBASE, step, ny), lambda i: (0, i, 0)),
        ],
        out_shape=[
            jax.ShapeDtypeStruct((4, lx, ny), F32),
            jax.ShapeDtypeStruct((NBASE, lx, ny), F32),
        ],
        scratch_shapes=[pltpu.VMEM((NBASE * 8 * step, ny), F32)],
        compiler_params=pltpu.CompilerParams(vmem_limit_bytes=24 * 2**20),
        cost_estimate=pl.CostEstimate(
            flops=50 * flow.size, bytes_accessed=4 * flow.size, transcendentals=0
        ),
        name="base_moments",
    )(flow)


def slope_kernel(
    flow, xl, xr, zl, zr, mean, base, dy, keep, send, raw, acc, mpad, dxm, weights, ysl, sems
):
    _, lx, lz, ny = flow.shape
    half = lx // 2
    core = lax.axis_index(CA)
    gi = lax.axis_index(GXA)
    gn = lax.axis_size(GXA)
    parts = 8
    piece = lx // parts
    first = half * (1 - core)

    def body_copy(k):
        at = lax.rem(first + piece * k, lx)
        return pltpu.make_async_copy(
            flow.at[:, pl.ds(at, piece)],
            raw.at[:, pl.ds(4 + at, piece), pl.ds(8, lz)],
            sems.at[k],
        )

    def rim_copies(side):
        if side == 0:
            plain = pltpu.make_async_copy(
                xl, raw.at[:, pl.ds(0, 4), pl.ds(8, lz)], sems.at[parts]
            )
            mirror = [
                pltpu.make_async_copy(
                    flow.at[:, pl.ds(3 - j, 1)],
                    raw.at[:, pl.ds(j, 1), pl.ds(8, lz)],
                    sems.at[parts + 2 + j],
                )
                for j in range(4)
            ]
        else:
            plain = pltpu.make_async_copy(
                xr, raw.at[:, pl.ds(4 + lx, 4), pl.ds(8, lz)], sems.at[parts + 1]
            )
            mirror = [
                pltpu.make_async_copy(
                    flow.at[:, pl.ds(lx - 1 - j, 1)],
                    raw.at[:, pl.ds(4 + lx + j, 1), pl.ds(8, lz)],
                    sems.at[parts + 6 + j],
                )
                for j in range(4)
            ]
        return plain, mirror

    ends = (gi == 0, gi == gn - 1)
    for side in range(2):
        plain, mirror = rim_copies(side)

        @pl.when(ends[side])
        def _():
            for c in mirror:
                c.start()

        @pl.when(jnp.logical_not(ends[side]))
        def _():
            plain.start()

    for k in range(parts):
        body_copy(k).start()

    d = dy[...].T * (1.0 / lead)
    dhi = d.astype(BF16)
    dlo = (d - dhi.astype(F32)).astype(BF16)
    weights[pl.ds(0, ny), pl.ds(0, ny)] = dhi
    weights[pl.ds(0, ny), pl.ds(ny, ny)] = dlo
    weights[pl.ds(ny, ny), pl.ds(0, ny)] = dhi
    weights[pl.ds(ny, ny), pl.ds(ny, ny)] = jnp.zeros_like(dlo)

    for side in range(2):
        plain, mirror = rim_copies(side)

        @pl.when(ends[side])
        def _():
            for c in mirror:
                c.wait()

        @pl.when(jnp.logical_not(ends[side]))
        def _():
            plain.wait()

    for c in range(4):
        mpad[c, pl.ds(8, lx), :] = mean[c]
        for j in range(4):
            for src, dst in ((j, 4 + j), (4 + lx + j, 8 + lx + j)):
                mpad[c, pl.ds(dst, 1), :] = jnp.sum(
                    raw[c, src, pl.ds(8, lz), :], axis=0, keepdims=True
                ) * (1.0 / lz)
    for c in range(4):
        out = None
        for k in range(4):
            diff = mpad[c, pl.ds(9 + k, lx), :] - mpad[c, pl.ds(7 - k, lx), :]
            out = diff if out is None else out + ratios[k] * diff
        dxm[c] = out

    for k in range(parts):
        body_copy(k).wait()

    def one(i, _):
        x = lax.rem(i + first, lx)
        for c in range(3):
            raw[c, x + 4, pl.ds(4, 4), :] = zl[c, x]
            raw[c, x + 4, pl.ds(8 + lz, 4), :] = zr[c, x]
        centre = [mean[c, pl.ds(x, 1), :] for c in range(4)]
        shift = [dxm[c, pl.ds(x, 1), :] for c in range(4)]
        for c in range(4):
            a = raw[c, x + 4, pl.ds(8, lz), :] - centre[c]
            hi = a.astype(BF16)
            lo = (a - hi.astype(F32)).astype(BF16)
            y = jnp.dot(
                jnp.concatenate([hi, lo], axis=1), weights[...], preferred_element_type=F32
            )
            ysl[c] = y[:, :ny] + y[:, ny:]
        total = [None] * NSLOPE

        def add(k, v):
            total[k] = v if total[k] is None else total[k] + v

        for b in range(lz // 8):
            at = 8 + 8 * b
            g = [[None] * 3 for _ in range(4)]
            for c in range(4):
                out = None
                for k in range(4):
                    diff = raw[c, x + 5 + k, pl.ds(at, 8), :] - raw[c, x + 3 - k, pl.ds(at, 8), :]
                    out = diff if out is None else out + ratios[k] * diff
                g[c][0] = out - shift[c]
                g[c][1] = ysl[c, pl.ds(8 * b, 8), :]
            for c in range(3):
                out = None
                for k in range(4):
                    diff = (
                        raw[c, x + 4, pl.ds(at + 1 + k, 8), :]
                        - raw[c, x + 4, pl.ds(at - 1 - k, 8), :]
                    )
                    out = diff if out is None else out + ratios[k] * diff
                g[c][2] = out
            u = [raw[c, x + 4, pl.ds(at, 8), :] - centre[c] for c in range(4)]
            p = u[3]
            for c in range(3):
                add(c, g[c][2])
            add(3, p * g[0][0])
            add(4, p * (g[0][1] + g[1][0]))
            add(5, p * g[0][2])
            add(6, p * g[2][0])
            add(7, p * g[1][1])
            add(8, p * g[1][2])
            add(9, p * g[2][1])
            add(10, p * g[2][2])
            for k, (i2, j2) in enumerate(pairs):
                for dim in range(3):
                    add(11 + k, g[i2][dim] * g[j2][dim])
            add(17, u[0] * g[3][0])
            add(18, u[0] * g[3][1] + u[1] * g[3][0])
            add(19, u[1] * g[3][1])
            add(20, u[2] * g[3][0])
            add(21, u[2] * g[3][1])
        for k in range(NSLOPE):
            acc[pl.ds(pl.multiple_of(k * 8 * lx + 8 * i, 8), 8), :] = total[k]
        return 0

    lax.fori_loop(0, lx, one, 0)

    for part, out in ((0, send), (1, keep)):
        src = half * (1 - core) if part == 0 else half * core
        src = pl.multiple_of(src, 8)

        def total(k):
            at = k * 8 * lx + 8 * half * part
            return sum(acc[pl.ds(at + s, half, stride=8), :] for s in range(8))

        for c in range(4):
            out[MEAN + c] = mean[c, pl.ds(src, half), :]
            out[DXM + c] = dxm[c, pl.ds(src, half), :]
        for k in range(NBASE):
            out[UU + k] = base[k, pl.ds(src, half), :]
        for c in range(3):
            out[ZSUM + c] = total(c)
        s02, s12 = total(5), total(8)
        out[PG + 0] = 2.0 * total(3)
        out[PG + 1] = total(4)
        out[PG + 2] = s02 + total(6)
        out[PG + 3] = 2.0 * total(7)
        out[PG + 4] = s12 + total(9)
        out[PG + 5] = 2.0 * total(10)
        for k in range(6):
            out[GG + k] = total(11 + k)
        out[UG + 0] = -2.0 * total(17)
        out[UG + 1] = -total(18)
        out[UG + 2] = s02 - total(20)
        out[UG + 3] = -2.0 * total(19)
        out[UG + 4] = s12 - total(21)


def slope_moments(flow, xl, xr, zl, zr, mean, base, dy):
    _, lx, lz, ny = flow.shape
    vm = pl.BlockSpec(memory_space=pltpu.VMEM)
    hb = pl.BlockSpec(memory_space=pl.ANY)
    shape = jax.ShapeDtypeStruct((STATE, lx // 2, ny), F32)
    return pl.pallas_call(
        slope_kernel,
        in_specs=[hb, hb, hb, vm, vm, vm, vm, vm],
        out_specs=[vm, vm],
        out_shape=[shape, shape],
        scratch_shapes=[
            pltpu.VMEM((4, lx + 8, lz + 16, ny), F32),
            pltpu.VMEM((NSLOPE * 8 * lx, ny), F32),
            pltpu.VMEM((4, lx + 16, ny), F32),
            pltpu.VMEM((4, lx, ny), F32),
            pltpu.VMEM((2 * ny, 2 * ny), BF16),
            pltpu.VMEM((4, lz, ny), F32),
            pltpu.SemaphoreType.DMA((18,)),
        ],
        compiler_params=pltpu.CompilerParams(vmem_limit_bytes=40 * 2**20),
        cost_estimate=pl.CostEstimate(
            flops=200 * flow.size, bytes_accessed=4 * flow.size, transcendentals=0
        ),
        name="slope_moments",
    )(flow, xl, xr, zl, zr, mean, base, dy)


def core_kernel(count, keep, got, dy, own, up, down, far):
    d = dy[...].T * (1.0 / lead)
    rows = own.shape[1]
    zi = lax.axis_index("z")
    zn = lax.axis_size("z")
    for k, out in ((0, own), (1, up), (zn - 1, down), (2, far)):
        at = pl.multiple_of(rows * lax.rem(zi + k, zn), 8)

        def put(f, v, out=out):
            out[f] = v

        combine(
            lambda f, at=at: keep[f, pl.ds(at, rows), :],
            lambda f, at=at: got[f, pl.ds(at, rows), :],
            count, d, put,
        )


def span_kernel(count, own, one, two, three, dy, out, left, right):
    d = dy[...].T * (1.0 / lead)

    def put_to(ref):
        def put(f, v):
            ref[f] = v
        return put

    combine(lambda f: own[f], lambda f: one[f], count, d, put_to(left))
    combine(lambda f: two[f], lambda f: three[f], count, d, put_to(right))
    combine(lambda f: left[f], lambda f: right[f], 2 * count, d, put_to(out))


def last_kernel(count, mine, other, dy, out, state):
    d = dy[...].T * (1.0 / lead)

    def put(f, v):
        state[f] = v

    combine(lambda f: mine[f], lambda f: other[f], count, d, put)
    scale = 1.0 / (2 * count)
    for c in range(3):
        out[c] = state[MEAN + c]
    for k in range(NBASE):
        out[3 + k] = state[UU + k] * scale
    for k in range(6):
        out[22 + k] = state[PG + k] * (scale * lead)
        out[28 + k] = state[GG + k] * (scale * lead * lead)
    for k in range(5):
        out[34 + k] = state[UG + k] * (scale * lead)
    out[39] = state[PG + 5] * (scale * lead)


def place_kernel(*refs):
    ins, out = refs[:-1], refs[-1]
    rows = ins[0].shape[1]
    zi = lax.axis_index("z")
    zn = lax.axis_size("z")
    core = lax.axis_index(CA)
    for k, ref in enumerate(ins):
        side, step = divmod(k, zn)
        c = core if side == 0 else 1 - core
        at = pl.multiple_of(rows * (zn * c + lax.rem(zi + zn - step, zn)), 8)
        out[:, pl.ds(at, rows), :] = ref[...]


def small_call(kernel, outs, scratch, name, *args):
    vm = pl.BlockSpec(memory_space=pltpu.VMEM)
    return pl.pallas_call(
        kernel,
        in_specs=[vm] * len(args),
        out_specs=[vm] * len(outs),
        out_shape=[jax.ShapeDtypeStruct(s, F32) for s in outs],
        scratch_shapes=[pltpu.VMEM(s, F32) for s in scratch],
        compiler_params=pltpu.CompilerParams(vmem_limit_bytes=24 * 2**20),
        name=name,
    )(*args)


def send(value, axis, step):
    size = lax.axis_size(axis)
    return lax.ppermute(value, axis, [(i, (i + step) % size) for i in range(size)])


def shards(flow, dy):
    _, lx, lz, ny = flow.shape
    gn = lax.axis_size(GXA)
    zn = lax.axis_size("z")
    up = [(i, i + 1) for i in range(gn - 1)]
    down = [(i + 1, i) for i in range(gn - 1)]
    with jax.named_scope("rims"):
        xl = lax.ppermute(flow[:, lx - 4 :], GXA, up)
        xr = lax.ppermute(flow[:, :4], GXA, down)
        zl = send(flow[:, :, lz - 4 :], ZA, 1)
        zr = send(flow[:, :, :4], ZA, -1)
    mean, base = base_moments(flow)
    keep, give = slope_moments(flow, xl, xr, zl, zr, mean, base, dy)
    with jax.named_scope("core_exchange"):
        got = send(give, CA, 1)
    rows = lx // 2 // zn
    piece = (STATE, rows, ny)
    own, up1, down1, far = small_call(
        functools.partial(core_kernel, lz), [piece] * 4, [], "core_merge", keep, got, dy
    )
    with jax.named_scope("span_exchange"):
        one = send(up1, "z", 1)
        three = send(down1, "z", -1)
        two = send(far, "z", 2)
    (part,) = small_call(
        functools.partial(span_kernel, 2 * lz),
        [piece], [piece, piece], "span_merge", own, one, two, three, dy,
    )
    with jax.named_scope("x_exchange"):
        other = send(part, "xh", 1)
    (done,) = small_call(
        functools.partial(last_kernel, 2 * zn * lz),
        [(OUT, rows, ny)], [piece], "last_merge", part, other, dy,
    )
    with jax.named_scope("spread"):
        mine = [done] + [send(done, "z", k) for k in (1, 2, 3)]
        theirs = [send(v, CA, 1) for v in mine]
    (out,) = small_call(place_kernel, [(OUT, lx, ny)], [], "place", *mine, *theirs)
    return out


def solution(mesh):
    gx, gz = mesh.shape["gx"], mesh.shape["gz"]
    fine = Mesh(mesh.devices.reshape(gx, 2, gz // 4, 2), (GXA,) + ZA)
    return jax.shard_map(
        shards,
        mesh=fine,
        in_specs=(P(None, GXA, ZA, None), P()),
        out_specs=P(None, GXA, None),
        check_vma=False,
    )
```

time: 440 us -> 99.4 us (0.23)
  waiting for transfers between devices: 293 us -> 26.1 us
  other arithmetic: 112 us -> 0 us
  starting transfers between devices: 7.14 us -> 37.7 us
  Pallas kernels: 0 us -> 28.5 us
  between operations: 13.9 us -> 0.1 us
  matrix products: 8.87 us -> 0 us
  local copies, waits for them, and re-layouts: 1.47 us -> 6.46 us
    psum x2 -> x0, waiting for transfers between devices: 283 us -> none  [the longest x1 144 us: shards(): merged = lax.psum(local_sums, 'gz')]
    add x1 -> x0, other arithmetic: 70.9 us -> none  [centered(): result = result + coeffs[offset - 1] * (upper - lower)]
    reduce_sum x4 -> x0, other arithmetic: 32.7 us -> none  [the longest x3 27.3 us: moment_sums(): return jnp.stack([jnp.sum(entry_term, axis=1) for entry_term in term_list])]
    ppermute x4 -> x16, starting transfers between devices: 7.1 us -> 37.7 us  [the longest x14 32.4 us: send(): lax.ppermute(value, axis, [(i, (i + step) % size) for i in range(size)])]
    pallas_call x0 -> x6, Pallas kernels: none -> 28.5 us  [the longest x1 19.3 us: slope_moments(): pl.pallas_call(slope_kernel, in_specs=[hb, hb, hb, vm, vm, vm, vm, vm], o...]
    ppermute x4 -> x16, waiting for transfers between devices: 9.98 us -> 26.1 us  [the longest x14 19.8 us: send(): lax.ppermute(value, axis, [(i, (i + step) % size) for i in range(size)])]
    dot_general x1 -> x0, matrix products: 8.87 us -> none  [shards(): slope_y = jnp.dot(fluct, dy_matrix.T, precision=lax.Precision.HIGHEST)]
    sub x1 -> x0, other arithmetic: 4.58 us -> none  [shards(): fluct = flow - averages[:, :, None, :]]
  transfers between devices with their start and end apart: 6 -> 16, of which waited for: 3 -> 8; matrix products, arithmetic and copies ran while one was open for 2% -> 2% of each run, Pallas kernels for 0% -> 6%
where the time goes in v1:
time: 99.4 us; the launch traced here: 98.9 us
  starting transfers between devices  37.7 us (38%)
  Pallas kernels  28.5 us (29%)
  waiting for transfers between devices  26.1 us (26%)
  local copies, waits for them, and re-layouts  6.46 us (6%)
    ppermute x14, starting transfers between devices, send(): lax.ppermute(value, axis, [(i, (i + step) % size) for i in range(size)])  32.4 us
    ppermute x14, waiting for transfers between devices, send(): lax.ppermute(value, axis, [(i, (i + step) % size) for i in range(size)])  19.8 us
    pallas_call x1, Pallas kernels, slope_moments(): pl.pallas_call(slope_kernel, in_specs=[hb, hb, hb, vm, vm, vm, vm, vm], o...  19.3 us
    ppermute x1, waiting for transfers between devices, shards(): xl = lax.ppermute(flow[:, lx - 4:], GXA, up)  6.33 us
    pallas_call x1, Pallas kernels, base_moments(): pl.pallas_call(base_kernel, grid=(lx // step,), in_specs=[pl.BlockSpec((4...  5.69 us
    pallas_call x4, Pallas kernels, small_call(): pl.pallas_call(kernel, in_specs=[vm] * len(args), out_specs=[vm] * len(ou...  3.48 us
    unnamed x6, local copies, waits for them, and re-layouts  3.39 us
    ppermute x1, starting transfers between devices, shards(): xr = lax.ppermute(flow[:, :4], GXA, down)  3.01 us
  transfers between devices with their start and end apart: 16, of which 8 were waited for; matrix products, arithmetic and copies ran while one was open for 2% of the time, Pallas kernels for 6%

profile of v1, /device:TPU:9, one launch (start us, length us, event | category | flops | bytes accessed | tf_op | source)
XLA Modules:
  0.0 98.9 jit_solution(8591145852330716199)
XLA Ops:
  0.0 0.0 copy-start.2
  0.0 1.3 %fusion.1 = (f32[4,4,64,128]{3,2,1,0:T(8,128)S(1)}, f32[4,4,64,128]{3,2,1,0:T(8,128)S(1)}) fusion(f32[4,64,64,128]{3,2,1,0:T(8,128)} %flow.3), kind=kLoop, calls=%fused_computation.1 | loop fusion | bytes 2097152 | tf_op jit(solution)/shard_map/rims/slice | solution.py:445
  1.3 3.0 %collective-permute-start.1 = (f32[4,4,64,128]{3,2,1,0:T(8,128)S(1)}, f32[4,4,64,128]{3,2,1,0:T(8,128)S(1)}, u32[]{:S(2)}, u32[]{:S(2)}) collective-permute-start(f32[4,4,64,128]{3,2,1,0:T(8,128)S(1)} %get-tuple-element.23), channel_id=1, source_target_pairs={{16,0},{32,16},{48,32},{64,48},{80,64},{96,80},{112,96},{17,1},{33... | collective-permute-start | bytes 1572872 | tf_op jit(solution)/shard_map/rims/ppermute | solution.py:445
  4.4 2.3 %collective-permute-start = (f32[4,4,64,128]{3,2,1,0:T(8,128)S(1)}, f32[4,4,64,128]{3,2,1,0:T(8,128)S(1)}, u32[]{:S(2)}, u32[]{:S(2)}) collective-permute-start(f32[4,4,64,128]{3,2,1,0:T(8,128)S(1)} %get-tuple-element.24), channel_id=1, source_target_pairs={{0,16},{16,32},{32,48},{48,64},{64,80},{80,96},{96,112},{1,17},{17... | collective-permute-start | bytes 1572872 | tf_op jit(solution)/shard_map/rims/ppermute | solution.py:444
  6.6 1.7 %fusion = (f32[4,64,4,128]{3,2,1,0:T(4,128)S(1)}, f32[4,64,4,128]{3,2,1,0:T(4,128)S(1)}) fusion(f32[4,64,64,128]{3,2,1,0:T(8,128)} %flow.3), kind=kLoop, calls=%fused_computation | loop fusion | bytes 2097152 | tf_op jit(solution)/shard_map/rims/slice | solution.py:447
  8.4 1.3 %collective-permute-start.3 = (f32[4,64,4,128]{3,2,1,0:T(4,128)S(1)}, f32[4,64,4,128]{3,2,1,0:T(4,128)S(1)}, u32[]{:S(2)}, u32[]{:S(2)}) collective-permute-start(f32[4,64,4,128]{3,2,1,0:T(4,128)S(1)} %get-tuple-element.21), channel_id=1, source_target_pairs={{0,15},{1,0},{2,1},{3,2},{4,3},{5,4},{6,5},{7,6},{8,7},{9,8},{10,9... | collective-permute-start | bytes 1572872 | tf_op jit(solution)/shard_map/rims/ppermute | solution.py:434
  9.7 1.6 %collective-permute-start.2 = (f32[4,64,4,128]{3,2,1,0:T(4,128)S(1)}, f32[4,64,4,128]{3,2,1,0:T(4,128)S(1)}, u32[]{:S(2)}, u32[]{:S(2)}) collective-permute-start(f32[4,64,4,128]{3,2,1,0:T(4,128)S(1)} %get-tuple-element.22), channel_id=1, source_target_pairs={{0,1},{1,2},{2,3},{3,4},{4,5},{5,6},{6,7},{7,8},{8,9},{9,10},{10,1... | collective-permute-start | bytes 1572872 | tf_op jit(solution)/shard_map/rims/ppermute | solution.py:434
  11.3 0.0 copy-start
  11.3 3.4 %copy-done = f32[4,64,64,128]{3,2,1,0:T(8,128)S(1)} copy-done((f32[4,64,64,128]{3,2,1,0:T(8,128)S(1)}, f32[4,64,64,128]{3,2,1,0:T(8,128)}, u32[]{:S(2)}) %copy-start) | copy-done | bytes 8388632
  14.7 0.0 copy-start.1
  14.7 5.7 %base_moments.1 = (f32[4,64,128]{2,1,0:T(8,128)S(1)}, f32[19,64,128]{2,1,0:T(8,128)S(1)}) custom-call(f32[4,64,64,128]{3,2,1,0:T(8,128)S(1)} %copy-done), custom_call_target="tpu_custom_call" | custom-call | flops 104857600 | bytes 8388608 | tf_op jit(solution)/shard_map/base_moments/pallas_call | solution.py:111
  20.4 0.0 collective-permute-done.1.xr
  20.4 6.3 %collective-permute-done.xl = f32[4,4,64,128]{3,2,1,0:T(8,128)S(1)} collective-permute-done((f32[4,4,64,128]{3,2,1,0:T(8,128)S(1)}, f32[4,4,64,128]{3,2,1,0:T(8,128)S(1)}, u32[]{:S(2)}, u32[]{:S(2)}) %collective-permute-start) | collective-permute-done | bytes 524320 | tf_op jit(solution)/shard_map/rims/ppermute | solution.py:444
  26.7 0.0 collective-permute-done.3.zr
  26.7 0.0 collective-permute-done.2.zl
  26.7 0.0 copy-done.2
  26.7 0.0 copy-done.1
  26.7 19.3 %slope_moments.1 = (f32[47,32,128]{2,1,0:T(8,128)S(1)}, f32[47,32,128]{2,1,0:T(8,128)S(1)}) custom-call(f32[4,64,64,128]{3,2,1,0:T(8,128)S(1)} %copy-done.1, f32[4,4,64,128]{3,2,1,0:T(8,128)S(1)} %collective-permute-done.xl, f32[4,4,64,128]{3,2,1,0:T(8,128)S(1)} %collective-permute-done.1.xr, f32[4,64,4,128]{3,2,1,0:T(4,128)S(1)} %collective-permute-done.2.zl, ...), custom_call_target="tpu_custom_call" | custom-call | flops 419430400 | bytes 8388608 | tf_op jit(solution)/shard_map/slope_moments/pallas_call | solution.py:333
  46.0 13.3 %collective-permute-start.4 = (f32[47,32,128]{2,1,0:T(8,128)S(1)}, f32[47,32,128]{2,1,0:T(8,128)S(1)}, u32[]{:S(2)}, u32[]{:S(2)}) collective-permute-start(f32[47,32,128]{2,1,0:T(8,128)S(1)} %get-tuple-element.16), channel_id=1, source_target_pairs={{0,1},{1,0},{2,3},{3,2},{4,5},{5,4},{6,7},{7,6},{8,9},{9,8},{10,11... | collective-permute-start | bytes 2310152 | tf_op jit(solution)/shard_map/core_exchange/ppermute | solution.py:434
  59.3 1.9 %collective-permute-done.4.got = f32[47,32,128]{2,1,0:T(8,128)S(1)} collective-permute-done((f32[47,32,128]{2,1,0:T(8,128)S(1)}, f32[47,32,128]{2,1,0:T(8,128)S(1)}, u32[]{:S(2)}, u32[]{:S(2)}) %collective-permute-start.4) | collective-permute-done | bytes 770080 | tf_op jit(solution)/shard_map/core_exchange/ppermute | solution.py:434
  61.2 1.0 %core_merge.1 = (f32[47,8,128]{2,1,0:T(8,128)S(1)}, f32[47,8,128]{2,1,0:T(8,128)S(1)}, f32[47,8,128]{2,1,0:T(8,128)S(1)}, f32[47,8,128]{2,1,0:T(8,128)S(1)}) custom-call(f32[47,32,128]{2,1,0:T(8,128)S(1)} %get-tuple-element.15.keep, f32[47,32,128]{2,1,0:T(8,128)S(1)} %collective-permute-done.4.got, f32[128,128]{1,0:T(8,128)S(1)} %copy-done.2), custom_call_target="tpu_custom_call" | custom-call | tf_op jit(solution)/shard_map/core_merge/pallas_call | solution.py:421
  62.2 0.0 collective-permute-start.5
  62.3 0.1 collective-permute-start.6
  62.4 2.6 %collective-permute-start.7 = (f32[47,8,128]{2,1,0:T(8,128)S(1)}, f32[47,8,128]{2,1,0:T(8,128)S(1)}, u32[]{:S(2)}, u32[]{:S(2)}) collective-permute-start(f32[47,8,128]{2,1,0:T(8,128)S(1)} %get-tuple-element.20), channel_id=1, source_target_pairs={{0,6},{2,0},{4,2},{6,4},{1,7},{3,1},{5,3},{7,5},{8,14},{10,8},{12,... | collective-permute-start | bytes 577544 | tf_op jit(solution)/shard_map/span_exchange/ppermute | solution.py:434
  64.9 8.7 %collective-permute-done.5.one = f32[47,8,128]{2,1,0:T(8,128)S(1)} collective-permute-done((f32[47,8,128]{2,1,0:T(8,128)S(1)}, f32[47,8,128]{2,1,0:T(8,128)S(1)}, u32[]{:S(2)}, u32[]{:S(2)}) %collective-permute-start.5) | collective-permute-done | bytes 192544 | tf_op jit(solution)/shard_map/span_exchange/ppermute | solution.py:434
  73.7 0.0 collective-permute-done.6.two
  73.7 0.3 collective-permute-done.7.three
  74.0 0.8 span_merge.1.mine
  74.8 0.5 collective-permute-start.8
  75.3 5.8 %collective-permute-done.8.other = f32[47,8,128]{2,1,0:T(8,128)S(1)} collective-permute-done((f32[47,8,128]{2,1,0:T(8,128)S(1)}, f32[47,8,128]{2,1,0:T(8,128)S(1)}, u32[]{:S(2)}, u32[]{:S(2)}) %collective-permute-start.8) | collective-permute-done | bytes 192544 | tf_op jit(solution)/shard_map/x_exchange/ppermute | solution.py:434
  81.1 0.4 last_merge.1.refs_0_
  81.5 3.5 %collective-permute-start.11 = (f32[40,8,128]{2,1,0:T(8,128)S(1)}, f32[40,8,128]{2,1,0:T(8,128)S(1)}, u32[]{:S(2)}, u32[]{:S(2)}) collective-permute-start(f32[40,8,128]{2,1,0:T(8,128)S(1)} %last_merge.1.refs_0_), channel_id=1, source_target_pairs={{0,6},{2,0},{4,2},{6,4},{1,7},{3,1},{5,3},{7,5},{8,14},{10,8},{12,... | collective-permute-start | bytes 491528 | tf_op jit(solution)/shard_map/spread/ppermute | solution.py:434
  85.0 0.3 collective-permute-start.10
  85.3 0.3 collective-permute-start.9
  85.7 2.2 %collective-permute-start.12 = (f32[40,8,128]{2,1,0:T(8,128)S(1)}, f32[40,8,128]{2,1,0:T(8,128)S(1)}, u32[]{:S(2)}, u32[]{:S(2)}) collective-permute-start(f32[40,8,128]{2,1,0:T(8,128)S(1)} %last_merge.1.refs_0_), channel_id=1, source_target_pairs={{0,1},{1,0},{2,3},{3,2},{4,5},{5,4},{6,7},{7,6},{8,9},{9,8},{10,11... | collective-permute-start | bytes 491528 | tf_op jit(solution)/shard_map/spread/ppermute | solution.py:434
  87.9 1.5 %collective-permute-done.11.refs_3_ = f32[40,8,128]{2,1,0:T(8,128)S(1)} collective-permute-done((f32[40,8,128]{2,1,0:T(8,128)S(1)}, f32[40,8,128]{2,1,0:T(8,128)S(1)}, u32[]{:S(2)}, u32[]{:S(2)}) %collective-permute-start.11) | collective-permute-done | bytes 163872 | tf_op jit(solution)/shard_map/spread/ppermute | solution.py:434
  89.4 3.5 %collective-permute-start.15 = (f32[40,8,128]{2,1,0:T(8,128)S(1)}, f32[40,8,128]{2,1,0:T(8,128)S(1)}, u32[]{:S(2)}, u32[]{:S(2)}) collective-permute-start(f32[40,8,128]{2,1,0:T(8,128)S(1)} %collective-permute-done.11.refs_3_), channel_id=1, source_target_pairs={{0,1},{1,0},{2,3},{3,2},{4,5},{5,4},{6,7},{7,6},{8,9},{9,8},{10,11... | collective-permute-start | bytes 491528 | tf_op jit(solution)/shard_map/spread/ppermute | solution.py:434
  92.9 0.0 collective-permute-done.10.refs_2_
  92.9 2.0 %collective-permute-start.14 = (f32[40,8,128]{2,1,0:T(8,128)S(1)}, f32[40,8,128]{2,1,0:T(8,128)S(1)}, u32[]{:S(2)}, u32[]{:S(2)}) collective-permute-start(f32[40,8,128]{2,1,0:T(8,128)S(1)} %collective-permute-done.10.refs_2_), channel_id=1, source_target_pairs={{0,1},{1,0},{2,3},{3,2},{4,5},{5,4},{6,7},{7,6},{8,9},{9,8},{10,11... | collective-permute-start | bytes 491528 | tf_op jit(solution)/shard_map/spread/ppermute | solution.py:434
  94.9 0.6 collective-permute-done.9.refs_1_
  95.5 1.1 %collective-permute-start.13 = (f32[40,8,128]{2,1,0:T(8,128)S(1)}, f32[40,8,128]{2,1,0:T(8,128)S(1)}, u32[]{:S(2)}, u32[]{:S(2)}) collective-permute-start(f32[40,8,128]{2,1,0:T(8,128)S(1)} %collective-permute-done.9.refs_1_), channel_id=1, source_target_pairs={{0,1},{1,0},{2,3},{3,2},{4,5},{5,4},{6,7},{7,6},{8,9},{9,8},{10,11... | collective-permute-start | bytes 491528 | tf_op jit(solution)/shard_map/spread/ppermute | solution.py:434
  96.6 0.0 collective-permute-done.12.refs_4_
  96.6 0.0 collective-permute-done.15.refs_7_
  96.6 0.0 collective-permute-done.14.refs_6_
  96.6 1.0 %collective-permute-done.13.refs_5_ = f32[40,8,128]{2,1,0:T(8,128)S(1)} collective-permute-done((f32[40,8,128]{2,1,0:T(8,128)S(1)}, f32[40,8,128]{2,1,0:T(8,128)S(1)}, u32[]{:S(2)}, u32[]{:S(2)}) %collective-permute-start.13) | collective-permute-done | bytes 163872 | tf_op jit(solution)/shard_map/spread/ppermute | solution.py:434
  97.7 1.2 %place.1 = f32[40,64,128]{2,1,0:T(8,128)} custom-call(f32[40,8,128]{2,1,0:T(8,128)S(1)} %last_merge.1.refs_0_, f32[40,8,128]{2,1,0:T(8,128)S(1)} %collective-permute-done.9.refs_1_, f32[40,8,128]{2,1,0:T(8,128)S(1)} %collective-permute-done.10.refs_2_, f32[40,8,128]{2,1,0:T(8,128)S(1)} %collective-permute-done.11.refs_3_, ...), custom_call_target="tpu_custom_call" | custom-call | tf_op jit(solution)/shard_map/place/pallas_call | solution.py:421
Async XLA Ops:
  0.0 26.7 %copy-start.2 = (f32[128,128]{1,0:T(8,128)S(1)}, f32[128,128]{1,0:T(8,128)}, u32[]{:S(2)}) copy-start(f32[128,128]{1,0:T(8,128)} %dy.7) | copy-start | bytes 196612
  1.3 19.0 %collective-permute-start.1 = (f32[4,4,64,128]{3,2,1,0:T(8,128)S(1)}, f32[4,4,64,128]{3,2,1,0:T(8,128)S(1)}, u32[]{:S(2)}, u32[]{:S(2)}) collective-permute-start(f32[4,4,64,128]{3,2,1,0:T(8,128)S(1)} %get-tuple-element.23), channel_id=1, source_target_pairs={{16,0},{32,16},{48,32},{64,48},{80,64},{96,80},{112,96},{17,1},{33... | collective-permute-start | bytes 1572872 | tf_op jit(solution)/shard_map/rims/ppermute | solution.py:445
  4.4 22.4 %collective-permute-start = (f32[4,4,64,128]{3,2,1,0:T(8,128)S(1)}, f32[4,4,64,128]{3,2,1,0:T(8,128)S(1)}, u32[]{:S(2)}, u32[]{:S(2)}) collective-permute-start(f32[4,4,64,128]{3,2,1,0:T(8,128)S(1)} %get-tuple-element.24), channel_id=1, source_target_pairs={{0,16},{16,32},{32,48},{48,64},{64,80},{80,96},{96,112},{1,17},{17... | collective-permute-start | bytes 1572872 | tf_op jit(solution)/shard_map/rims/ppermute | solution.py:444
  8.4 18.3 %collective-permute-start.3 = (f32[4,64,4,128]{3,2,1,0:T(4,128)S(1)}, f32[4,64,4,128]{3,2,1,0:T(4,128)S(1)}, u32[]{:S(2)}, u32[]{:S(2)}) collective-permute-start(f32[4,64,4,128]{3,2,1,0:T(4,128)S(1)} %get-tuple-element.21), channel_id=1, source_target_pairs={{0,15},{1,0},{2,1},{3,2},{4,3},{5,4},{6,5},{7,6},{8,7},{9,8},{10,9... | collective-permute-start | bytes 1572872 | tf_op jit(solution)/shard_map/rims/ppermute | solution.py:434
  9.7 17.0 %collective-permute-start.2 = (f32[4,64,4,128]{3,2,1,0:T(4,128)S(1)}, f32[4,64,4,128]{3,2,1,0:T(4,128)S(1)}, u32[]{:S(2)}, u32[]{:S(2)}) collective-permute-start(f32[4,64,4,128]{3,2,1,0:T(4,128)S(1)} %get-tuple-element.22), channel_id=1, source_target_pairs={{0,1},{1,2},{2,3},{3,4},{4,5},{5,6},{6,7},{7,8},{8,9},{9,10},{10,1... | collective-permute-start | bytes 1572872 | tf_op jit(solution)/shard_map/rims/ppermute | solution.py:434
  11.3 3.4 %copy-start = (f32[4,64,64,128]{3,2,1,0:T(8,128)S(1)}, f32[4,64,64,128]{3,2,1,0:T(8,128)}, u32[]{:S(2)}) copy-start(f32[4,64,64,128]{3,2,1,0:T(8,128)} %flow.3) | copy-start | bytes 25165828
  14.7 12.1 %copy-start.1 = (f32[4,64,64,128]{3,2,1,0:T(8,128)S(1)}, f32[4,64,64,128]{3,2,1,0:T(8,128)}, u32[]{:S(2)}) copy-start(f32[4,64,64,128]{3,2,1,0:T(8,128)} %flow.3) | copy-start | bytes 25165828
  46.0 15.2 %collective-permute-start.4 = (f32[47,32,128]{2,1,0:T(8,128)S(1)}, f32[47,32,128]{2,1,0:T(8,128)S(1)}, u32[]{:S(2)}, u32[]{:S(2)}) collective-permute-start(f32[47,32,128]{2,1,0:T(8,128)S(1)} %get-tuple-element.16), channel_id=1, source_target_pairs={{0,1},{1,0},{2,3},{3,2},{4,5},{5,4},{6,7},{7,6},{8,9},{9,8},{10,11... | collective-permute-start | bytes 2310152 | tf_op jit(solution)/shard_map/core_exchange/ppermute | solution.py:434
  62.2 11.4 %collective-permute-start.5 = (f32[47,8,128]{2,1,0:T(8,128)S(1)}, f32[47,8,128]{2,1,0:T(8,128)S(1)}, u32[]{:S(2)}, u32[]{:S(2)}) collective-permute-start(f32[47,8,128]{2,1,0:T(8,128)S(1)} %get-tuple-element.18), channel_id=1, source_target_pairs={{0,2},{2,4},{4,6},{6,0},{1,3},{3,5},{5,7},{7,1},{8,10},{10,12},{12... | collective-permute-start | bytes 577544 | tf_op jit(solution)/shard_map/span_exchange/ppermute | solution.py:434
  62.3 11.4 %collective-permute-start.6 = (f32[47,8,128]{2,1,0:T(8,128)S(1)}, f32[47,8,128]{2,1,0:T(8,128)S(1)}, u32[]{:S(2)}, u32[]{:S(2)}) collective-permute-start(f32[47,8,128]{2,1,0:T(8,128)S(1)} %get-tuple-element.19), channel_id=1, source_target_pairs={{0,4},{2,6},{4,0},{6,2},{1,5},{3,7},{5,1},{7,3},{8,12},{10,14},{12... | collective-permute-start | bytes 577544 | tf_op jit(solution)/shard_map/span_exchange/ppermute | solution.py:434
  62.4 11.6 %collective-permute-start.7 = (f32[47,8,128]{2,1,0:T(8,128)S(1)}, f32[47,8,128]{2,1,0:T(8,128)S(1)}, u32[]{:S(2)}, u32[]{:S(2)}) collective-permute-start(f32[47,8,128]{2,1,0:T(8,128)S(1)} %get-tuple-element.20), channel_id=1, source_target_pairs={{0,6},{2,0},{4,2},{6,4},{1,7},{3,1},{5,3},{7,5},{8,14},{10,8},{12,... | collective-permute-start | bytes 577544 | tf_op jit(solution)/shard_map/span_exchange/ppermute | solution.py:434
  74.8 6.3 %collective-permute-start.8 = (f32[47,8,128]{2,1,0:T(8,128)S(1)}, f32[47,8,128]{2,1,0:T(8,128)S(1)}, u32[]{:S(2)}, u32[]{:S(2)}) collective-permute-start(f32[47,8,128]{2,1,0:T(8,128)S(1)} %span_merge.1.mine), channel_id=1, source_target_pairs={{0,8},{8,0},{1,9},{9,1},{2,10},{10,2},{3,11},{11,3},{4,12},{12,4},... | collective-permute-start | bytes 577544 | tf_op jit(solution)/shard_map/x_exchange/ppermute | solution.py:434
  81.5 7.9 %collective-permute-start.11 = (f32[40,8,128]{2,1,0:T(8,128)S(1)}, f32[40,8,128]{2,1,0:T(8,128)S(1)}, u32[]{:S(2)}, u32[]{:S(2)}) collective-permute-start(f32[40,8,128]{2,1,0:T(8,128)S(1)} %last_merge.1.refs_0_), channel_id=1, source_target_pairs={{0,6},{2,0},{4,2},{6,4},{1,7},{3,1},{5,3},{7,5},{8,14},{10,8},{12,... | collective-permute-start | bytes 491528 | tf_op jit(solution)/shard_map/spread/ppermute | solution.py:434
  85.0 7.9 %collective-permute-start.10 = (f32[40,8,128]{2,1,0:T(8,128)S(1)}, f32[40,8,128]{2,1,0:T(8,128)S(1)}, u32[]{:S(2)}, u32[]{:S(2)}) collective-permute-start(f32[40,8,128]{2,1,0:T(8,128)S(1)} %last_merge.1.refs_0_), channel_id=1, source_target_pairs={{0,4},{2,6},{4,0},{6,2},{1,5},{3,7},{5,1},{7,3},{8,12},{10,14},{12... | collective-permute-start | bytes 491528 | tf_op jit(solution)/shard_map/spread/ppermute | solution.py:434
  85.3 10.2 %collective-permute-start.9 = (f32[40,8,128]{2,1,0:T(8,128)S(1)}, f32[40,8,128]{2,1,0:T(8,128)S(1)}, u32[]{:S(2)}, u32[]{:S(2)}) collective-permute-start(f32[40,8,128]{2,1,0:T(8,128)S(1)} %last_merge.1.refs_0_), channel_id=1, source_target_pairs={{0,2},{2,4},{4,6},{6,0},{1,3},{3,5},{5,7},{7,1},{8,10},{10,12},{12... | collective-permute-start | bytes 491528 | tf_op jit(solution)/shard_map/spread/ppermute | solution.py:434
  85.7 11.0 %collective-permute-start.12 = (f32[40,8,128]{2,1,0:T(8,128)S(1)}, f32[40,8,128]{2,1,0:T(8,128)S(1)}, u32[]{:S(2)}, u32[]{:S(2)}) collective-permute-start(f32[40,8,128]{2,1,0:T(8,128)S(1)} %last_merge.1.refs_0_), channel_id=1, source_target_pairs={{0,1},{1,0},{2,3},{3,2},{4,5},{5,4},{6,7},{7,6},{8,9},{9,8},{10,11... | collective-permute-start | bytes 491528 | tf_op jit(solution)/shard_map/spread/ppermute | solution.py:434
  89.4 7.2 %collective-permute-start.15 = (f32[40,8,128]{2,1,0:T(8,128)S(1)}, f32[40,8,128]{2,1,0:T(8,128)S(1)}, u32[]{:S(2)}, u32[]{:S(2)}) collective-permute-start(f32[40,8,128]{2,1,0:T(8,128)S(1)} %collective-permute-done.11.refs_3_), channel_id=1, source_target_pairs={{0,1},{1,0},{2,3},{3,2},{4,5},{5,4},{6,7},{7,6},{8,9},{9,8},{10,11... | collective-permute-start | bytes 491528 | tf_op jit(solution)/shard_map/spread/ppermute | solution.py:434
  92.9 3.7 %collective-permute-start.14 = (f32[40,8,128]{2,1,0:T(8,128)S(1)}, f32[40,8,128]{2,1,0:T(8,128)S(1)}, u32[]{:S(2)}, u32[]{:S(2)}) collective-permute-start(f32[40,8,128]{2,1,0:T(8,128)S(1)} %collective-permute-done.10.refs_2_), channel_id=1, source_target_pairs={{0,1},{1,0},{2,3},{3,2},{4,5},{5,4},{6,7},{7,6},{8,9},{9,8},{10,11... | collective-permute-start | bytes 491528 | tf_op jit(solution)/shard_map/spread/ppermute | solution.py:434
  95.5 2.1 %collective-permute-start.13 = (f32[40,8,128]{2,1,0:T(8,128)S(1)}, f32[40,8,128]{2,1,0:T(8,128)S(1)}, u32[]{:S(2)}, u32[]{:S(2)}) collective-permute-start(f32[40,8,128]{2,1,0:T(8,128)S(1)} %collective-permute-done.9.refs_1_), channel_id=1, source_target_pairs={{0,1},{1,0},{2,3},{3,2},{4,5},{5,4},{6,7},{7,6},{8,9},{9,8},{10,11... | collective-permute-start | bytes 491528 | tf_op jit(solution)/shard_map/spread/ppermute | solution.py:434

commit v2 on v1

v2 whole, which is shorter than its diff:
```python
import functools

import jax
import jax.numpy as jnp
from jax import lax
from jax.experimental import pallas as pl
from jax.experimental.pallas import tpu as pltpu
from jax.sharding import Mesh, PartitionSpec as P

F32 = jnp.float32
BF16 = jnp.bfloat16
lead = 4.0 / 5.0
ratios = (1.0, -0.25, 1.0 / 21.0, -1.0 / 224.0)
pairs = ((0, 0), (0, 1), (0, 2), (1, 1), (1, 2), (2, 2))
triples = (
    (0, 0, 0), (0, 0, 1), (0, 0, 2), (0, 1, 1), (0, 1, 2),
    (0, 2, 2), (1, 1, 1), (1, 1, 2), (1, 2, 2), (2, 2, 2),
)
MEAN, DXM, ZSUM, UU, UUU, PU, PG, GG, UG = 0, 4, 8, 11, 17, 27, 30, 36, 42
STATE = 47
OUT = 40
NBASE = 19
NSLOPE = 22
GXA, ZA, CA = "gx", ("xh", "z", "c"), "c"


def combine(left, right, count, dmat, put):
    half = [0.5 * (left(MEAN + c) - right(MEAN + c)) for c in range(4)]
    gx = [0.5 * (left(DXM + c) - right(DXM + c)) for c in range(4)]
    gy = [
        jnp.dot(h, dmat, precision=lax.Precision.HIGHEST, preferred_element_type=F32) for h in half
    ]
    dz = [half[3] * (left(ZSUM + c) - right(ZSUM + c)) for c in range(3)]
    both = float(2 * count)
    nh = [both * h for h in half]
    for c in range(4):
        put(MEAN + c, 0.5 * (left(MEAN + c) + right(MEAN + c)))
        put(DXM + c, 0.5 * (left(DXM + c) + right(DXM + c)))
    for c in range(3):
        put(ZSUM + c, left(ZSUM + c) + right(ZSUM + c))
    gap = {}
    for k, (i, j) in enumerate(pairs):
        a, b = left(UU + k), right(UU + k)
        gap[i, j] = gap[j, i] = a - b
        put(UU + k, (a + b) + nh[i] * half[j])
    for k, (i, j, l) in enumerate(triples):
        fix = half[i] * gap[j, l] + half[j] * gap[i, l] + half[l] * gap[i, j]
        put(UUU + k, (left(UUU + k) + right(UUU + k)) + fix)
    for c in range(3):
        put(PU + c, (left(PU + c) + right(PU + c)) + nh[3] * half[c])
    fixes = (
        2.0 * nh[3] * gx[0],
        nh[3] * (gy[0] + gx[1]),
        dz[0] + nh[3] * gx[2],
        2.0 * nh[3] * gy[1],
        dz[1] + nh[3] * gy[2],
        2.0 * dz[2],
    )
    for k in range(6):
        put(PG + k, (left(PG + k) + right(PG + k)) + fixes[k])
    for k, (i, j) in enumerate(pairs):
        fix = both * (gx[i] * gx[j] + gy[i] * gy[j])
        put(GG + k, (left(GG + k) + right(GG + k)) + fix)
    fixes = (
        -2.0 * nh[0] * gx[3],
        -(nh[0] * gy[3] + nh[1] * gx[3]),
        dz[0] - nh[2] * gx[3],
        -2.0 * nh[1] * gy[3],
        dz[1] - nh[2] * gy[3],
    )
    for k in range(5):
        put(UG + k, (left(UG + k) + right(UG + k)) + fixes[k])


def row_sum(k, rows, acc, first=0, count=None):
    count = rows if count is None else count
    return sum(acc[pl.ds(8 * (k * rows + first) + s, count, stride=8), :] for s in range(8))


def copy_all(copies):
    for c in copies:
        c.start()
    for c in copies:
        c.wait()


def z_rim_kernel(flow, zl, zr, sems):
    lz = flow.shape[2]
    copy_all([
        pltpu.make_async_copy(flow.at[pl.ds(0, 3), :, pl.ds(lz - 4, 4)], zl, sems.at[0]),
        pltpu.make_async_copy(flow.at[pl.ds(0, 3), :, pl.ds(0, 4)], zr, sems.at[1]),
    ])


def x_rim_kernel(flow, after, xl, xr, sems):
    lx = flow.shape[1]
    copy_all([
        pltpu.make_async_copy(flow.at[:, pl.ds(lx - 4, 4)], xl, sems.at[0]),
        pltpu.make_async_copy(flow.at[:, pl.ds(0, 4)], xr, sems.at[1]),
    ])


def pad_kernel(flow, after, pad, sems):
    _, lx, lz, _ = flow.shape
    copy_all([
        pltpu.make_async_copy(flow.at[c], pad.at[c, pl.ds(4, lx), pl.ds(8, lz)], sems.at[c])
        for c in range(4)
    ])


def cut(kernel, shapes, copies, name, flow, *after):
    flow = pltpu.with_memory_space_constraint(flow, pltpu.HBM)
    return pl.pallas_call(
        kernel,
        in_specs=[pl.BlockSpec(memory_space=pltpu.HBM)]
        + [pl.BlockSpec(memory_space=pl.ANY)] * len(after),
        out_specs=[pl.BlockSpec(memory_space=pltpu.VMEM)] * len(shapes),
        out_shape=[pltpu.VMEM(s, F32) for s in shapes],
        scratch_shapes=[pltpu.SemaphoreType.DMA((copies,))],
        compiler_params=pltpu.CompilerParams(vmem_limit_bytes=4 * 2**20),
        name=name,
    )(flow, *after)


def base_kernel(pad_in, dy, pad, ysl, mean, base, acc, weights):
    _, lx, lz, ny = ysl.shape
    step = 8
    parts = lx // step

    d = dy[...].T * (1.0 / lead)
    dhi = d.astype(BF16)
    dlo = (d - dhi.astype(F32)).astype(BF16)
    weights[pl.ds(0, ny), pl.ds(0, ny)] = dhi
    weights[pl.ds(0, ny), pl.ds(ny, ny)] = dlo
    weights[pl.ds(ny, ny), pl.ds(0, ny)] = dhi
    weights[pl.ds(ny, ny), pl.ds(ny, ny)] = jnp.zeros_like(dlo)

    def one(x, _):
        centre = []
        for c in range(4):
            m = jnp.sum(pad[c, x + 4, pl.ds(8, lz), :], axis=0, keepdims=True) * (1.0 / lz)
            mean[c, pl.ds(x, 1), :] = m
            centre.append(m)
        total = [None] * NBASE

        def add(k, v):
            total[k] = v if total[k] is None else total[k] + v

        for b in range(lz // 8):
            f = [pad[c, x + 4, pl.ds(8 + 8 * b, 8), :] - centre[c] for c in range(4)]
            for c in range(4):
                pad[c, x + 4, pl.ds(8 + 8 * b, 8), :] = f[c]
            prod = {}
            for k, (i, j) in enumerate(pairs):
                prod[i, j] = f[i] * f[j]
                add(k, prod[i, j])
            for k, (i, j, l) in enumerate(triples):
                add(6 + k, prod[i, j] * f[l])
            for c in range(3):
                add(16 + c, f[3] * f[c])
        for k in range(NBASE):
            acc[pl.ds(pl.multiple_of(k * 8 * lx + 8 * x, 8), 8), :] = total[k]
        return 0

    def part(k, _):
        lax.fori_loop(step * k, step * k + step, one, 0)
        left = []
        for r in range(step):
            for c in range(4):
                a = pad[c, step * k + r + 4, pl.ds(8, lz), :]
                hi = a.astype(BF16)
                lo = (a - hi.astype(F32)).astype(BF16)
                left.append(jnp.concatenate([hi, lo], axis=1))
        y = jnp.dot(jnp.concatenate(left, axis=0), weights[...], preferred_element_type=F32)
        y = y[:, :ny] + y[:, ny:]
        for r in range(step):
            for c in range(4):
                at = (4 * r + c) * lz
                ysl[c, step * k + r] = y[at : at + lz]
        return 0

    lax.fori_loop(0, parts, part, 0)
    for k in range(NBASE):
        base[k] = row_sum(k, lx, acc)


def base_moments(pad, dy):
    ny = dy.shape[0]
    lx, lz = pad.shape[1] - 8, pad.shape[2] - 16
    vm = pl.BlockSpec(memory_space=pltpu.VMEM)
    shapes = [pad.shape, (4, lx, lz, ny), (4, lx, ny), (NBASE, lx, ny)]
    return pl.pallas_call(
        base_kernel,
        in_specs=[vm, vm],
        out_specs=[vm] * 4,
        out_shape=[pltpu.VMEM(s, F32) for s in shapes],
        input_output_aliases={0: 0},
        scratch_shapes=[
            pltpu.VMEM((NBASE * 8 * lx, ny), F32),
            pltpu.VMEM((2 * ny, 2 * ny), BF16),
        ],
        compiler_params=pltpu.CompilerParams(vmem_limit_bytes=16 * 2**20),
        cost_estimate=pl.CostEstimate(
            flops=1000, bytes_accessed=1000, transcendentals=0
        ),
        name="base_moments",
    )(pad, dy)


def difference(upper, lower):
    out = None
    for k in range(4):
        diff = upper(k) - lower(k)
        out = diff if out is None else out + ratios[k] * diff
    return out


def slope_row(pad, ysl, x):
    lz = ysl.shape[2]
    total = [None] * NSLOPE

    def add(k, v):
        total[k] = v if total[k] is None else total[k] + v

    for b in range(lz // 8):
        at = 8 + 8 * b
        u = [pad[c, x + 4, pl.ds(at, 8), :] for c in range(4)]
        p = u[3]
        g = [[None] * 3 for _ in range(4)]
        for c in range(4):
            g[c][0] = difference(
                lambda k: pad[c, x + 5 + k, pl.ds(at, 8), :],
                lambda k: pad[c, x + 3 - k, pl.ds(at, 8), :],
            )
            g[c][1] = ysl[c, x, pl.ds(8 * b, 8), :]
        for c in range(3):
            g[c][2] = difference(
                lambda k: pad[c, x + 4, pl.ds(at + 1 + k, 8), :],
                lambda k: pad[c, x + 4, pl.ds(at - 1 - k, 8), :],
            )
        for c in range(3):
            add(c, g[c][2])
        add(3, p * g[0][0])
        add(4, p * (g[0][1] + g[1][0]))
        add(5, p * g[0][2])
        add(6, p * g[2][0])
        add(7, p * g[1][1])
        add(8, p * g[1][2])
        add(9, p * g[2][1])
        add(10, p * g[2][2])
        for k, (i, j) in enumerate(pairs):
            for dim in range(3):
                add(11 + k, g[i][dim] * g[j][dim])
        add(17, u[0] * g[3][0])
        add(18, u[0] * g[3][1] + u[1] * g[3][0])
        add(19, u[1] * g[3][1])
        add(20, u[2] * g[3][0])
        add(21, u[2] * g[3][1])
    return total


def slope_fields(total):
    s02, s12 = total(5), total(8)
    yield PG + 0, 2.0 * total(3)
    yield PG + 1, total(4)
    yield PG + 2, s02 + total(6)
    yield PG + 3, 2.0 * total(7)
    yield PG + 4, s12 + total(9)
    yield PG + 5, 2.0 * total(10)
    for c in range(3):
        yield ZSUM + c, total(c)
    for k in range(6):
        yield GG + k, total(11 + k)
    yield UG + 0, -2.0 * total(17)
    yield UG + 1, -total(18)
    yield UG + 2, s02 - total(20)
    yield UG + 3, -2.0 * total(19)
    yield UG + 4, s12 - total(21)


def inner_kernel(pad_in, ysl, zl, zr, mean, base, pad, keep, send, acc):
    _, lx, lz, ny = ysl.shape
    half = lx // 2
    core = lax.axis_index(CA)

    def rim(x, _):
        for c in range(3):
            m = mean[c, pl.ds(x, 1), :]
            pad[c, x + 4, pl.ds(4, 4), :] = zl[c, x] - m
            pad[c, x + 4, pl.ds(8 + lz, 4), :] = zr[c, x] - m
        return 0

    lax.fori_loop(0, lx, rim, 0, unroll=4)

    def one(x, _):
        total = slope_row(pad, ysl, x)
        for k in range(NSLOPE):
            acc[pl.ds(pl.multiple_of(k * 8 * lx + 8 * x, 8), 8), :] = total[k]
        return 0

    lax.fori_loop(4, lx - 4, one, 0)

    for out, side in ((send, 1 - core), (keep, core)):
        at = pl.multiple_of(half * side, 8)

        def total(k, at=at):
            where = pl.multiple_of(8 * (k * lx + at), 8)
            return sum(acc[pl.ds(where + s, half, stride=8), :] for s in range(8))

        for c in range(4):
            out[MEAN + c] = mean[c, pl.ds(at, half), :]
        for k in range(NBASE):
            out[UU + k] = base[k, pl.ds(at, half), :]
        for f, v in slope_fields(total):
            out[f] = v


def inner_moments(pad, ysl, zl, zr, mean, base):
    _, lx, lz, ny = ysl.shape
    vm = pl.BlockSpec(memory_space=pltpu.VMEM)
    shape = pltpu.VMEM((STATE, lx // 2, ny), F32)
    return pl.pallas_call(
        inner_kernel,
        in_specs=[vm] * 6,
        out_specs=[vm] * 3,
        out_shape=[pltpu.VMEM(pad.shape, F32), shape, shape],
        input_output_aliases={0: 0},
        scratch_shapes=[pltpu.VMEM((NSLOPE * 8 * lx, ny), F32)],
        compiler_params=pltpu.CompilerParams(vmem_limit_bytes=16 * 2**20),
        cost_estimate=pl.CostEstimate(
            flops=5000 * ysl.size, bytes_accessed=40 * ysl.size, transcendentals=0
        ),
        name="inner_moments",
    )(pad, ysl, zl, zr, mean, base)


def edge_kernel(
    pad_in, keep_in, send_in, ysl, xl, xr, mean, pad, keep, send, acc, mpad, dxm
):
    _, lx, lz, ny = ysl.shape
    half = lx // 2
    core = lax.axis_index(CA)
    gi = lax.axis_index(GXA)
    at_ends = (gi == 0, gi == lax.axis_size(GXA) - 1)

    for c in range(4):
        mpad[c, pl.ds(8, lx), :] = mean[c]
        for j in range(4):
            for halo, at_end, src, dst in (
                (xl, at_ends[0], 3 - j, j), (xr, at_ends[1], lx - 1 - j, lx + 4 + j)
            ):
                own = pad[c, src + 4, pl.ds(8, lz), :]
                m = jnp.sum(halo[c, j], axis=0, keepdims=True) * (1.0 / lz)
                pad[c, dst, pl.ds(8, lz), :] = jnp.where(at_end, own, halo[c, j] - m)
                mpad[c, pl.ds(dst + 4, 1), :] = jnp.where(at_end, mean[c, pl.ds(src, 1), :], m)
        dxm[c] = difference(
            lambda k: mpad[c, pl.ds(9 + k, lx), :], lambda k: mpad[c, pl.ds(7 - k, lx), :]
        )

    for out, side in ((send, 1 - core), (keep, core)):
        for c in range(4):
            out[DXM + c] = dxm[c, pl.ds(pl.multiple_of(half * side, 8), half), :]

    def one(i, _):
        x = jnp.where(i < 4, i, lx - 8 + i)
        total = slope_row(pad, ysl, x)
        for k in range(NSLOPE):
            acc[pl.ds(pl.multiple_of(k * 64 + 8 * i, 8), 8), :] = total[k]
        return 0

    lax.fori_loop(0, 8, one, 0)

    fields = list(slope_fields(lambda k: row_sum(k, 8, acc)))
    for side, rows in ((0, slice(0, 4)), (1, slice(4, 8))):
        at = 0 if side == 0 else half - 4

        @pl.when(core == side)
        def _():
            for f, v in fields:
                keep[f, pl.ds(at, 4), :] = v[rows]

        @pl.when(core != side)
        def _():
            for f, v in fields:
                send[f, pl.ds(at, 4), :] = v[rows]


def edge_moments(pad, keep, send, ysl, xl, xr, mean):
    _, lx, lz, ny = ysl.shape
    vm = pl.BlockSpec(memory_space=pltpu.VMEM)
    out = pl.pallas_call(
        edge_kernel,
        in_specs=[vm] * 7,
        out_specs=[vm] * 3,
        out_shape=[pltpu.VMEM(v.shape, F32) for v in (pad, keep, send)],
        input_output_aliases={0: 0, 1: 1, 2: 2},
        scratch_shapes=[
            pltpu.VMEM((NSLOPE * 64, ny), F32),
            pltpu.VMEM((4, lx + 16, ny), F32),
            pltpu.VMEM((4, lx, ny), F32),
        ],
        compiler_params=pltpu.CompilerParams(vmem_limit_bytes=16 * 2**20),
        cost_estimate=pl.CostEstimate(
            flops=25 * ysl.size, bytes_accessed=ysl.size // 2, transcendentals=0
        ),
        name="edge_moments",
    )(pad, keep, send, ysl, xl, xr, mean)
    return out[1:]


def core_kernel(count, keep, got, dy, own, up, down, far):
    d = dy[...].T * (1.0 / lead)
    rows = own.shape[1]
    zi = lax.axis_index("z")
    zn = lax.axis_size("z")
    for k, out in ((0, own), (1, up), (zn - 1, down), (2, far)):
        at = pl.multiple_of(rows * lax.rem(zi + k, zn), 8)

        def put(f, v, out=out):
            out[f] = v

        combine(
            lambda f, at=at: keep[f, pl.ds(at, rows), :],
            lambda f, at=at: got[f, pl.ds(at, rows), :],
            count, d, put,
        )


def span_kernel(count, own, one, two, three, dy, out, left, right):
    d = dy[...].T * (1.0 / lead)

    def put_to(ref):
        def put(f, v):
            ref[f] = v
        return put

    combine(lambda f: own[f], lambda f: one[f], count, d, put_to(left))
    combine(lambda f: two[f], lambda f: three[f], count, d, put_to(right))
    combine(lambda f: left[f], lambda f: right[f], 2 * count, d, put_to(out))


def last_kernel(count, mine, other, dy, out, state):
    d = dy[...].T * (1.0 / lead)

    def put(f, v):
        state[f] = v

    combine(lambda f: mine[f], lambda f: other[f], count, d, put)
    scale = 1.0 / (2 * count)
    for c in range(3):
        out[c] = state[MEAN + c]
    for k in range(NBASE):
        out[3 + k] = state[UU + k] * scale
    for k in range(6):
        out[22 + k] = state[PG + k] * (scale * lead)
        out[28 + k] = state[GG + k] * (scale * lead * lead)
    for k in range(5):
        out[34 + k] = state[UG + k] * (scale * lead)
    out[39] = state[PG + 5] * (scale * lead)


def place_kernel(*refs):
    ins, out = refs[:-1], refs[-1]
    rows = ins[0].shape[1]
    zi = lax.axis_index("z")
    zn = lax.axis_size("z")
    core = lax.axis_index(CA)
    for k, ref in enumerate(ins):
        side, step = divmod(k, zn)
        c = core if side == 0 else 1 - core
        at = pl.multiple_of(rows * (zn * c + lax.rem(zi + zn - step, zn)), 8)
        out[:, pl.ds(at, rows), :] = ref[...]


def small_call(kernel, outs, scratch, name, *args):
    vm = pl.BlockSpec(memory_space=pltpu.VMEM)
    return pl.pallas_call(
        kernel,
        in_specs=[vm] * len(args),
        out_specs=[vm] * len(outs),
        out_shape=[jax.ShapeDtypeStruct(s, F32) for s in outs],
        scratch_shapes=[pltpu.VMEM(s, F32) for s in scratch],
        compiler_params=pltpu.CompilerParams(vmem_limit_bytes=24 * 2**20),
        name=name,
    )(*args)


def send(value, axis, step):
    size = lax.axis_size(axis)
    return lax.ppermute(value, axis, [(i, (i + step) % size) for i in range(size)])


def shards(flow, dy):
    _, lx, lz, ny = flow.shape
    gn = lax.axis_size(GXA)
    zn = lax.axis_size("z")
    up = [(i, i + 1) for i in range(gn - 1)]
    down = [(i + 1, i) for i in range(gn - 1)]
    zs, xs = (3, lx, 4, ny), (4, 4, lz, ny)
    zl, zr = cut(z_rim_kernel, [zs, zs], 2, "z_rims", flow)
    xl, xr = cut(x_rim_kernel, [xs, xs], 2, "x_rims", flow, zl)
    (pad,) = cut(pad_kernel, [(4, lx + 8, lz + 16, ny)], 4, "load", flow, xl)
    with jax.named_scope("rim_exchange"):
        zl = send(zl, ZA, 1)
        zr = send(zr, ZA, -1)
        xl = lax.ppermute(xl, GXA, up)
        xr = lax.ppermute(xr, GXA, down)
    pad, ysl, mean, base = base_moments(pad, dy)
    pad, keep, give = inner_moments(pad, ysl, zl, zr, mean, base)
    keep, give = edge_moments(pad, keep, give, ysl, xl, xr, mean)
    with jax.named_scope("core_exchange"):
        got = send(give, CA, 1)
    rows = lx // 2 // zn
    piece = (STATE, rows, ny)
    own, up1, down1, far = small_call(
        functools.partial(core_kernel, lz), [piece] * 4, [], "core_merge", keep, got, dy
    )
    with jax.named_scope("span_exchange"):
        one = send(up1, "z", 1)
        three = send(down1, "z", -1)
        two = send(far, "z", 2)
    (part,) = small_call(
        functools.partial(span_kernel, 2 * lz),
        [piece], [piece, piece], "span_merge", own, one, two, three, dy,
    )
    with jax.named_scope("x_exchange"):
        other = send(part, "xh", 1)
    (done,) = small_call(
        functools.partial(last_kernel, 2 * zn * lz),
        [(OUT, rows, ny)], [piece], "last_merge", part, other, dy,
    )
    with jax.named_scope("spread"):
        mine = [done] + [send(done, "z", k) for k in (1, 2, 3)]
        theirs = [send(v, CA, 1) for v in mine]
    (out,) = small_call(place_kernel, [(OUT, lx, ny)], [], "place", *mine, *theirs)
    return out


def solution(mesh):
    gx, gz = mesh.shape["gx"], mesh.shape["gz"]
    fine = Mesh(mesh.devices.reshape(gx, 2, gz // 4, 2), (GXA,) + ZA)
    return jax.shard_map(
        shards,
        mesh=fine,
        in_specs=(P(None, GXA, ZA, None), P()),
        out_specs=P(None, GXA, None),
        check_vma=False,
    )
```

time: 99.4 us -> 79.8 us (0.80)
  waiting for transfers between devices: 26.1 us -> 18.5 us
  starting transfers between devices: 37.7 us -> 31 us
  local copies, waits for them, and re-layouts: 6.46 us -> 0.01 us
    ppermute x14, starting transfers between devices: 32.4 us -> 25.6 us  [send(): lax.ppermute(value, axis, [(i, (i + step) % size) for i in range(size)])]
    ppermute x2, waiting for transfers between devices: 6.34 us -> 0.01 us  [the longest x1 0.01 us: shards(): xr = lax.ppermute(xr, GXA, down)]
    unnamed x6 -> x2, local copies, waits for them, and re-layouts: 3.39 us -> 0.01 us
    slice x2 -> x0, local copies, waits for them, and re-layouts: 3.07 us -> none  [the longest x1 1.74 us: shards(): zr = send(flow[:, :, :4], ZA, -1)]
    ppermute x14, waiting for transfers between devices: 19.8 us -> 18.5 us  [send(): lax.ppermute(value, axis, [(i, (i + step) % size) for i in range(size)])]
    pallas_call x2 -> x6, Pallas kernels: 25 us -> 25.7 us  [the longest x1 9.56 us: inner_moments(): pl.pallas_call(inner_kernel, in_specs=[vm] * 6, out_specs=[vm] * 3, out_s...]
  transfers between devices with their start and end apart: 16 -> 16, of which waited for: 8 -> 7; matrix products, arithmetic and copies ran while one was open for 2% -> 0% of each run, Pallas kernels for 6% -> 29%
where the time goes in v2:
time: 79.8 us; the launch traced here: 78.7 us
  starting transfers between devices  31 us (39%)
  Pallas kernels  29.1 us (36%)
  waiting for transfers between devices  18.5 us (23%)
    ppermute x14, starting transfers between devices, send(): lax.ppermute(value, axis, [(i, (i + step) % size) for i in range(size)])  25.6 us
    ppermute x14, waiting for transfers between devices, send(): lax.ppermute(value, axis, [(i, (i + step) % size) for i in range(size)])  18.5 us
    pallas_call x1, Pallas kernels, inner_moments(): pl.pallas_call(inner_kernel, in_specs=[vm] * 6, out_specs=[vm] * 3, out_s...  9.56 us
    pallas_call x1, Pallas kernels, base_moments(): pl.pallas_call(base_kernel, in_specs=[vm, vm], out_specs=[vm] * 4, out_sh...  8.65 us
    pallas_call x3, Pallas kernels, cut(): pl.pallas_call(kernel, in_specs=[pl.BlockSpec(memory_space=pltpu.HBM)] +...  5.86 us
    pallas_call x4, Pallas kernels, small_call(): pl.pallas_call(kernel, in_specs=[vm] * len(args), out_specs=[vm] * len(ou...  3.48 us
    ppermute x1, starting transfers between devices, shards(): xr = lax.ppermute(xr, GXA, down)  3.14 us
    ppermute x1, starting transfers between devices, shards(): xl = lax.ppermute(xl, GXA, up)  2.28 us
  transfers between devices with their start and end apart: 16, of which 7 were waited for; matrix products, arithmetic and copies ran while one was open for 0% of the time, Pallas kernels for 29%

profile of v2, /device:TPU:9, one launch (start us, length us, event | category | flops | bytes accessed | tf_op | source)
XLA Modules:
  0.0 78.7 jit_solution(11140322120227165071)
XLA Ops:
  0.0 1.1 %z_rims.1 = (f32[3,64,4,128]{3,2,1,0:T(4,128)S(1)}, f32[3,64,4,128]{3,2,1,0:T(4,128)S(1)}) custom-call(f32[4,64,64,128]{3,2,1,0:T(8,128)} %flow.5), custom_call_target="tpu_custom_call" | custom-call | tf_op jit(solution)/shard_map/z_rims/pallas_call | solution.py:113
  1.2 0.7 collective-permute-start.1
  1.9 1.6 %collective-permute-start = (f32[3,64,4,128]{3,2,1,0:T(4,128)S(1)}, f32[3,64,4,128]{3,2,1,0:T(4,128)S(1)}, u32[]{:S(2)}, u32[]{:S(2)}) collective-permute-start(f32[3,64,4,128]{3,2,1,0:T(4,128)S(1)} %get-tuple-element.22.after), channel_id=1, source_target_pairs={{0,1},{1,2},{2,3},{3,4},{4,5},{5,6},{6,7},{7,8},{8,9},{9,10},{10,1... | collective-permute-start | bytes 1179656 | tf_op jit(solution)/shard_map/rim_exchange/ppermute | solution.py:490
  3.5 1.2 %x_rims.1 = (f32[4,4,64,128]{3,2,1,0:T(8,128)S(1)}, f32[4,4,64,128]{3,2,1,0:T(8,128)S(1)}) custom-call(f32[4,64,64,128]{3,2,1,0:T(8,128)} %flow.5, f32[3,64,4,128]{3,2,1,0:T(4,128)S(1)} %get-tuple-element.22.after), custom_call_target="tpu_custom_call" | custom-call | tf_op jit(solution)/shard_map/x_rims/pallas_call | solution.py:113
  4.7 0.0 copy-start
  4.7 3.1 %collective-permute-start.3 = (f32[4,4,64,128]{3,2,1,0:T(8,128)S(1)}, f32[4,4,64,128]{3,2,1,0:T(8,128)S(1)}, u32[]{:S(2)}, u32[]{:S(2)}) collective-permute-start(f32[4,4,64,128]{3,2,1,0:T(8,128)S(1)} %get-tuple-element.32), channel_id=1, source_target_pairs={{16,0},{32,16},{48,32},{64,48},{80,64},{96,80},{112,96},{17,1},{33... | collective-permute-start | bytes 1572872 | tf_op jit(solution)/shard_map/rim_exchange/ppermute | solution.py:507
  7.9 2.3 %collective-permute-start.2 = (f32[4,4,64,128]{3,2,1,0:T(8,128)S(1)}, f32[4,4,64,128]{3,2,1,0:T(8,128)S(1)}, u32[]{:S(2)}, u32[]{:S(2)}) collective-permute-start(f32[4,4,64,128]{3,2,1,0:T(8,128)S(1)} %get-tuple-element.23.after), channel_id=1, source_target_pairs={{0,16},{16,32},{32,48},{48,64},{64,80},{80,96},{96,112},{1,17},{17... | collective-permute-start | bytes 1572872 | tf_op jit(solution)/shard_map/rim_exchange/ppermute | solution.py:506
  10.2 3.5 %load.1.pad_in = f32[4,72,80,128]{3,2,1,0:T(8,128)S(1)} custom-call(f32[4,64,64,128]{3,2,1,0:T(8,128)} %flow.5, f32[4,4,64,128]{3,2,1,0:T(8,128)S(1)} %get-tuple-element.23.after), custom_call_target="tpu_custom_call" | custom-call | tf_op jit(solution)/shard_map/load/pallas_call | solution.py:113
  13.7 0.0 copy-done
  13.7 8.6 %base_moments.1 = (f32[4,72,80,128]{3,2,1,0:T(8,128)S(1)}, f32[4,64,64,128]{3,2,1,0:T(8,128)S(1)}, f32[4,64,128]{2,1,0:T(8,128)S(1)}, f32[19,64,128]{2,1,0:T(8,128)S(1)}) custom-call(f32[4,72,80,128]{3,2,1,0:T(8,128)S(1)} %load.1.pad_in, f32[128,128]{1,0:T(8,128)S(1)} %copy-done), custom_call_target="tpu_custom_call", output_to_operand_aliasing={{0}: (0, {})} | custom-call | flops 1000 | bytes 1000 | tf_op jit(solution)/shard_map/base_moments/pallas_call | solution.py:192
  22.3 0.0 collective-permute-done.1.zr
  22.4 0.0 collective-permute-done.zl
  22.4 9.6 %inner_moments.1 = (f32[4,72,80,128]{3,2,1,0:T(8,128)S(1)}, f32[47,32,128]{2,1,0:T(8,128)S(1)}, f32[47,32,128]{2,1,0:T(8,128)S(1)}) custom-call(f32[4,72,80,128]{3,2,1,0:T(8,128)S(1)} %get-tuple-element.24.pad_in, f32[4,64,64,128]{3,2,1,0:T(8,128)S(1)} %get-tuple-element.25.ysl, ...), custom_call_target="tpu_custom_call", output_to_operand_aliasing={{0}: (0, {})} | custom-call | flops 10485760000 | bytes 83886080 | tf_op jit(solution)/shard_map/inner_moments/pallas_call | solution.py:322
  31.9 0.0 collective-permute-done.3.xr
  31.9 0.0 collective-permute-done.2.xl
  32.0 1.6 %edge_moments.1 = (f32[4,72,80,128]{3,2,1,0:T(8,128)S(1)}, f32[47,32,128]{2,1,0:T(8,128)S(1)}, f32[47,32,128]{2,1,0:T(8,128)S(1)}) custom-call(f32[4,72,80,128]{3,2,1,0:T(8,128)S(1)} %get-tuple-element.29.pad_in, f32[47,32,128]{2,1,0:T(8,128)S(1)} %get-tuple-element.30.keep_in, ...), custom_call_target="tpu_custom_call", output_to_operand_aliasing={{0}: (0, {}), {1}: (1, {}), {2}: (2, {})} | custom-call | flops 52428800 | bytes 1048576 | tf_op jit(solution)/shard_map/edge_moments/pallas_call | solution.py:391
  33.5 5.0 %collective-permute-start.4 = (f32[47,32,128]{2,1,0:T(8,128)S(1)}, f32[47,32,128]{2,1,0:T(8,128)S(1)}, u32[]{:S(2)}, u32[]{:S(2)}) collective-permute-start(f32[47,32,128]{2,1,0:T(8,128)S(1)} %get-tuple-element.34), channel_id=1, source_target_pairs={{0,1},{1,0},{2,3},{3,2},{4,5},{5,4},{6,7},{7,6},{8,9},{9,8},{10,11... | collective-permute-start | bytes 2310152 | tf_op jit(solution)/shard_map/core_exchange/ppermute | solution.py:490
  38.5 1.9 %collective-permute-done.4.got = f32[47,32,128]{2,1,0:T(8,128)S(1)} collective-permute-done((f32[47,32,128]{2,1,0:T(8,128)S(1)}, f32[47,32,128]{2,1,0:T(8,128)S(1)}, u32[]{:S(2)}, u32[]{:S(2)}) %collective-permute-start.4) | collective-permute-done | bytes 770080 | tf_op jit(solution)/shard_map/core_exchange/ppermute | solution.py:490
  40.4 1.0 %core_merge.1 = (f32[47,8,128]{2,1,0:T(8,128)S(1)}, f32[47,8,128]{2,1,0:T(8,128)S(1)}, f32[47,8,128]{2,1,0:T(8,128)S(1)}, f32[47,8,128]{2,1,0:T(8,128)S(1)}) custom-call(f32[47,32,128]{2,1,0:T(8,128)S(1)} %get-tuple-element.33.keep, f32[47,32,128]{2,1,0:T(8,128)S(1)} %collective-permute-done.4.got, f32[128,128]{1,0:T(8,128)S(1)} %copy-done), custom_call_target="tpu_custom_call" | custom-call | tf_op jit(solution)/shard_map/core_merge/pallas_call | solution.py:477
  41.4 0.0 collective-permute-start.5
  41.4 3.6 %collective-permute-start.6 = (f32[47,8,128]{2,1,0:T(8,128)S(1)}, f32[47,8,128]{2,1,0:T(8,128)S(1)}, u32[]{:S(2)}, u32[]{:S(2)}) collective-permute-start(f32[47,8,128]{2,1,0:T(8,128)S(1)} %get-tuple-element.37), channel_id=1, source_target_pairs={{0,4},{2,6},{4,0},{6,2},{1,5},{3,7},{5,1},{7,3},{8,12},{10,14},{12... | collective-permute-start | bytes 577544 | tf_op jit(solution)/shard_map/span_exchange/ppermute | solution.py:490
  45.0 0.0 collective-permute-start.7
  45.0 3.7 %collective-permute-done.5.one = f32[47,8,128]{2,1,0:T(8,128)S(1)} collective-permute-done((f32[47,8,128]{2,1,0:T(8,128)S(1)}, f32[47,8,128]{2,1,0:T(8,128)S(1)}, u32[]{:S(2)}, u32[]{:S(2)}) %collective-permute-start.5) | collective-permute-done | bytes 192544 | tf_op jit(solution)/shard_map/span_exchange/ppermute | solution.py:490
  48.7 5.3 %collective-permute-done.6.two = f32[47,8,128]{2,1,0:T(8,128)S(1)} collective-permute-done((f32[47,8,128]{2,1,0:T(8,128)S(1)}, f32[47,8,128]{2,1,0:T(8,128)S(1)}, u32[]{:S(2)}, u32[]{:S(2)}) %collective-permute-start.6) | collective-permute-done | bytes 192544 | tf_op jit(solution)/shard_map/span_exchange/ppermute | solution.py:490
  53.9 0.0 collective-permute-done.7.three
  53.9 0.8 %span_merge.1.mine = f32[47,8,128]{2,1,0:T(8,128)S(1)} custom-call(f32[47,8,128]{2,1,0:T(8,128)S(1)} %get-tuple-element.35.own, f32[47,8,128]{2,1,0:T(8,128)S(1)} %collective-permute-done.5.one, f32[47,8,128]{2,1,0:T(8,128)S(1)} %collective-permute-done.6.two, f32[47,8,128]{2,1,0:T(8,128)S(1)} %collective-permute-done.7.three, f32[128,128]{1,0:T(8,128)S(1)} %copy-done), custom_call_target="tpu_custom_call" | custom-call | tf_op jit(solution)/shard_map/span_merge/pallas_call | solution.py:477
  54.8 2.7 %collective-permute-start.8 = (f32[47,8,128]{2,1,0:T(8,128)S(1)}, f32[47,8,128]{2,1,0:T(8,128)S(1)}, u32[]{:S(2)}, u32[]{:S(2)}) collective-permute-start(f32[47,8,128]{2,1,0:T(8,128)S(1)} %span_merge.1.mine), channel_id=1, source_target_pairs={{0,8},{8,0},{1,9},{9,1},{2,10},{10,2},{3,11},{11,3},{4,12},{12,4},... | collective-permute-start | bytes 577544 | tf_op jit(solution)/shard_map/x_exchange/ppermute | solution.py:490
  57.4 4.2 %collective-permute-done.8.other = f32[47,8,128]{2,1,0:T(8,128)S(1)} collective-permute-done((f32[47,8,128]{2,1,0:T(8,128)S(1)}, f32[47,8,128]{2,1,0:T(8,128)S(1)}, u32[]{:S(2)}, u32[]{:S(2)}) %collective-permute-start.8) | collective-permute-done | bytes 192544 | tf_op jit(solution)/shard_map/x_exchange/ppermute | solution.py:490
  61.6 0.4 last_merge.1.refs_0_
  62.0 3.1 %collective-permute-start.11 = (f32[40,8,128]{2,1,0:T(8,128)S(1)}, f32[40,8,128]{2,1,0:T(8,128)S(1)}, u32[]{:S(2)}, u32[]{:S(2)}) collective-permute-start(f32[40,8,128]{2,1,0:T(8,128)S(1)} %last_merge.1.refs_0_), channel_id=1, source_target_pairs={{0,6},{2,0},{4,2},{6,4},{1,7},{3,1},{5,3},{7,5},{8,14},{10,8},{12,... | collective-permute-start | bytes 491528 | tf_op jit(solution)/shard_map/spread/ppermute | solution.py:490
  65.1 0.0 collective-permute-start.10
  65.1 0.7 collective-permute-start.9
  65.8 1.9 %collective-permute-start.12 = (f32[40,8,128]{2,1,0:T(8,128)S(1)}, f32[40,8,128]{2,1,0:T(8,128)S(1)}, u32[]{:S(2)}, u32[]{:S(2)}) collective-permute-start(f32[40,8,128]{2,1,0:T(8,128)S(1)} %last_merge.1.refs_0_), channel_id=1, source_target_pairs={{0,1},{1,0},{2,3},{3,2},{4,5},{5,4},{6,7},{7,6},{8,9},{9,8},{10,11... | collective-permute-start | bytes 491528 | tf_op jit(solution)/shard_map/spread/ppermute | solution.py:490
  67.7 1.9 %collective-permute-done.11.refs_3_ = f32[40,8,128]{2,1,0:T(8,128)S(1)} collective-permute-done((f32[40,8,128]{2,1,0:T(8,128)S(1)}, f32[40,8,128]{2,1,0:T(8,128)S(1)}, u32[]{:S(2)}, u32[]{:S(2)}) %collective-permute-start.11) | collective-permute-done | bytes 163872 | tf_op jit(solution)/shard_map/spread/ppermute | solution.py:490
  69.6 3.5 %collective-permute-start.15 = (f32[40,8,128]{2,1,0:T(8,128)S(1)}, f32[40,8,128]{2,1,0:T(8,128)S(1)}, u32[]{:S(2)}, u32[]{:S(2)}) collective-permute-start(f32[40,8,128]{2,1,0:T(8,128)S(1)} %collective-permute-done.11.refs_3_), channel_id=1, source_target_pairs={{0,1},{1,0},{2,3},{3,2},{4,5},{5,4},{6,7},{7,6},{8,9},{9,8},{10,11... | collective-permute-start | bytes 491528 | tf_op jit(solution)/shard_map/spread/ppermute | solution.py:490
  73.1 0.0 collective-permute-done.10.refs_2_
  73.1 2.0 %collective-permute-start.14 = (f32[40,8,128]{2,1,0:T(8,128)S(1)}, f32[40,8,128]{2,1,0:T(8,128)S(1)}, u32[]{:S(2)}, u32[]{:S(2)}) collective-permute-start(f32[40,8,128]{2,1,0:T(8,128)S(1)} %collective-permute-done.10.refs_2_), channel_id=1, source_target_pairs={{0,1},{1,0},{2,3},{3,2},{4,5},{5,4},{6,7},{7,6},{8,9},{9,8},{10,11... | collective-permute-start | bytes 491528 | tf_op jit(solution)/shard_map/spread/ppermute | solution.py:490
  75.1 0.5 collective-permute-done.9.refs_1_
  75.6 0.9 %collective-permute-start.13 = (f32[40,8,128]{2,1,0:T(8,128)S(1)}, f32[40,8,128]{2,1,0:T(8,128)S(1)}, u32[]{:S(2)}, u32[]{:S(2)}) collective-permute-start(f32[40,8,128]{2,1,0:T(8,128)S(1)} %collective-permute-done.9.refs_1_), channel_id=1, source_target_pairs={{0,1},{1,0},{2,3},{3,2},{4,5},{5,4},{6,7},{7,6},{8,9},{9,8},{10,11... | collective-permute-start | bytes 491528 | tf_op jit(solution)/shard_map/spread/ppermute | solution.py:490
  76.5 0.0 collective-permute-done.12.refs_4_
  76.5 0.0 collective-permute-done.15.refs_7_
  76.5 0.0 collective-permute-done.14.refs_6_
  76.5 1.0 %collective-permute-done.13.refs_5_ = f32[40,8,128]{2,1,0:T(8,128)S(1)} collective-permute-done((f32[40,8,128]{2,1,0:T(8,128)S(1)}, f32[40,8,128]{2,1,0:T(8,128)S(1)}, u32[]{:S(2)}, u32[]{:S(2)}) %collective-permute-start.13) | collective-permute-done | bytes 163872 | tf_op jit(solution)/shard_map/spread/ppermute | solution.py:490
  77.5 1.2 %place.1 = f32[40,64,128]{2,1,0:T(8,128)} custom-call(f32[40,8,128]{2,1,0:T(8,128)S(1)} %last_merge.1.refs_0_, f32[40,8,128]{2,1,0:T(8,128)S(1)} %collective-permute-done.9.refs_1_, f32[40,8,128]{2,1,0:T(8,128)S(1)} %collective-permute-done.10.refs_2_, f32[40,8,128]{2,1,0:T(8,128)S(1)} %collective-permute-done.11.refs_3_, ...), custom_call_target="tpu_custom_call" | custom-call | tf_op jit(solution)/shard_map/place/pallas_call | solution.py:477
Async XLA Ops:
  1.2 21.2 %collective-permute-start.1 = (f32[3,64,4,128]{3,2,1,0:T(4,128)S(1)}, f32[3,64,4,128]{3,2,1,0:T(4,128)S(1)}, u32[]{:S(2)}, u32[]{:S(2)}) collective-permute-start(f32[3,64,4,128]{3,2,1,0:T(4,128)S(1)} %get-tuple-element.26), channel_id=1, source_target_pairs={{0,15},{1,0},{2,1},{3,2},{4,3},{5,4},{6,5},{7,6},{8,7},{9,8},{10,9... | collective-permute-start | bytes 1179656 | tf_op jit(solution)/shard_map/rim_exchange/ppermute | solution.py:490
  1.9 20.5 %collective-permute-start = (f32[3,64,4,128]{3,2,1,0:T(4,128)S(1)}, f32[3,64,4,128]{3,2,1,0:T(4,128)S(1)}, u32[]{:S(2)}, u32[]{:S(2)}) collective-permute-start(f32[3,64,4,128]{3,2,1,0:T(4,128)S(1)} %get-tuple-element.22.after), channel_id=1, source_target_pairs={{0,1},{1,2},{2,3},{3,4},{4,5},{5,6},{6,7},{7,8},{8,9},{9,10},{10,1... | collective-permute-start | bytes 1179656 | tf_op jit(solution)/shard_map/rim_exchange/ppermute | solution.py:490
  4.7 9.0 %copy-start = (f32[128,128]{1,0:T(8,128)S(1)}, f32[128,128]{1,0:T(8,128)}, u32[]{:S(2)}) copy-start(f32[128,128]{1,0:T(8,128)} %dy.7) | copy-start | bytes 196612
  4.7 27.2 %collective-permute-start.3 = (f32[4,4,64,128]{3,2,1,0:T(8,128)S(1)}, f32[4,4,64,128]{3,2,1,0:T(8,128)S(1)}, u32[]{:S(2)}, u32[]{:S(2)}) collective-permute-start(f32[4,4,64,128]{3,2,1,0:T(8,128)S(1)} %get-tuple-element.32), channel_id=1, source_target_pairs={{16,0},{32,16},{48,32},{64,48},{80,64},{96,80},{112,96},{17,1},{33... | collective-permute-start | bytes 1572872 | tf_op jit(solution)/shard_map/rim_exchange/ppermute | solution.py:507
  7.9 24.1 %collective-permute-start.2 = (f32[4,4,64,128]{3,2,1,0:T(8,128)S(1)}, f32[4,4,64,128]{3,2,1,0:T(8,128)S(1)}, u32[]{:S(2)}, u32[]{:S(2)}) collective-permute-start(f32[4,4,64,128]{3,2,1,0:T(8,128)S(1)} %get-tuple-element.23.after), channel_id=1, source_target_pairs={{0,16},{16,32},{32,48},{48,64},{64,80},{80,96},{96,112},{1,17},{17... | collective-permute-start | bytes 1572872 | tf_op jit(solution)/shard_map/rim_exchange/ppermute | solution.py:506
  33.5 6.9 %collective-permute-start.4 = (f32[47,32,128]{2,1,0:T(8,128)S(1)}, f32[47,32,128]{2,1,0:T(8,128)S(1)}, u32[]{:S(2)}, u32[]{:S(2)}) collective-permute-start(f32[47,32,128]{2,1,0:T(8,128)S(1)} %get-tuple-element.34), channel_id=1, source_target_pairs={{0,1},{1,0},{2,3},{3,2},{4,5},{5,4},{6,7},{7,6},{8,9},{9,8},{10,11... | collective-permute-start | bytes 2310152 | tf_op jit(solution)/shard_map/core_exchange/ppermute | solution.py:490
  41.4 7.2 %collective-permute-start.5 = (f32[47,8,128]{2,1,0:T(8,128)S(1)}, f32[47,8,128]{2,1,0:T(8,128)S(1)}, u32[]{:S(2)}, u32[]{:S(2)}) collective-permute-start(f32[47,8,128]{2,1,0:T(8,128)S(1)} %get-tuple-element.36), channel_id=1, source_target_pairs={{0,2},{2,4},{4,6},{6,0},{1,3},{3,5},{5,7},{7,1},{8,10},{10,12},{12... | collective-permute-start | bytes 577544 | tf_op jit(solution)/shard_map/span_exchange/ppermute | solution.py:490
  41.4 12.5 %collective-permute-start.6 = (f32[47,8,128]{2,1,0:T(8,128)S(1)}, f32[47,8,128]{2,1,0:T(8,128)S(1)}, u32[]{:S(2)}, u32[]{:S(2)}) collective-permute-start(f32[47,8,128]{2,1,0:T(8,128)S(1)} %get-tuple-element.37), channel_id=1, source_target_pairs={{0,4},{2,6},{4,0},{6,2},{1,5},{3,7},{5,1},{7,3},{8,12},{10,14},{12... | collective-permute-start | bytes 577544 | tf_op jit(solution)/shard_map/span_exchange/ppermute | solution.py:490
  45.0 8.9 %collective-permute-start.7 = (f32[47,8,128]{2,1,0:T(8,128)S(1)}, f32[47,8,128]{2,1,0:T(8,128)S(1)}, u32[]{:S(2)}, u32[]{:S(2)}) collective-permute-start(f32[47,8,128]{2,1,0:T(8,128)S(1)} %get-tuple-element.38), channel_id=1, source_target_pairs={{0,6},{2,0},{4,2},{6,4},{1,7},{3,1},{5,3},{7,5},{8,14},{10,8},{12,... | collective-permute-start | bytes 577544 | tf_op jit(solution)/shard_map/span_exchange/ppermute | solution.py:490
  54.8 6.9 %collective-permute-start.8 = (f32[47,8,128]{2,1,0:T(8,128)S(1)}, f32[47,8,128]{2,1,0:T(8,128)S(1)}, u32[]{:S(2)}, u32[]{:S(2)}) collective-permute-start(f32[47,8,128]{2,1,0:T(8,128)S(1)} %span_merge.1.mine), channel_id=1, source_target_pairs={{0,8},{8,0},{1,9},{9,1},{2,10},{10,2},{3,11},{11,3},{4,12},{12,4},... | collective-permute-start | bytes 577544 | tf_op jit(solution)/shard_map/x_exchange/ppermute | solution.py:490
  62.0 7.5 %collective-permute-start.11 = (f32[40,8,128]{2,1,0:T(8,128)S(1)}, f32[40,8,128]{2,1,0:T(8,128)S(1)}, u32[]{:S(2)}, u32[]{:S(2)}) collective-permute-start(f32[40,8,128]{2,1,0:T(8,128)S(1)} %last_merge.1.refs_0_), channel_id=1, source_target_pairs={{0,6},{2,0},{4,2},{6,4},{1,7},{3,1},{5,3},{7,5},{8,14},{10,8},{12,... | collective-permute-start | bytes 491528 | tf_op jit(solution)/shard_map/spread/ppermute | solution.py:490
  65.1 7.9 %collective-permute-start.10 = (f32[40,8,128]{2,1,0:T(8,128)S(1)}, f32[40,8,128]{2,1,0:T(8,128)S(1)}, u32[]{:S(2)}, u32[]{:S(2)}) collective-permute-start(f32[40,8,128]{2,1,0:T(8,128)S(1)} %last_merge.1.refs_0_), channel_id=1, source_target_pairs={{0,4},{2,6},{4,0},{6,2},{1,5},{3,7},{5,1},{7,3},{8,12},{10,14},{12... | collective-permute-start | bytes 491528 | tf_op jit(solution)/shard_map/spread/ppermute | solution.py:490
  65.1 10.5 %collective-permute-start.9 = (f32[40,8,128]{2,1,0:T(8,128)S(1)}, f32[40,8,128]{2,1,0:T(8,128)S(1)}, u32[]{:S(2)}, u32[]{:S(2)}) collective-permute-start(f32[40,8,128]{2,1,0:T(8,128)S(1)} %last_merge.1.refs_0_), channel_id=1, source_target_pairs={{0,2},{2,4},{4,6},{6,0},{1,3},{3,5},{5,7},{7,1},{8,10},{10,12},{12... | collective-permute-start | bytes 491528 | tf_op jit(solution)/shard_map/spread/ppermute | solution.py:490
  65.8 10.7 %collective-permute-start.12 = (f32[40,8,128]{2,1,0:T(8,128)S(1)}, f32[40,8,128]{2,1,0:T(8,128)S(1)}, u32[]{:S(2)}, u32[]{:S(2)}) collective-permute-start(f32[40,8,128]{2,1,0:T(8,128)S(1)} %last_merge.1.refs_0_), channel_id=1, source_target_pairs={{0,1},{1,0},{2,3},{3,2},{4,5},{5,4},{6,7},{7,6},{8,9},{9,8},{10,11... | collective-permute-start | bytes 491528 | tf_op jit(solution)/shard_map/spread/ppermute | solution.py:490
  69.6 6.9 %collective-permute-start.15 = (f32[40,8,128]{2,1,0:T(8,128)S(1)}, f32[40,8,128]{2,1,0:T(8,128)S(1)}, u32[]{:S(2)}, u32[]{:S(2)}) collective-permute-start(f32[40,8,128]{2,1,0:T(8,128)S(1)} %collective-permute-done.11.refs_3_), channel_id=1, source_target_pairs={{0,1},{1,0},{2,3},{3,2},{4,5},{5,4},{6,7},{7,6},{8,9},{9,8},{10,11... | collective-permute-start | bytes 491528 | tf_op jit(solution)/shard_map/spread/ppermute | solution.py:490
  73.1 3.4 %collective-permute-start.14 = (f32[40,8,128]{2,1,0:T(8,128)S(1)}, f32[40,8,128]{2,1,0:T(8,128)S(1)}, u32[]{:S(2)}, u32[]{:S(2)}) collective-permute-start(f32[40,8,128]{2,1,0:T(8,128)S(1)} %collective-permute-done.10.refs_2_), channel_id=1, source_target_pairs={{0,1},{1,0},{2,3},{3,2},{4,5},{5,4},{6,7},{7,6},{8,9},{9,8},{10,11... | collective-permute-start | bytes 491528 | tf_op jit(solution)/shard_map/spread/ppermute | solution.py:490
  75.6 1.9 %collective-permute-start.13 = (f32[40,8,128]{2,1,0:T(8,128)S(1)}, f32[40,8,128]{2,1,0:T(8,128)S(1)}, u32[]{:S(2)}, u32[]{:S(2)}) collective-permute-start(f32[40,8,128]{2,1,0:T(8,128)S(1)} %collective-permute-done.9.refs_1_), channel_id=1, source_target_pairs={{0,1},{1,0},{2,3},{3,2},{4,5},{5,4},{6,7},{7,6},{8,9},{9,8},{10,11... | collective-permute-start | bytes 491528 | tf_op jit(solution)/shard_map/spread/ppermute | solution.py:490

commit v3 on v2

v3 whole, which is shorter than its diff:
```python
import functools

import jax
import jax.numpy as jnp
from jax import lax
from jax.experimental import pallas as pl
from jax.experimental.pallas import tpu as pltpu
from jax.sharding import Mesh, PartitionSpec as P

F32 = jnp.float32
BF16 = jnp.bfloat16
lead = 4.0 / 5.0
ratios = (1.0, -0.25, 1.0 / 21.0, -1.0 / 224.0)
pairs = ((0, 0), (0, 1), (0, 2), (1, 1), (1, 2), (2, 2))
triples = (
    (0, 0, 0), (0, 0, 1), (0, 0, 2), (0, 1, 1), (0, 1, 2),
    (0, 2, 2), (1, 1, 1), (1, 1, 2), (1, 2, 2), (2, 2, 2),
)
MEAN, UU, UUU, PU, DXM, PG, GG, UG = 0, 4, 10, 20, 23, 27, 33, 39
FIRST = 23
STATE = 44
OUT = 40
NBASE = 19
NSLOPE = 22
GXA, ZA, CA = "gx", ("xh", "z", "c"), "c"


def combine_base(left, right, count, put):
    half = [0.5 * (left(MEAN + c) - right(MEAN + c)) for c in range(4)]
    nh = [float(2 * count) * h for h in half]
    for c in range(4):
        put(MEAN + c, 0.5 * (left(MEAN + c) + right(MEAN + c)))
    gap = {}
    for k, (i, j) in enumerate(pairs):
        a, b = left(UU + k), right(UU + k)
        gap[i, j] = gap[j, i] = a - b
        put(UU + k, (a + b) + nh[i] * half[j])
    for k, (i, j, l) in enumerate(triples):
        fix = half[i] * gap[j, l] + half[j] * gap[i, l] + half[l] * gap[i, j]
        put(UUU + k, (left(UUU + k) + right(UUU + k)) + fix)
    for c in range(3):
        put(PU + c, (left(PU + c) + right(PU + c)) + nh[3] * half[c])


def combine_slopes(left, right, count, dmat, put):
    half = [0.5 * (left(MEAN + c) - right(MEAN + c)) for c in range(4)]
    gx = [0.5 * (left(DXM + c) - right(DXM + c)) for c in range(4)]
    rows = half[0].shape[0]
    turned = jnp.dot(
        jnp.concatenate(half, axis=0), dmat,
        precision=lax.Precision.HIGHEST, preferred_element_type=F32,
    )
    gy = [turned[c * rows : (c + 1) * rows] for c in range(4)]
    both = float(2 * count)
    nh = [both * h for h in half]
    for c in range(4):
        put(DXM + c, 0.5 * (left(DXM + c) + right(DXM + c)))
    fixes = (
        2.0 * nh[3] * gx[0],
        nh[3] * (gy[0] + gx[1]),
        nh[3] * gx[2],
        2.0 * nh[3] * gy[1],
        nh[3] * gy[2],
    )
    for k in range(5):
        put(PG + k, (left(PG + k) + right(PG + k)) + fixes[k])
    put(PG + 5, left(PG + 5) + right(PG + 5))
    for k, (i, j) in enumerate(pairs):
        fix = both * (gx[i] * gx[j] + gy[i] * gy[j])
        put(GG + k, (left(GG + k) + right(GG + k)) + fix)
    fixes = (
        2.0 * nh[0] * gx[3],
        nh[0] * gy[3] + nh[1] * gx[3],
        nh[2] * gx[3],
        2.0 * nh[1] * gy[3],
        nh[2] * gy[3],
    )
    for k in range(5):
        put(UG + k, (left(UG + k) + right(UG + k)) - fixes[k])


def copy_all(copies):
    for c in copies:
        c.start()
    for c in copies:
        c.wait()


def rim_kernel(flow, zl, zr, xl, xr, sems):
    _, lx, lz, _ = flow.shape
    copy_all([
        pltpu.make_async_copy(flow.at[pl.ds(0, 3), :, pl.ds(lz - 4, 4)], zl, sems.at[0]),
        pltpu.make_async_copy(flow.at[pl.ds(0, 3), :, pl.ds(0, 4)], zr, sems.at[1]),
        pltpu.make_async_copy(flow.at[:, pl.ds(lx - 4, 4)], xl, sems.at[2]),
        pltpu.make_async_copy(flow.at[:, pl.ds(0, 4)], xr, sems.at[3]),
    ])


def cut(kernel, shapes, copies, name, flow, *after):
    flow = pltpu.with_memory_space_constraint(flow, pltpu.HBM)
    return pl.pallas_call(
        kernel,
        in_specs=[pl.BlockSpec(memory_space=pltpu.HBM)]
        + [pl.BlockSpec(memory_space=pl.ANY)] * len(after),
        out_specs=[pl.BlockSpec(memory_space=pltpu.VMEM)] * len(shapes),
        out_shape=[pltpu.VMEM(s, F32) for s in shapes],
        scratch_shapes=[pltpu.SemaphoreType.DMA((copies,))],
        compiler_params=pltpu.CompilerParams(vmem_limit_bytes=4 * 2**20),
        name=name,
    )(flow, *after)


def base_kernel(flow, dy, pad, ysl, mean, keep, send, dmat, acc, weights, sems):
    _, lx, lz, ny = ysl.shape
    half = lx // 2
    core = lax.axis_index(CA)
    step = 8
    parts = lx // step

    def fetch(k):
        return pltpu.make_async_copy(
            flow.at[:, pl.ds(step * k, step)],
            pad.at[:, pl.ds(step * k + 4, step), pl.ds(8, lz)],
            sems.at[k],
        )

    for k in range(parts):
        fetch(k).start()

    d = dy[...].T * (1.0 / lead)
    dmat[...] = d
    dhi = d.astype(BF16)
    dlo = (d - dhi.astype(F32)).astype(BF16)
    weights[pl.ds(0, ny), pl.ds(0, ny)] = dhi
    weights[pl.ds(0, ny), pl.ds(ny, ny)] = dlo
    weights[pl.ds(ny, ny), pl.ds(0, ny)] = dhi
    weights[pl.ds(ny, ny), pl.ds(ny, ny)] = jnp.zeros_like(dlo)

    def part(k, _):
        fetch(k).wait()
        left = []
        for r in range(step):
            x = step * k + r
            for c in range(4):
                f = pad[c, x + 4, pl.ds(8, lz), :]
                m = jnp.sum(f, axis=0, keepdims=True) * (1.0 / lz)
                mean[c, pl.ds(x, 1), :] = m
                a = f - m
                pad[c, x + 4, pl.ds(8, lz), :] = a
                hi = a.astype(BF16)
                lo = (a - hi.astype(F32)).astype(BF16)
                left.append(jnp.concatenate([hi, lo], axis=1))
        y = jnp.dot(jnp.concatenate(left, axis=0), weights[...], preferred_element_type=F32)
        for r in range(step):
            x = step * k + r
            total = [None] * NBASE

            def add(n, v):
                total[n] = v if total[n] is None else total[n] + v

            for b in range(lz // 8):
                f = [pad[c, x + 4, pl.ds(8 + 8 * b, 8), :] for c in range(4)]
                prod = {}
                for n, (i, j) in enumerate(pairs):
                    prod[i, j] = f[i] * f[j]
                    add(n, prod[i, j])
                for n, (i, j, l) in enumerate(triples):
                    add(6 + n, prod[i, j] * f[l])
                for c in range(3):
                    add(16 + c, f[3] * f[c])
            for n in range(NBASE):
                acc[pl.ds(pl.multiple_of(n * 8 * lx + 8 * x, 8), 8), :] = total[n]
        y = y[:, :ny] + y[:, ny:]
        for r in range(step):
            for c in range(4):
                at = (4 * r + c) * lz
                ysl[c, step * k + r] = y[at : at + lz]
        return 0

    lax.fori_loop(0, parts, part, 0)
    for out, side in ((send, 1 - core), (keep, core)):
        at = pl.multiple_of(half * side, 8)
        for c in range(4):
            out[MEAN + c] = mean[c, pl.ds(at, half), :]
        for k in range(NBASE):
            out[UU + k] = half_sum(k, acc, lx, at)


def row_sum(k, rows, acc):
    return sum(acc[pl.ds(8 * k * rows + s, rows, stride=8), :] for s in range(8))


def half_sum(k, acc, rows, at):
    where = pl.multiple_of(8 * (k * rows + at), 8)
    return sum(acc[pl.ds(where + s, rows // 2, stride=8), :] for s in range(8))


def base_moments(flow, dy):
    _, lx, lz, ny = flow.shape
    vm = pl.BlockSpec(memory_space=pltpu.VMEM)
    half = (FIRST, lx // 2, ny)
    shapes = [
        (4, lx + 8, lz + 16, ny), (4, lx, lz, ny), (4, lx, ny), half, half, (ny, ny),
    ]
    return pl.pallas_call(
        base_kernel,
        in_specs=[pl.BlockSpec(memory_space=pltpu.HBM), vm],
        out_specs=[vm] * 6,
        out_shape=[pltpu.VMEM(s, F32) for s in shapes],
        scratch_shapes=[
            pltpu.VMEM((NBASE * 8 * lx, ny), F32),
            pltpu.VMEM((2 * ny, 2 * ny), BF16),
            pltpu.SemaphoreType.DMA((lx // 8,)),
        ],
        compiler_params=pltpu.CompilerParams(vmem_limit_bytes=16 * 2**20),
        cost_estimate=pl.CostEstimate(flops=1000, bytes_accessed=1000, transcendentals=0),
        name="base_moments",
    )(pltpu.with_memory_space_constraint(flow, pltpu.HBM), dy)


def difference(upper, lower):
    out = None
    for k in range(4):
        diff = upper(k) - lower(k)
        out = diff if out is None else out + ratios[k] * diff
    return out


def slope_row(pad, ysl, x):
    lz, ny = ysl.shape[2:]
    total = [None] * NSLOPE
    row = lax.broadcasted_iota(jnp.int32, (8, ny), 0)
    row = jnp.minimum(row, 7 - row)
    weight = jnp.full((8, ny), sum(ratios), F32)
    for k in range(3):
        weight = jnp.where(row == k, sum(ratios[3 - k :]), weight)
    for c in range(3):
        total[c] = weight * (
            pad[c, x + 4, pl.ds(4 + lz, 8), :] - pad[c, x + 4, pl.ds(4, 8), :]
        )

    def add(k, v):
        total[k] = v if total[k] is None else total[k] + v

    for b in range(lz // 8):
        at = 8 + 8 * b
        u = [pad[c, x + 4, pl.ds(at, 8), :] for c in range(4)]
        p = u[3]
        g = [[None] * 3 for _ in range(4)]
        for c in range(4):
            g[c][0] = difference(
                lambda k: pad[c, x + 5 + k, pl.ds(at, 8), :],
                lambda k: pad[c, x + 3 - k, pl.ds(at, 8), :],
            )
            g[c][1] = ysl[c, x, pl.ds(8 * b, 8), :]
        for c in range(3):
            g[c][2] = difference(
                lambda k: pad[c, x + 4, pl.ds(at + 1 + k, 8), :],
                lambda k: pad[c, x + 4, pl.ds(at - 1 - k, 8), :],
            )
        add(3, p * g[0][0])
        add(4, p * (g[0][1] + g[1][0]))
        add(5, p * g[0][2])
        add(6, p * g[2][0])
        add(7, p * g[1][1])
        add(8, p * g[1][2])
        add(9, p * g[2][1])
        add(10, p * g[2][2])
        for k, (i, j) in enumerate(pairs):
            for dim in range(3):
                add(11 + k, g[i][dim] * g[j][dim])
        add(17, u[0] * g[3][0])
        add(18, u[0] * g[3][1] + u[1] * g[3][0])
        add(19, u[1] * g[3][1])
        add(20, u[2] * g[3][0])
        add(21, u[2] * g[3][1])
    return total


def slope_fields(total, pressure):
    s02, s12, s22 = (total(n) + pressure * total(c) for c, n in enumerate((5, 8, 10)))
    yield PG + 0, 2.0 * total(3)
    yield PG + 1, total(4)
    yield PG + 2, s02 + total(6)
    yield PG + 3, 2.0 * total(7)
    yield PG + 4, s12 + total(9)
    yield PG + 5, 2.0 * s22
    for k in range(6):
        yield GG + k, total(11 + k)
    yield UG + 0, -2.0 * total(17)
    yield UG + 1, -total(18)
    yield UG + 2, s02 - total(20)
    yield UG + 3, -2.0 * total(19)
    yield UG + 4, s12 - total(21)


def inner_kernel(pad_in, ysl, zl, zr, mean, after, pad, keep, send, acc):
    _, lx, lz, ny = ysl.shape
    half = lx // 2
    core = lax.axis_index(CA)

    def rim(x, _):
        for c in range(3):
            m = mean[c, pl.ds(x, 1), :]
            pad[c, x + 4, pl.ds(4, 4), :] = zl[c, x] - m
            pad[c, x + 4, pl.ds(8 + lz, 4), :] = zr[c, x] - m
        return 0

    lax.fori_loop(0, lx, rim, 0, unroll=4)

    def one(x, _):
        total = slope_row(pad, ysl, x)
        for k in range(NSLOPE):
            acc[pl.ds(pl.multiple_of(k * 8 * lx + 8 * x, 8), 8), :] = total[k]
        return 0

    lax.fori_loop(4, lx - 4, one, 0)

    for out, side in ((send, 1 - core), (keep, core)):
        at = pl.multiple_of(half * side, 8)

        fields = slope_fields(
            lambda k, at=at: half_sum(k, acc, lx, at), mean[3, pl.ds(at, half), :]
        )
        for f, v in fields:
            out[f - FIRST] = v


def inner_moments(pad, ysl, zl, zr, mean, after):
    _, lx, lz, ny = ysl.shape
    vm = pl.BlockSpec(memory_space=pltpu.VMEM)
    shape = pltpu.VMEM((STATE - FIRST, lx // 2, ny), F32)
    return pl.pallas_call(
        inner_kernel,
        in_specs=[vm] * 5 + [pl.BlockSpec(memory_space=pl.ANY)],
        out_specs=[vm] * 3,
        out_shape=[pltpu.VMEM(pad.shape, F32), shape, shape],
        input_output_aliases={0: 0},
        scratch_shapes=[pltpu.VMEM((NSLOPE * 8 * lx, ny), F32)],
        compiler_params=pltpu.CompilerParams(vmem_limit_bytes=16 * 2**20),
        cost_estimate=pl.CostEstimate(
            flops=1500000000, bytes_accessed=84_000_000, transcendentals=0
        ),
        name="inner_moments",
    )(pad, ysl, zl, zr, mean, after)


def edge_kernel(
    pad_in, keep_in, send_in, ysl, xl, xr, mean, after, pad, keep, send, acc, mpad, dxm
):
    _, lx, lz, ny = ysl.shape
    half = lx // 2
    core = lax.axis_index(CA)
    gi = lax.axis_index(GXA)
    at_ends = (gi == 0, gi == lax.axis_size(GXA) - 1)

    for c in range(4):
        mpad[c, pl.ds(8, lx), :] = mean[c]
        for j in range(4):
            for halo, at_end, src, dst in (
                (xl, at_ends[0], 3 - j, j), (xr, at_ends[1], lx - 1 - j, lx + 4 + j)
            ):
                own = pad[c, src + 4, pl.ds(8, lz), :]
                m = jnp.sum(halo[c, j], axis=0, keepdims=True) * (1.0 / lz)
                pad[c, dst, pl.ds(8, lz), :] = jnp.where(at_end, own, halo[c, j] - m)
                mpad[c, pl.ds(dst + 4, 1), :] = jnp.where(at_end, mean[c, pl.ds(src, 1), :], m)
        dxm[c] = difference(
            lambda k: mpad[c, pl.ds(9 + k, lx), :], lambda k: mpad[c, pl.ds(7 - k, lx), :]
        )

    for out, side in ((send, 1 - core), (keep, core)):
        for c in range(4):
            out[DXM - FIRST + c] = dxm[c, pl.ds(pl.multiple_of(half * side, 8), half), :]

    def one(i, _):
        x = jnp.where(i < 4, i, lx - 8 + i)
        total = slope_row(pad, ysl, x)
        for k in range(NSLOPE):
            acc[pl.ds(pl.multiple_of(k * 64 + 8 * i, 8), 8), :] = total[k]
        return 0

    lax.fori_loop(0, 8, one, 0)

    pressure = jnp.concatenate([mean[3, pl.ds(0, 4), :], mean[3, pl.ds(lx - 4, 4), :]], axis=0)
    fields = list(slope_fields(lambda k: row_sum(k, 8, acc), pressure))
    for side, rows in ((0, slice(0, 4)), (1, slice(4, 8))):
        at = 0 if side == 0 else half - 4

        @pl.when(core == side)
        def _():
            for f, v in fields:
                keep[f - FIRST, pl.ds(at, 4), :] = v[rows]

        @pl.when(core != side)
        def _():
            for f, v in fields:
                send[f - FIRST, pl.ds(at, 4), :] = v[rows]


def edge_moments(pad, keep, send, ysl, xl, xr, mean, after):
    _, lx, lz, ny = ysl.shape
    vm = pl.BlockSpec(memory_space=pltpu.VMEM)
    out = pl.pallas_call(
        edge_kernel,
        in_specs=[vm] * 7 + [pl.BlockSpec(memory_space=pl.ANY)],
        out_specs=[vm] * 3,
        out_shape=[pltpu.VMEM(v.shape, F32) for v in (pad, keep, send)],
        input_output_aliases={0: 0, 1: 1, 2: 2},
        scratch_shapes=[
            pltpu.VMEM((NSLOPE * 64, ny), F32),
            pltpu.VMEM((4, lx + 16, ny), F32),
            pltpu.VMEM((4, lx, ny), F32),
        ],
        compiler_params=pltpu.CompilerParams(vmem_limit_bytes=16 * 2**20),
        cost_estimate=pl.CostEstimate(
            flops=25 * ysl.size, bytes_accessed=ysl.size // 2, transcendentals=0
        ),
        name="edge_moments",
    )(pad, keep, send, ysl, xl, xr, mean, after)
    return out[1:]


def picker(one, two=None):
    return lambda f: one[f] if f < FIRST else two[f - FIRST]


def storer(one, two=None):
    def put(f, v):
        if f < FIRST:
            one[f] = v
        else:
            two[f - FIRST] = v
    return put


def z_places(rows):
    zi = lax.axis_index("z")
    zn = lax.axis_size("z")
    return [pl.multiple_of(rows * lax.rem(zi + k, zn), 8) for k in (0, 1, zn - 1, 2)]


def core_base_kernel(count, keep, got, *outs):
    rows = outs[0].shape[1]
    for out, at in zip(outs, z_places(rows)):
        combine_base(
            lambda f, at=at: keep[f, pl.ds(at, rows), :],
            lambda f, at=at: got[f, pl.ds(at, rows), :],
            count, storer(out),
        )


def core_slope_kernel(count, keep1, got1, keep2, got2, dmat, *outs):
    rows = outs[0].shape[1]
    places = z_places(rows)

    def pick(one, two):
        def field(f):
            ref, k = (one, f) if f < FIRST else (two, f - FIRST)
            return jnp.concatenate([ref[k, pl.ds(at, rows), :] for at in places], axis=0)
        return field

    def put(f, v):
        for n, ref in enumerate(outs):
            ref[f - FIRST] = v[rows * n : rows * (n + 1)]

    combine_slopes(pick(keep1, keep2), pick(got1, got2), count, dmat[...], put)


def span_base_kernel(count, own, one, two, three, out, left, right):
    combine_base(picker(own), picker(one), count, storer(left))
    combine_base(picker(two), picker(three), count, storer(right))
    combine_base(picker(left), picker(right), 2 * count, storer(out))


def span_slope_kernel(count, *refs):
    base, (own, one, two, three) = refs[:4], refs[4:8]
    left1, right1, dmat, out, left, right = refs[8:]
    d = dmat[...]
    combine_slopes(picker(base[0], own), picker(base[1], one), count, d, storer(None, left))
    combine_slopes(picker(base[2], two), picker(base[3], three), count, d, storer(None, right))
    combine_slopes(
        picker(left1, left), picker(right1, right), 2 * count, d, storer(None, out)
    )


def last_base_kernel(count, mine, other, out, state):
    combine_base(picker(mine), picker(other), count, storer(state))
    scale = 1.0 / (2 * count)
    for c in range(3):
        out[c] = state[MEAN + c]
    for k in range(NBASE):
        out[3 + k] = state[UU + k] * scale


def last_slope_kernel(count, mine1, other1, mine2, other2, dmat, out, state):
    combine_slopes(
        picker(mine1, mine2), picker(other1, other2), count, dmat[...], storer(None, state)
    )
    scale = 1.0 / (2 * count)
    for k in range(6):
        out[k] = state[PG - FIRST + k] * (scale * lead)
        out[6 + k] = state[GG - FIRST + k] * (scale * lead * lead)
    for k in range(5):
        out[12 + k] = state[UG - FIRST + k] * (scale * lead)
    out[17] = state[PG - FIRST + 5] * (scale * lead)


def place_kernel(first, *refs):
    ins, out, sems = refs[:8], refs[-2], refs[-1]
    fields, rows = ins[0].shape[:2]
    zi = lax.axis_index("z")
    zn = lax.axis_size("z")
    core = lax.axis_index(CA)
    copies = []
    for k, ref in enumerate(ins):
        side, step = divmod(k, zn)
        c = core if side == 0 else 1 - core
        at = pl.multiple_of(rows * (zn * c + lax.rem(zi + zn - step, zn)), 8)
        copies.append(
            pltpu.make_async_copy(
                ref, out.at[pl.ds(first, fields), pl.ds(at, rows)], sems.at[k]
            )
        )
    copy_all(copies)


def place(first, pieces, shape, name, base=None):
    hbm = pl.BlockSpec(memory_space=pltpu.HBM)
    extra = [] if base is None else [base]
    return pl.pallas_call(
        functools.partial(place_kernel, first),
        in_specs=[pl.BlockSpec(memory_space=pltpu.VMEM)] * len(pieces) + [hbm] * len(extra),
        out_specs=hbm,
        out_shape=pltpu.HBM(shape, F32),
        input_output_aliases={} if base is None else {len(pieces): 0},
        scratch_shapes=[pltpu.SemaphoreType.DMA((len(pieces),))],
        compiler_params=pltpu.CompilerParams(vmem_limit_bytes=4 * 2**20),
        name=name,
    )(*pieces, *extra)


def small_call(kernel, outs, scratch, name, *args):
    vm = pl.BlockSpec(memory_space=pltpu.VMEM)
    return pl.pallas_call(
        kernel,
        in_specs=[vm] * len(args),
        out_specs=[vm] * len(outs),
        out_shape=[pltpu.VMEM(s, F32) for s in outs],
        scratch_shapes=[pltpu.VMEM(s, F32) for s in scratch],
        compiler_params=pltpu.CompilerParams(vmem_limit_bytes=8 * 2**20),
        cost_estimate=pl.CostEstimate(flops=1000, bytes_accessed=1000, transcendentals=0),
        name=name,
    )(*args)


def send(value, axis, step):
    size = lax.axis_size(axis)
    return lax.ppermute(value, axis, [(i, (i + step) % size) for i in range(size)])


def shards(flow, dy):
    _, lx, lz, ny = flow.shape
    gn = lax.axis_size(GXA)
    zn = lax.axis_size("z")
    up = [(i, i + 1) for i in range(gn - 1)]
    down = [(i + 1, i) for i in range(gn - 1)]
    zs, xs = (3, lx, 4, ny), (4, 4, lz, ny)
    zl, zr, xl, xr = cut(rim_kernel, [zs, zs, xs, xs], 4, "rims", flow)
    with jax.named_scope("rim_exchange"):
        zl = send(zl, ZA, 1)
        zr = send(zr, ZA, -1)
        xl = lax.ppermute(xl, GXA, up)
        xr = lax.ppermute(xr, GXA, down)
    pad, ysl, mean, keep1, give1, dmat = base_moments(flow, dy)
    rows = lx // 2 // zn
    one_piece, two_piece = (FIRST, rows, ny), (STATE - FIRST, rows, ny)

    def along_z(own, up, down, far):
        return [own, send(up, "z", 1), send(far, "z", 2), send(down, "z", -1)]

    def spread(done):
        mine = [done] + [send(done, "z", k) for k in (1, 2, 3)]
        return mine + [send(v, CA, 1) for v in mine]

    with jax.named_scope("base_core"):
        got1 = send(give1, CA, 1)
        parts1 = small_call(
            functools.partial(core_base_kernel, lz), [one_piece] * 4, [], "core_base", keep1, got1
        )
    with jax.named_scope("base_span"):
        pieces1 = along_z(*parts1)
    pad, keep2, give2 = inner_moments(pad, ysl, zl, zr, mean, parts1[0])
    with jax.named_scope("base_span"):
        part1, left1, right1 = small_call(
            functools.partial(span_base_kernel, 2 * lz), [one_piece] * 3, [], "span_base", *pieces1
        )
    with jax.named_scope("base_x"):
        other1 = send(part1, "xh", 1)
        (done1,) = small_call(
            functools.partial(last_base_kernel, 2 * zn * lz),
            [(FIRST - 1, rows, ny)], [one_piece], "last_base", part1, other1,
        )
    with jax.named_scope("base_spread"):
        out1 = place(0, spread(done1), (OUT, lx, ny), "place_base")
    keep2, give2 = edge_moments(pad, keep2, give2, ysl, xl, xr, mean, part1)
    with jax.named_scope("slope_core"):
        got2 = send(give2, CA, 1)
        parts2 = small_call(
            functools.partial(core_slope_kernel, lz), [two_piece] * 4, [], "core_slope",
            keep1, got1, keep2, got2, dmat,
        )
    with jax.named_scope("slope_span"):
        pieces2 = along_z(*parts2)
        (part2,) = small_call(
            functools.partial(span_slope_kernel, 2 * lz), [two_piece], [two_piece] * 2,
            "span_slope", *pieces1, *pieces2, left1, right1, dmat,
        )
    with jax.named_scope("slope_x"):
        other2 = send(part2, "xh", 1)
        (done2,) = small_call(
            functools.partial(last_slope_kernel, 2 * zn * lz),
            [(OUT - FIRST + 1, rows, ny)], [two_piece], "last_slope",
            part1, other1, part2, other2, dmat,
        )
    with jax.named_scope("slope_spread"):
        return place(FIRST - 1, spread(done2), (OUT, lx, ny), "place_slope", out1)


def solution(mesh):
    gx, gz = mesh.shape["gx"], mesh.shape["gz"]
    fine = Mesh(mesh.devices.reshape(gx, 2, gz // 4, 2), (GXA,) + ZA)
    return jax.shard_map(
        shards,
        mesh=fine,
        in_specs=(P(None, GXA, ZA, None), P()),
        out_specs=P(None, GXA, None),
        check_vma=False,
    )
```

time: 79.8 us -> 71.2 us (0.89); the launches traced: 78.7 us -> 71.1 us
  waiting for transfers between devices: 18.5 us -> 2.83 us
  starting transfers between devices: 31 us -> 43.6 us
  Pallas kernels: 29.1 us -> 24.5 us
    ppermute x14 -> x26, waiting for transfers between devices: 18.5 us -> 2.83 us  [send(): lax.ppermute(value, axis, [(i, (i + step) % size) for i in range(size)])]
    ppermute x14 -> x26, starting transfers between devices: 25.6 us -> 37.4 us  [send(): lax.ppermute(value, axis, [(i, (i + step) % size) for i in range(size)])]
    pallas_call x3 -> x1, Pallas kernels: 5.86 us -> 1.53 us  [cut(): pl.pallas_call(kernel, in_specs=[pl.BlockSpec(memory_space=pltpu.HBM)] +...]
    pallas_call x4 -> x6, Pallas kernels: 3.48 us -> 0.85 us  [small_call(): pl.pallas_call(kernel, in_specs=[vm] * len(args), out_specs=[vm] * len(ou...]
    pallas_call x3 -> x5, Pallas kernels: 19.8 us -> 22.1 us  [the longest x1 9.86 us: inner_moments(): pl.pallas_call(inner_kernel, in_specs=[vm] * 5 + [pl.BlockSpec(memory_spa...]
    ppermute x1, starting transfers between devices: 2.28 us -> 3.11 us  [shards(): xl = lax.ppermute(xl, GXA, up)]
  transfers between devices with their start and end apart: 16 -> 28, of which waited for: 7 -> 2; matrix products, arithmetic and copies ran while one was open for 0% -> 0% of each run, Pallas kernels for 29% -> 29%
where the time goes in v3:
time: 71.2 us; the launch traced here: 71.1 us
  starting transfers between devices  43.6 us (61%)
  Pallas kernels  24.5 us (34%)
  waiting for transfers between devices  2.83 us (4%)
    ppermute x26, starting transfers between devices, send(): lax.ppermute(value, axis, [(i, (i + step) % size) for i in range(size)])  37.4 us
    pallas_call x1, Pallas kernels, inner_moments(): pl.pallas_call(inner_kernel, in_specs=[vm] * 5 + [pl.BlockSpec(memory_spa...  9.86 us
    pallas_call x1, Pallas kernels, base_moments(): pl.pallas_call(base_kernel, in_specs=[pl.BlockSpec(memory_space=pltpu.HBM...  8.75 us
    ppermute x1, starting transfers between devices, shards(): xl = lax.ppermute(xl, GXA, up)  3.11 us
    ppermute x1, starting transfers between devices, shards(): xr = lax.ppermute(xr, GXA, down)  3.06 us
    ppermute x26, waiting for transfers between devices, send(): lax.ppermute(value, axis, [(i, (i + step) % size) for i in range(size)])  2.83 us
    pallas_call x2, Pallas kernels, place(): pl.pallas_call(functools.partial(place_kernel, first), in_specs=[pl.Block...  1.81 us
    pallas_call x1, Pallas kernels, edge_moments(): pl.pallas_call(edge_kernel, in_specs=[vm] * 7 + [pl.BlockSpec(memory_spac...  1.65 us
  transfers between devices with their start and end apart: 28, of which 2 were waited for; matrix products, arithmetic and copies ran while one was open for 0% of the time, Pallas kernels for 29%

profile of v3, /device:TPU:9, one launch (start us, length us, event | category | flops | bytes accessed | tf_op | source)
XLA Modules:
  0.0 71.1 jit_solution(10882159920045147964)
XLA Ops:
  0.0 1.5 %rims.1 = (f32[3,64,4,128]{3,2,1,0:T(4,128)S(1)}, f32[3,64,4,128]{3,2,1,0:T(4,128)S(1)}, f32[4,4,64,128]{3,2,1,0:T(8,128)S(1)}, f32[4,4,64,128]{3,2,1,0:T(8,128)S(1)}) custom-call(f32[4,64,64,128]{3,2,1,0:T(8,128)} %flow.3), custom_call_target="tpu_custom_call" | custom-call | tf_op jit(solution)/shard_map/rims/pallas_call | solution.py:101
  1.5 2.3 %collective-permute-start.5 = (f32[3,64,4,128]{3,2,1,0:T(4,128)S(1)}, f32[3,64,4,128]{3,2,1,0:T(4,128)S(1)}, u32[]{:S(2)}, u32[]{:S(2)}) collective-permute-start(f32[3,64,4,128]{3,2,1,0:T(4,128)S(1)} %get-tuple-element.40), channel_id=1, source_target_pairs={{0,1},{1,2},{2,3},{3,4},{4,5},{5,6},{6,7},{7,8},{8,9},{9,10},{10,1... | collective-permute-start | bytes 1179656 | tf_op jit(solution)/shard_map/rim_exchange/ppermute | solution.py:558
  3.8 0.0 collective-permute-start.6
  3.8 3.1 %collective-permute-start.7 = (f32[4,4,64,128]{3,2,1,0:T(8,128)S(1)}, f32[4,4,64,128]{3,2,1,0:T(8,128)S(1)}, u32[]{:S(2)}, u32[]{:S(2)}) collective-permute-start(f32[4,4,64,128]{3,2,1,0:T(8,128)S(1)} %get-tuple-element.46), channel_id=1, source_target_pairs={{0,16},{16,32},{32,48},{48,64},{64,80},{80,96},{96,112},{1,17},{17... | collective-permute-start | bytes 1572872 | tf_op jit(solution)/shard_map/rim_exchange/ppermute | solution.py:572
  6.9 3.1 %collective-permute-start.8 = (f32[4,4,64,128]{3,2,1,0:T(8,128)S(1)}, f32[4,4,64,128]{3,2,1,0:T(8,128)S(1)}, u32[]{:S(2)}, u32[]{:S(2)}) collective-permute-start(f32[4,4,64,128]{3,2,1,0:T(8,128)S(1)} %get-tuple-element.47), channel_id=1, source_target_pairs={{16,0},{32,16},{48,32},{64,48},{80,64},{96,80},{112,96},{17,1},{33... | collective-permute-start | bytes 1572872 | tf_op jit(solution)/shard_map/rim_exchange/ppermute | solution.py:573
  10.0 8.7 %base_moments.1 = (f32[4,72,80,128]{3,2,1,0:T(8,128)S(1)}, f32[4,64,64,128]{3,2,1,0:T(8,128)S(1)}, f32[4,64,128]{2,1,0:T(8,128)S(1)}, f32[23,32,128]{2,1,0:T(8,1...) custom-call(f32[4,64,64,128]{3,2,1,0:T(8,128)} %flow.3, f32[128,128]{1,0:T(8,128)S(1)} %copy-done), custom_call_target="tpu_custom_call" | custom-call | flops 1000 | bytes 1000 | tf_op jit(solution)/shard_map/base_moments/pallas_call | solution.py:205
  18.8 5.1 %collective-permute-start = (f32[23,32,128]{2,1,0:T(8,128)S(1)}, f32[23,32,128]{2,1,0:T(8,128)S(1)}, u32[]{:S(2)}, u32[]{:S(2)}) collective-permute-start(f32[23,32,128]{2,1,0:T(8,128)S(1)} %get-tuple-element.32), channel_id=1, source_target_pairs={{0,1},{1,0},{2,3},{3,2},{4,5},{5,4},{6,7},{7,6},{8,9},{9,8},{10,11... | collective-permute-start | bytes 1130504 | tf_op jit(solution)/shard_map/base_core/ppermute | solution.py:558
  23.9 1.3 %collective-permute-done.got.got1 = f32[23,32,128]{2,1,0:T(8,128)S(1)} collective-permute-done((f32[23,32,128]{2,1,0:T(8,128)S(1)}, f32[23,32,128]{2,1,0:T(8,128)S(1)}, u32[]{:S(2)}, u32[]{:S(2)}) %collective-permute-start) | collective-permute-done | bytes 376864 | tf_op jit(solution)/shard_map/base_core/ppermute | solution.py:558
  25.2 0.1 core_base.1
  25.3 0.1 collective-permute-start.1
  25.4 0.0 collective-permute-done.5.zl
  25.4 0.6 collective-permute-start.2
  26.1 2.1 %collective-permute-start.3 = (f32[23,8,128]{2,1,0:T(8,128)S(1)}, f32[23,8,128]{2,1,0:T(8,128)S(1)}, u32[]{:S(2)}, u32[]{:S(2)}) collective-permute-start(f32[23,8,128]{2,1,0:T(8,128)S(1)} %get-tuple-element.36), channel_id=1, source_target_pairs={{0,6},{2,0},{4,2},{6,4},{1,7},{3,1},{5,3},{7,5},{8,14},{10,8},{12,... | collective-permute-start | bytes 282632 | tf_op jit(solution)/shard_map/base_span/ppermute | solution.py:558
  28.1 9.9 %inner_moments.1 = (f32[4,72,80,128]{3,2,1,0:T(8,128)S(1)}, f32[21,32,128]{2,1,0:T(8,128)S(1)}, f32[21,32,128]{2,1,0:T(8,128)S(1)}) custom-call(f32[4,72,80,128]{3,2,1,0:T(8,128)S(1)} %get-tuple-element.38.pad_in, f32[4,64,64,128]{3,2,1,0:T(8,128)S(1)} %get-tuple-element.39.ysl, ...), custom_call_target="tpu_custom_call", output_to_operand_aliasing={{0}: (0, {})} | custom-call | flops 1500000000 | bytes 84000000 | tf_op jit(solution)/shard_map/inner_moments/pallas_call | solution.py:333
  38.0 0.0 collective-permute-done.1.one.refs_1_
  38.0 0.0 collective-permute-done.2.two.refs_2_
  38.0 0.1 span_base.1
  38.1 0.0 collective-permute-done.8.xr
  38.1 1.7 %edge_moments.1 = (f32[4,72,80,128]{3,2,1,0:T(8,128)S(1)}, f32[21,32,128]{2,1,0:T(8,128)S(1)}, f32[21,32,128]{2,1,0:T(8,128)S(1)}) custom-call(f32[4,72,80,128]{3,2,1,0:T(8,128)S(1)} %get-tuple-element.43.pad_in, f32[21,32,128]{2,1,0:T(8,128)S(1)} %get-tuple-element.44.keep_in, ...), custom_call_target="tpu_custom_call", output_to_operand_aliasing={{0}: (0, {}), {1}: (1, {}), {2}: (2, {})} | custom-call | flops 52428800 | bytes 1048576 | tf_op jit(solution)/shard_map/edge_moments/pallas_call | solution.py:403
  39.8 1.0 %collective-permute-start.9 = (f32[21,32,128]{2,1,0:T(8,128)S(1)}, f32[21,32,128]{2,1,0:T(8,128)S(1)}, u32[]{:S(2)}, u32[]{:S(2)}) collective-permute-start(f32[21,32,128]{2,1,0:T(8,128)S(1)} %get-tuple-element.49), channel_id=1, source_target_pairs={{0,1},{1,0},{2,3},{3,2},{4,5},{5,4},{6,7},{7,6},{8,9},{9,8},{10,11... | collective-permute-start | bytes 1032200 | tf_op jit(solution)/shard_map/slope_core/ppermute | solution.py:558
  40.8 2.1 %collective-permute-start.4 = (f32[23,8,128]{2,1,0:T(8,128)S(1)}, f32[23,8,128]{2,1,0:T(8,128)S(1)}, u32[]{:S(2)}, u32[]{:S(2)}) collective-permute-start(f32[23,8,128]{2,1,0:T(8,128)S(1)} %get-tuple-element.37.after.mine1.mine), channel_id=1, source_target_pairs={{0,8},{8,0},{1,9},{9,1},{2,10},{10,2},{3,11},{11,3},{4,12},{12,4},... | collective-permute-start | bytes 282632 | tf_op jit(solution)/shard_map/base_x/ppermute | solution.py:558
  42.9 0.0 collective-permute-done.9.got2
  42.9 0.2 core_slope.1
  43.1 0.6 collective-permute-start.10
  43.7 2.2 %collective-permute-start.11 = (f32[21,8,128]{2,1,0:T(8,128)S(1)}, f32[21,8,128]{2,1,0:T(8,128)S(1)}, u32[]{:S(2)}, u32[]{:S(2)}) collective-permute-start(f32[21,8,128]{2,1,0:T(8,128)S(1)} %get-tuple-element.53), channel_id=1, source_target_pairs={{0,4},{2,6},{4,0},{6,2},{1,5},{3,7},{5,1},{7,3},{8,12},{10,14},{12... | collective-permute-start | bytes 258056 | tf_op jit(solution)/shard_map/slope_span/ppermute | solution.py:558
  45.9 2.0 %collective-permute-start.12 = (f32[21,8,128]{2,1,0:T(8,128)S(1)}, f32[21,8,128]{2,1,0:T(8,128)S(1)}, u32[]{:S(2)}, u32[]{:S(2)}) collective-permute-start(f32[21,8,128]{2,1,0:T(8,128)S(1)} %get-tuple-element.54), channel_id=1, source_target_pairs={{0,6},{2,0},{4,2},{6,4},{1,7},{3,1},{5,3},{7,5},{8,14},{10,8},{12,... | collective-permute-start | bytes 258056 | tf_op jit(solution)/shard_map/slope_span/ppermute | solution.py:558
  47.9 0.1 collective-permute-start.23
  48.0 1.4 %collective-permute-start.22 = (f32[22,8,128]{2,1,0:T(8,128)S(1)}, f32[22,8,128]{2,1,0:T(8,128)S(1)}, u32[]{:S(2)}, u32[]{:S(2)}) collective-permute-start(f32[22,8,128]{2,1,0:T(8,128)S(1)} %last_base.1.refs_0_), channel_id=1, source_target_pairs={{0,4},{2,6},{4,0},{6,2},{1,5},{3,7},{5,1},{7,3},{8,12},{10,14},{12... | collective-permute-start | bytes 270344 | tf_op jit(solution)/shard_map/base_spread/ppermute | solution.py:558
  49.3 0.0 collective-permute-done.10.refs_5_
  49.3 1.4 %collective-permute-start.24 = (f32[22,8,128]{2,1,0:T(8,128)S(1)}, f32[22,8,128]{2,1,0:T(8,128)S(1)}, u32[]{:S(2)}, u32[]{:S(2)}) collective-permute-start(f32[22,8,128]{2,1,0:T(8,128)S(1)} %last_base.1.refs_0_), channel_id=1, source_target_pairs={{0,1},{1,0},{2,3},{3,2},{4,5},{5,4},{6,7},{7,6},{8,9},{9,8},{10,11... | collective-permute-start | bytes 270344 | tf_op jit(solution)/shard_map/base_spread/ppermute | solution.py:558
  50.7 0.8 %collective-permute-start.21 = (f32[22,8,128]{2,1,0:T(8,128)S(1)}, f32[22,8,128]{2,1,0:T(8,128)S(1)}, u32[]{:S(2)}, u32[]{:S(2)}) collective-permute-start(f32[22,8,128]{2,1,0:T(8,128)S(1)} %last_base.1.refs_0_), channel_id=1, source_target_pairs={{0,2},{2,4},{4,6},{6,0},{1,3},{3,5},{5,7},{7,1},{8,10},{10,12},{12... | collective-permute-start | bytes 270344 | tf_op jit(solution)/shard_map/base_spread/ppermute | solution.py:558
  51.5 0.0 collective-permute-done.12.refs_7_
  51.5 0.3 span_slope.1.mine2
  51.8 2.2 %collective-permute-start.13 = (f32[21,8,128]{2,1,0:T(8,128)S(1)}, f32[21,8,128]{2,1,0:T(8,128)S(1)}, u32[]{:S(2)}, u32[]{:S(2)}) collective-permute-start(f32[21,8,128]{2,1,0:T(8,128)S(1)} %span_slope.1.mine2), channel_id=1, source_target_pairs={{0,8},{8,0},{1,9},{9,1},{2,10},{10,2},{3,11},{11,3},{4,12},{12,4},... | collective-permute-start | bytes 258056 | tf_op jit(solution)/shard_map/slope_x/ppermute | solution.py:558
  54.0 1.2 %collective-permute-start.27 = (f32[22,8,128]{2,1,0:T(8,128)S(1)}, f32[22,8,128]{2,1,0:T(8,128)S(1)}, u32[]{:S(2)}, u32[]{:S(2)}) collective-permute-start(f32[22,8,128]{2,1,0:T(8,128)S(1)} %collective-permute-done.23.refs_3_), channel_id=1, source_target_pairs={{0,1},{1,0},{2,3},{3,2},{4,5},{5,4},{6,7},{7,6},{8,9},{9,8},{10,11... | collective-permute-start | bytes 270344 | tf_op jit(solution)/shard_map/base_spread/ppermute | solution.py:558
  55.2 0.1 collective-permute-start.26
  55.3 1.4 %collective-permute-done.13.other2 = f32[21,8,128]{2,1,0:T(8,128)S(1)} collective-permute-done((f32[21,8,128]{2,1,0:T(8,128)S(1)}, f32[21,8,128]{2,1,0:T(8,128)S(1)}, u32[]{:S(2)}, u32[]{:S(2)}) %collective-permute-start.13) | collective-permute-done | bytes 86048 | tf_op jit(solution)/shard_map/slope_x/ppermute | solution.py:558
  56.8 0.2 last_slope.1.refs_0_
  56.9 2.1 %collective-permute-start.16 = (f32[18,8,128]{2,1,0:T(8,128)S(1)}, f32[18,8,128]{2,1,0:T(8,128)S(1)}, u32[]{:S(2)}, u32[]{:S(2)}) collective-permute-start(f32[18,8,128]{2,1,0:T(8,128)S(1)} %last_slope.1.refs_0_), channel_id=1, source_target_pairs={{0,6},{2,0},{4,2},{6,4},{1,7},{3,1},{5,3},{7,5},{8,14},{10,8},{12,... | collective-permute-start | bytes 221192 | tf_op jit(solution)/shard_map/slope_spread/ppermute | solution.py:558
  59.0 1.3 %collective-permute-start.15 = (f32[18,8,128]{2,1,0:T(8,128)S(1)}, f32[18,8,128]{2,1,0:T(8,128)S(1)}, u32[]{:S(2)}, u32[]{:S(2)}) collective-permute-start(f32[18,8,128]{2,1,0:T(8,128)S(1)} %last_slope.1.refs_0_), channel_id=1, source_target_pairs={{0,4},{2,6},{4,0},{6,2},{1,5},{3,7},{5,1},{7,3},{8,12},{10,14},{12... | collective-permute-start | bytes 221192 | tf_op jit(solution)/shard_map/slope_spread/ppermute | solution.py:558
  60.3 0.8 %collective-permute-start.14 = (f32[18,8,128]{2,1,0:T(8,128)S(1)}, f32[18,8,128]{2,1,0:T(8,128)S(1)}, u32[]{:S(2)}, u32[]{:S(2)}) collective-permute-start(f32[18,8,128]{2,1,0:T(8,128)S(1)} %last_slope.1.refs_0_), channel_id=1, source_target_pairs={{0,2},{2,4},{4,6},{6,0},{1,3},{3,5},{5,7},{7,1},{8,10},{10,12},{12... | collective-permute-start | bytes 221192 | tf_op jit(solution)/shard_map/slope_spread/ppermute | solution.py:558
  61.1 2.7 %collective-permute-start.25 = (f32[22,8,128]{2,1,0:T(8,128)S(1)}, f32[22,8,128]{2,1,0:T(8,128)S(1)}, u32[]{:S(2)}, u32[]{:S(2)}) collective-permute-start(f32[22,8,128]{2,1,0:T(8,128)S(1)} %collective-permute-done.21.refs_1_), channel_id=1, source_target_pairs={{0,1},{1,0},{2,3},{3,2},{4,5},{5,4},{6,7},{7,6},{8,9},{9,8},{10,11... | collective-permute-start | bytes 270344 | tf_op jit(solution)/shard_map/base_spread/ppermute | solution.py:558
  63.8 0.1 collective-permute-start.17
  63.9 0.7 %collective-permute-start.20 = (f32[18,8,128]{2,1,0:T(8,128)S(1)}, f32[18,8,128]{2,1,0:T(8,128)S(1)}, u32[]{:S(2)}, u32[]{:S(2)}) collective-permute-start(f32[18,8,128]{2,1,0:T(8,128)S(1)} %collective-permute-done.16.refs_3_), channel_id=1, source_target_pairs={{0,1},{1,0},{2,3},{3,2},{4,5},{5,4},{6,7},{7,6},{8,9},{9,8},{10,11... | collective-permute-start | bytes 221192 | tf_op jit(solution)/shard_map/slope_spread/ppermute | solution.py:558
  64.6 4.0 %collective-permute-start.19 = (f32[18,8,128]{2,1,0:T(8,128)S(1)}, f32[18,8,128]{2,1,0:T(8,128)S(1)}, u32[]{:S(2)}, u32[]{:S(2)}) collective-permute-start(f32[18,8,128]{2,1,0:T(8,128)S(1)} %collective-permute-done.15.refs_2_), channel_id=1, source_target_pairs={{0,1},{1,0},{2,3},{3,2},{4,5},{5,4},{6,7},{7,6},{8,9},{9,8},{10,11... | collective-permute-start | bytes 221192 | tf_op jit(solution)/shard_map/slope_spread/ppermute | solution.py:558
  68.6 0.6 collective-permute-start.18
  69.2 0.9 %place_base.1.refs_8_ = f32[40,64,128]{2,1,0:T(8,128)} custom-call(f32[22,8,128]{2,1,0:T(8,128)S(1)} %last_base.1.refs_0_, f32[22,8,128]{2,1,0:T(8,128)S(1)} %collective-permute-done.21.refs_1_, f32[22,8,128]{2,1,0:T(8,128)S(1)} %collective-permute-done.22.refs_2_, f32[22,8,128]{2,1,0:T(8,128)S(1)} %collective-permute-done.23.refs_3_, ...), custom_call_target="tpu_custom_call" | custom-call | tf_op jit(solution)/shard_map/base_spread/place_base/pallas_call | solution.py:530
  70.2 0.9 %place_slope.1 = f32[40,64,128]{2,1,0:T(8,128)} custom-call(f32[18,8,128]{2,1,0:T(8,128)S(1)} %last_slope.1.refs_0_, f32[18,8,128]{2,1,0:T(8,128)S(1)} %collective-permute-done.14.refs_1_, f32[18,8,128]{2,1,0:T(8,128)S(1)} %collective-permute-done.15.refs_2_, f32[18,8,128]{2,1,0:T(8,128)S(1)} %collective-permute-done.16.refs_3_, ...), custom_call_target="tpu_custom_call", output_to_operand_aliasing={{}: (8, {})} | custom-call | tf_op jit(solution)/shard_map/slope_spread/place_slope/pallas_call | solution.py:530
  (22 shorter events, 0.1 us)
Async XLA Ops:
  0.0 10.0 %copy-start = (f32[128,128]{1,0:T(8,128)S(1)}, f32[128,128]{1,0:T(8,128)}, u32[]{:S(2)}) copy-start(f32[128,128]{1,0:T(8,128)} %dy.1) | copy-start | bytes 196612
  1.5 23.9 %collective-permute-start.5 = (f32[3,64,4,128]{3,2,1,0:T(4,128)S(1)}, f32[3,64,4,128]{3,2,1,0:T(4,128)S(1)}, u32[]{:S(2)}, u32[]{:S(2)}) collective-permute-start(f32[3,64,4,128]{3,2,1,0:T(4,128)S(1)} %get-tuple-element.40), channel_id=1, source_target_pairs={{0,1},{1,2},{2,3},{3,4},{4,5},{5,6},{6,7},{7,8},{8,9},{9,10},{10,1... | collective-permute-start | bytes 1179656 | tf_op jit(solution)/shard_map/rim_exchange/ppermute | solution.py:558
  3.8 22.3 %collective-permute-start.6 = (f32[3,64,4,128]{3,2,1,0:T(4,128)S(1)}, f32[3,64,4,128]{3,2,1,0:T(4,128)S(1)}, u32[]{:S(2)}, u32[]{:S(2)}) collective-permute-start(f32[3,64,4,128]{3,2,1,0:T(4,128)S(1)} %get-tuple-element.41), channel_id=1, source_target_pairs={{0,15},{1,0},{2,1},{3,2},{4,3},{5,4},{6,5},{7,6},{8,7},{9,8},{10,9... | collective-permute-start | bytes 1179656 | tf_op jit(solution)/shard_map/rim_exchange/ppermute | solution.py:558
  3.8 34.3 %collective-permute-start.7 = (f32[4,4,64,128]{3,2,1,0:T(8,128)S(1)}, f32[4,4,64,128]{3,2,1,0:T(8,128)S(1)}, u32[]{:S(2)}, u32[]{:S(2)}) collective-permute-start(f32[4,4,64,128]{3,2,1,0:T(8,128)S(1)} %get-tuple-element.46), channel_id=1, source_target_pairs={{0,16},{16,32},{32,48},{48,64},{64,80},{80,96},{96,112},{1,17},{17... | collective-permute-start | bytes 1572872 | tf_op jit(solution)/shard_map/rim_exchange/ppermute | solution.py:572
  6.9 31.2 %collective-permute-start.8 = (f32[4,4,64,128]{3,2,1,0:T(8,128)S(1)}, f32[4,4,64,128]{3,2,1,0:T(8,128)S(1)}, u32[]{:S(2)}, u32[]{:S(2)}) collective-permute-start(f32[4,4,64,128]{3,2,1,0:T(8,128)S(1)} %get-tuple-element.47), channel_id=1, source_target_pairs={{16,0},{32,16},{48,32},{64,48},{80,64},{96,80},{112,96},{17,1},{33... | collective-permute-start | bytes 1572872 | tf_op jit(solution)/shard_map/rim_exchange/ppermute | solution.py:573
  18.8 6.5 %collective-permute-start = (f32[23,32,128]{2,1,0:T(8,128)S(1)}, f32[23,32,128]{2,1,0:T(8,128)S(1)}, u32[]{:S(2)}, u32[]{:S(2)}) collective-permute-start(f32[23,32,128]{2,1,0:T(8,128)S(1)} %get-tuple-element.32), channel_id=1, source_target_pairs={{0,1},{1,0},{2,3},{3,2},{4,5},{5,4},{6,7},{7,6},{8,9},{9,8},{10,11... | collective-permute-start | bytes 1130504 | tf_op jit(solution)/shard_map/base_core/ppermute | solution.py:558
  25.3 12.7 %collective-permute-start.1 = (f32[23,8,128]{2,1,0:T(8,128)S(1)}, f32[23,8,128]{2,1,0:T(8,128)S(1)}, u32[]{:S(2)}, u32[]{:S(2)}) collective-permute-start(f32[23,8,128]{2,1,0:T(8,128)S(1)} %get-tuple-element.34), channel_id=1, source_target_pairs={{0,2},{2,4},{4,6},{6,0},{1,3},{3,5},{5,7},{7,1},{8,10},{10,12},{12... | collective-permute-start | bytes 282632 | tf_op jit(solution)/shard_map/base_span/ppermute | solution.py:558
  25.4 12.6 %collective-permute-start.2 = (f32[23,8,128]{2,1,0:T(8,128)S(1)}, f32[23,8,128]{2,1,0:T(8,128)S(1)}, u32[]{:S(2)}, u32[]{:S(2)}) collective-permute-start(f32[23,8,128]{2,1,0:T(8,128)S(1)} %get-tuple-element.35), channel_id=1, source_target_pairs={{0,4},{2,6},{4,0},{6,2},{1,5},{3,7},{5,1},{7,3},{8,12},{10,14},{12... | collective-permute-start | bytes 282632 | tf_op jit(solution)/shard_map/base_span/ppermute | solution.py:558
  26.1 12.0 %collective-permute-start.3 = (f32[23,8,128]{2,1,0:T(8,128)S(1)}, f32[23,8,128]{2,1,0:T(8,128)S(1)}, u32[]{:S(2)}, u32[]{:S(2)}) collective-permute-start(f32[23,8,128]{2,1,0:T(8,128)S(1)} %get-tuple-element.36), channel_id=1, source_target_pairs={{0,6},{2,0},{4,2},{6,4},{1,7},{3,1},{5,3},{7,5},{8,14},{10,8},{12,... | collective-permute-start | bytes 282632 | tf_op jit(solution)/shard_map/base_span/ppermute | solution.py:558
  39.8 3.1 %collective-permute-start.9 = (f32[21,32,128]{2,1,0:T(8,128)S(1)}, f32[21,32,128]{2,1,0:T(8,128)S(1)}, u32[]{:S(2)}, u32[]{:S(2)}) collective-permute-start(f32[21,32,128]{2,1,0:T(8,128)S(1)} %get-tuple-element.49), channel_id=1, source_target_pairs={{0,1},{1,0},{2,3},{3,2},{4,5},{5,4},{6,7},{7,6},{8,9},{9,8},{10,11... | collective-permute-start | bytes 1032200 | tf_op jit(solution)/shard_map/slope_core/ppermute | solution.py:558
  40.8 7.1 %collective-permute-start.4 = (f32[23,8,128]{2,1,0:T(8,128)S(1)}, f32[23,8,128]{2,1,0:T(8,128)S(1)}, u32[]{:S(2)}, u32[]{:S(2)}) collective-permute-start(f32[23,8,128]{2,1,0:T(8,128)S(1)} %get-tuple-element.37.after.mine1.mine), channel_id=1, source_target_pairs={{0,8},{8,0},{1,9},{9,1},{2,10},{10,2},{3,11},{11,3},{4,12},{12,4},... | collective-permute-start | bytes 282632 | tf_op jit(solution)/shard_map/base_x/ppermute | solution.py:558
  43.1 6.2 %collective-permute-start.10 = (f32[21,8,128]{2,1,0:T(8,128)S(1)}, f32[21,8,128]{2,1,0:T(8,128)S(1)}, u32[]{:S(2)}, u32[]{:S(2)}) collective-permute-start(f32[21,8,128]{2,1,0:T(8,128)S(1)} %get-tuple-element.52), channel_id=1, source_target_pairs={{0,2},{2,4},{4,6},{6,0},{1,3},{3,5},{5,7},{7,1},{8,10},{10,12},{12... | collective-permute-start | bytes 258056 | tf_op jit(solution)/shard_map/slope_span/ppermute | solution.py:558
  43.7 7.0 %collective-permute-start.11 = (f32[21,8,128]{2,1,0:T(8,128)S(1)}, f32[21,8,128]{2,1,0:T(8,128)S(1)}, u32[]{:S(2)}, u32[]{:S(2)}) collective-permute-start(f32[21,8,128]{2,1,0:T(8,128)S(1)} %get-tuple-element.53), channel_id=1, source_target_pairs={{0,4},{2,6},{4,0},{6,2},{1,5},{3,7},{5,1},{7,3},{8,12},{10,14},{12... | collective-permute-start | bytes 258056 | tf_op jit(solution)/shard_map/slope_span/ppermute | solution.py:558
  45.9 5.7 %collective-permute-start.12 = (f32[21,8,128]{2,1,0:T(8,128)S(1)}, f32[21,8,128]{2,1,0:T(8,128)S(1)}, u32[]{:S(2)}, u32[]{:S(2)}) collective-permute-start(f32[21,8,128]{2,1,0:T(8,128)S(1)} %get-tuple-element.54), channel_id=1, source_target_pairs={{0,6},{2,0},{4,2},{6,4},{1,7},{3,1},{5,3},{7,5},{8,14},{10,8},{12,... | collective-permute-start | bytes 258056 | tf_op jit(solution)/shard_map/slope_span/ppermute | solution.py:558
  47.9 6.1 %collective-permute-start.23 = (f32[22,8,128]{2,1,0:T(8,128)S(1)}, f32[22,8,128]{2,1,0:T(8,128)S(1)}, u32[]{:S(2)}, u32[]{:S(2)}) collective-permute-start(f32[22,8,128]{2,1,0:T(8,128)S(1)} %last_base.1.refs_0_), channel_id=1, source_target_pairs={{0,6},{2,0},{4,2},{6,4},{1,7},{3,1},{5,3},{7,5},{8,14},{10,8},{12,... | collective-permute-start | bytes 270344 | tf_op jit(solution)/shard_map/base_spread/ppermute | solution.py:558
  48.0 7.3 %collective-permute-start.22 = (f32[22,8,128]{2,1,0:T(8,128)S(1)}, f32[22,8,128]{2,1,0:T(8,128)S(1)}, u32[]{:S(2)}, u32[]{:S(2)}) collective-permute-start(f32[22,8,128]{2,1,0:T(8,128)S(1)} %last_base.1.refs_0_), channel_id=1, source_target_pairs={{0,4},{2,6},{4,0},{6,2},{1,5},{3,7},{5,1},{7,3},{8,12},{10,14},{12... | collective-permute-start | bytes 270344 | tf_op jit(solution)/shard_map/base_spread/ppermute | solution.py:558
  49.3 9.7 %collective-permute-start.24 = (f32[22,8,128]{2,1,0:T(8,128)S(1)}, f32[22,8,128]{2,1,0:T(8,128)S(1)}, u32[]{:S(2)}, u32[]{:S(2)}) collective-permute-start(f32[22,8,128]{2,1,0:T(8,128)S(1)} %last_base.1.refs_0_), channel_id=1, source_target_pairs={{0,1},{1,0},{2,3},{3,2},{4,5},{5,4},{6,7},{7,6},{8,9},{9,8},{10,11... | collective-permute-start | bytes 270344 | tf_op jit(solution)/shard_map/base_spread/ppermute | solution.py:558
  50.7 9.6 %collective-permute-start.21 = (f32[22,8,128]{2,1,0:T(8,128)S(1)}, f32[22,8,128]{2,1,0:T(8,128)S(1)}, u32[]{:S(2)}, u32[]{:S(2)}) collective-permute-start(f32[22,8,128]{2,1,0:T(8,128)S(1)} %last_base.1.refs_0_), channel_id=1, source_target_pairs={{0,2},{2,4},{4,6},{6,0},{1,3},{3,5},{5,7},{7,1},{8,10},{10,12},{12... | collective-permute-start | bytes 270344 | tf_op jit(solution)/shard_map/base_spread/ppermute | solution.py:558
  51.8 4.9 %collective-permute-start.13 = (f32[21,8,128]{2,1,0:T(8,128)S(1)}, f32[21,8,128]{2,1,0:T(8,128)S(1)}, u32[]{:S(2)}, u32[]{:S(2)}) collective-permute-start(f32[21,8,128]{2,1,0:T(8,128)S(1)} %span_slope.1.mine2), channel_id=1, source_target_pairs={{0,8},{8,0},{1,9},{9,1},{2,10},{10,2},{3,11},{11,3},{4,12},{12,4},... | collective-permute-start | bytes 258056 | tf_op jit(solution)/shard_map/slope_x/ppermute | solution.py:558
  54.0 7.1 %collective-permute-start.27 = (f32[22,8,128]{2,1,0:T(8,128)S(1)}, f32[22,8,128]{2,1,0:T(8,128)S(1)}, u32[]{:S(2)}, u32[]{:S(2)}) collective-permute-start(f32[22,8,128]{2,1,0:T(8,128)S(1)} %collective-permute-done.23.refs_3_), channel_id=1, source_target_pairs={{0,1},{1,0},{2,3},{3,2},{4,5},{5,4},{6,7},{7,6},{8,9},{9,8},{10,11... | collective-permute-start | bytes 270344 | tf_op jit(solution)/shard_map/base_spread/ppermute | solution.py:558
  55.2 8.6 %collective-permute-start.26 = (f32[22,8,128]{2,1,0:T(8,128)S(1)}, f32[22,8,128]{2,1,0:T(8,128)S(1)}, u32[]{:S(2)}, u32[]{:S(2)}) collective-permute-start(f32[22,8,128]{2,1,0:T(8,128)S(1)} %collective-permute-done.22.refs_2_), channel_id=1, source_target_pairs={{0,1},{1,0},{2,3},{3,2},{4,5},{5,4},{6,7},{7,6},{8,9},{9,8},{10,11... | collective-permute-start | bytes 270344 | tf_op jit(solution)/shard_map/base_spread/ppermute | solution.py:558
  56.9 6.9 %collective-permute-start.16 = (f32[18,8,128]{2,1,0:T(8,128)S(1)}, f32[18,8,128]{2,1,0:T(8,128)S(1)}, u32[]{:S(2)}, u32[]{:S(2)}) collective-permute-start(f32[18,8,128]{2,1,0:T(8,128)S(1)} %last_slope.1.refs_0_), channel_id=1, source_target_pairs={{0,6},{2,0},{4,2},{6,4},{1,7},{3,1},{5,3},{7,5},{8,14},{10,8},{12,... | collective-permute-start | bytes 221192 | tf_op jit(solution)/shard_map/slope_spread/ppermute | solution.py:558
  59.0 5.6 %collective-permute-start.15 = (f32[18,8,128]{2,1,0:T(8,128)S(1)}, f32[18,8,128]{2,1,0:T(8,128)S(1)}, u32[]{:S(2)}, u32[]{:S(2)}) collective-permute-start(f32[18,8,128]{2,1,0:T(8,128)S(1)} %last_slope.1.refs_0_), channel_id=1, source_target_pairs={{0,4},{2,6},{4,0},{6,2},{1,5},{3,7},{5,1},{7,3},{8,12},{10,14},{12... | collective-permute-start | bytes 221192 | tf_op jit(solution)/shard_map/slope_spread/ppermute | solution.py:558
  60.3 8.3 %collective-permute-start.14 = (f32[18,8,128]{2,1,0:T(8,128)S(1)}, f32[18,8,128]{2,1,0:T(8,128)S(1)}, u32[]{:S(2)}, u32[]{:S(2)}) collective-permute-start(f32[18,8,128]{2,1,0:T(8,128)S(1)} %last_slope.1.refs_0_), channel_id=1, source_target_pairs={{0,2},{2,4},{4,6},{6,0},{1,3},{3,5},{5,7},{7,1},{8,10},{10,12},{12... | collective-permute-start | bytes 221192 | tf_op jit(solution)/shard_map/slope_spread/ppermute | solution.py:558
  61.1 8.1 %collective-permute-start.25 = (f32[22,8,128]{2,1,0:T(8,128)S(1)}, f32[22,8,128]{2,1,0:T(8,128)S(1)}, u32[]{:S(2)}, u32[]{:S(2)}) collective-permute-start(f32[22,8,128]{2,1,0:T(8,128)S(1)} %collective-permute-done.21.refs_1_), channel_id=1, source_target_pairs={{0,1},{1,0},{2,3},{3,2},{4,5},{5,4},{6,7},{7,6},{8,9},{9,8},{10,11... | collective-permute-start | bytes 270344 | tf_op jit(solution)/shard_map/base_spread/ppermute | solution.py:558
  63.8 6.3 %collective-permute-start.17 = (f32[18,8,128]{2,1,0:T(8,128)S(1)}, f32[18,8,128]{2,1,0:T(8,128)S(1)}, u32[]{:S(2)}, u32[]{:S(2)}) collective-permute-start(f32[18,8,128]{2,1,0:T(8,128)S(1)} %last_slope.1.refs_0_), channel_id=1, source_target_pairs={{0,1},{1,0},{2,3},{3,2},{4,5},{5,4},{6,7},{7,6},{8,9},{9,8},{10,11... | collective-permute-start | bytes 221192 | tf_op jit(solution)/shard_map/slope_spread/ppermute | solution.py:558
  63.9 6.3 %collective-permute-start.20 = (f32[18,8,128]{2,1,0:T(8,128)S(1)}, f32[18,8,128]{2,1,0:T(8,128)S(1)}, u32[]{:S(2)}, u32[]{:S(2)}) collective-permute-start(f32[18,8,128]{2,1,0:T(8,128)S(1)} %collective-permute-done.16.refs_3_), channel_id=1, source_target_pairs={{0,1},{1,0},{2,3},{3,2},{4,5},{5,4},{6,7},{7,6},{8,9},{9,8},{10,11... | collective-permute-start | bytes 221192 | tf_op jit(solution)/shard_map/slope_spread/ppermute | solution.py:558
  64.6 5.5 %collective-permute-start.19 = (f32[18,8,128]{2,1,0:T(8,128)S(1)}, f32[18,8,128]{2,1,0:T(8,128)S(1)}, u32[]{:S(2)}, u32[]{:S(2)}) collective-permute-start(f32[18,8,128]{2,1,0:T(8,128)S(1)} %collective-permute-done.15.refs_2_), channel_id=1, source_target_pairs={{0,1},{1,0},{2,3},{3,2},{4,5},{5,4},{6,7},{7,6},{8,9},{9,8},{10,11... | collective-permute-start | bytes 221192 | tf_op jit(solution)/shard_map/slope_spread/ppermute | solution.py:558
  68.6 1.6 %collective-permute-start.18 = (f32[18,8,128]{2,1,0:T(8,128)S(1)}, f32[18,8,128]{2,1,0:T(8,128)S(1)}, u32[]{:S(2)}, u32[]{:S(2)}) collective-permute-start(f32[18,8,128]{2,1,0:T(8,128)S(1)} %collective-permute-done.14.refs_1_), channel_id=1, source_target_pairs={{0,1},{1,0},{2,3},{3,2},{4,5},{5,4},{6,7},{7,6},{8,9},{9,8},{10,11... | collective-permute-start | bytes 221192 | tf_op jit(solution)/shard_map/slope_spread/ppermute | solution.py:558

commit v4 on v3

--- a/solution.py
+++ b/solution.py
@@ -110,8 +110,9 @@
     )(flow, *after)
 
 
-def base_kernel(flow, dy, pad, ysl, mean, keep, send, dmat, acc, weights, sems):
-    _, lx, lz, ny = ysl.shape
+def base_kernel(flow, pad, mean, keep, send, raw, acc, sems):
+    _, lx, ny = mean.shape
+    lz = pad.shape[2] - 16
     half = lx // 2
     core = lax.axis_index(CA)
     step = 8
@@ -120,13 +121,56 @@
     def fetch(k):
         return pltpu.make_async_copy(
             flow.at[:, pl.ds(step * k, step)],
-            pad.at[:, pl.ds(step * k + 4, step), pl.ds(8, lz)],
+            raw.at[:, pl.ds(step * k, step)],
             sems.at[k],
         )
 
     for k in range(parts):
         fetch(k).start()
 
+    def one(x, _):
+        centre = []
+        for c in range(4):
+            m = jnp.sum(raw[c, x], axis=0, keepdims=True) * (1.0 / lz)
+            mean[c, pl.ds(x, 1), :] = m
+            centre.append(m)
+        total = [None] * NBASE
+
+        def add(n, v):
+            total[n] = v if total[n] is None else total[n] + v
+
+        for b in range(lz // 8):
+            f = [raw[c, x, pl.ds(8 * b, 8), :] - centre[c] for c in range(4)]
+            for c in range(4):
+                pad[c, x + 4, pl.ds(8 + 8 * b, 8), :] = f[c]
+            prod = {}
+            for n, (i, j) in enumerate(pairs):
+                prod[i, j] = f[i] * f[j]
+                add(n, prod[i, j])
+            for n, (i, j, l) in enumerate(triples):
+                add(6 + n, prod[i, j] * f[l])
+            for c in range(3):
+                add(16 + c, f[3] * f[c])
+        for n in range(NBASE):
+            acc[pl.ds(pl.multiple_of(n * 8 * lx + 8 * x, 8), 8), :] = total[n]
+        return 0
+
+    def part(k, _):
+        fetch(k).wait()
+        return lax.fori_loop(0, step, lambda r, _: one(step * k + r, _), 0, unroll=2)
+
+    lax.fori_loop(0, parts, part, 0)
+    for out, side in ((send, 1 - core), (keep, core)):
+        at = pl.multiple_of(half * side, 8)
+        for c in range(4):
+            out[MEAN + c] = mean[c, pl.ds(at, half), :]
+        for k in range(NBASE):
+            out[UU + k] = half_sum(k, acc, lx, at)
+
+
+def y_kernel(pad, dy, ysl, dmat, weights):
+    _, lx, lz, ny = ysl.shape
+    step = 8
     d = dy[...].T * (1.0 / lead)
     dmat[...] = d
     dhi = d.astype(BF16)
@@ -137,39 +181,14 @@
     weights[pl.ds(ny, ny), pl.ds(ny, ny)] = jnp.zeros_like(dlo)
 
     def part(k, _):
-        fetch(k).wait()
         left = []
         for r in range(step):
-            x = step * k + r
             for c in range(4):
-                f = pad[c, x + 4, pl.ds(8, lz), :]
-                m = jnp.sum(f, axis=0, keepdims=True) * (1.0 / lz)
-                mean[c, pl.ds(x, 1), :] = m
-                a = f - m
-                pad[c, x + 4, pl.ds(8, lz), :] = a
+                a = pad[c, step * k + r + 4, pl.ds(8, lz), :]
                 hi = a.astype(BF16)
                 lo = (a - hi.astype(F32)).astype(BF16)
                 left.append(jnp.concatenate([hi, lo], axis=1))
         y = jnp.dot(jnp.concatenate(left, axis=0), weights[...], preferred_element_type=F32)
-        for r in range(step):
-            x = step * k + r
-            total = [None] * NBASE
-
-            def add(n, v):
-                total[n] = v if total[n] is None else total[n] + v
-
-            for b in range(lz // 8):
-                f = [pad[c, x + 4, pl.ds(8 + 8 * b, 8), :] for c in range(4)]
-                prod = {}
-                for n, (i, j) in enumerate(pairs):
-                    prod[i, j] = f[i] * f[j]
-                    add(n, prod[i, j])
-                for n, (i, j, l) in enumerate(triples):
-                    add(6 + n, prod[i, j] * f[l])
-                for c in range(3):
-                    add(16 + c, f[3] * f[c])
-            for n in range(NBASE):
-                acc[pl.ds(pl.multiple_of(n * 8 * lx + 8 * x, 8), 8), :] = total[n]
         y = y[:, :ny] + y[:, ny:]
         for r in range(step):
             for c in range(4):
@@ -177,13 +196,7 @@
                 ysl[c, step * k + r] = y[at : at + lz]
         return 0
 
-    lax.fori_loop(0, parts, part, 0)
-    for out, side in ((send, 1 - core), (keep, core)):
-        at = pl.multiple_of(half * side, 8)
-        for c in range(4):
-            out[MEAN + c] = mean[c, pl.ds(at, half), :]
-        for k in range(NBASE):
-            out[UU + k] = half_sum(k, acc, lx, at)
+    lax.fori_loop(0, lx // step, part, 0)
 
 
 def row_sum(k, rows, acc):
@@ -195,27 +208,41 @@
     return sum(acc[pl.ds(where + s, rows // 2, stride=8), :] for s in range(8))
 
 
-def base_moments(flow, dy):
+def base_moments(flow):
     _, lx, lz, ny = flow.shape
     vm = pl.BlockSpec(memory_space=pltpu.VMEM)
     half = (FIRST, lx // 2, ny)
-    shapes = [
-        (4, lx + 8, lz + 16, ny), (4, lx, lz, ny), (4, lx, ny), half, half, (ny, ny),
-    ]
+    shapes = [(4, lx + 8, lz + 16, ny), (4, lx, ny), half, half]
     return pl.pallas_call(
         base_kernel,
-        in_specs=[pl.BlockSpec(memory_space=pltpu.HBM), vm],
-        out_specs=[vm] * 6,
+        in_specs=[pl.BlockSpec(memory_space=pltpu.HBM)],
+        out_specs=[vm] * 4,
         out_shape=[pltpu.VMEM(s, F32) for s in shapes],
         scratch_shapes=[
+            pltpu.VMEM((4, lx, lz, ny), F32),
             pltpu.VMEM((NBASE * 8 * lx, ny), F32),
-            pltpu.VMEM((2 * ny, 2 * ny), BF16),
             pltpu.SemaphoreType.DMA((lx // 8,)),
         ],
         compiler_params=pltpu.CompilerParams(vmem_limit_bytes=16 * 2**20),
         cost_estimate=pl.CostEstimate(flops=1000, bytes_accessed=1000, transcendentals=0),
         name="base_moments",
-    )(pltpu.with_memory_space_constraint(flow, pltpu.HBM), dy)
+    )(pltpu.with_memory_space_constraint(flow, pltpu.HBM))
+
+
+def y_slopes(pad, dy):
+    ny = dy.shape[0]
+    lx, lz = pad.shape[1] - 8, pad.shape[2] - 16
+    vm = pl.BlockSpec(memory_space=pltpu.VMEM)
+    return pl.pallas_call(
+        y_kernel,
+        in_specs=[vm, vm],
+        out_specs=[vm, vm],
+        out_shape=[pltpu.VMEM((4, lx, lz, ny), F32), pltpu.VMEM((ny, ny), F32)],
+        scratch_shapes=[pltpu.VMEM((2 * ny, 2 * ny), BF16)],
+        compiler_params=pltpu.CompilerParams(vmem_limit_bytes=16 * 2**20),
+        cost_estimate=pl.CostEstimate(flops=1000, bytes_accessed=1000, transcendentals=0),
+        name="y_slopes",
+    )(pad, dy)
 
 
 def difference(upper, lower):
@@ -314,7 +341,7 @@
             acc[pl.ds(pl.multiple_of(k * 8 * lx + 8 * x, 8), 8), :] = total[k]
         return 0
 
-    lax.fori_loop(4, lx - 4, one, 0)
+    lax.fori_loop(4, lx - 4, one, 0, unroll=4)
 
     for out, side in ((send, 1 - core), (keep, core)):
         at = pl.multiple_of(half * side, 8)
@@ -483,7 +510,7 @@
     )
 
 
-def last_base_kernel(count, mine, other, out, state):
+def last_base_kernel(count, mine, other, after, out, state):
     combine_base(picker(mine), picker(other), count, storer(state))
     scale = 1.0 / (2 * count)
     for c in range(3):
@@ -505,17 +532,33 @@
     out[17] = state[PG - FIRST + 5] * (scale * lead)
 
 
-def place_kernel(first, *refs):
-    ins, out, sems = refs[:8], refs[-2], refs[-1]
-    fields, rows = ins[0].shape[:2]
+def gather_kernel(after, *refs):
+    ins, out = refs[:-1], refs[-1]
+    rows = ins[0].shape[1]
+    zi = lax.axis_index("z")
+    zn = lax.axis_size("z")
+    for step, ref in enumerate(ins):
+        at = pl.multiple_of(rows * lax.rem(zi + zn - step, zn), 8)
+        out[:, pl.ds(at, rows), :] = ref[...]
+
+
+def place_kernel(*refs):
+    ins, out, sems = refs[:-2], refs[-2], refs[-1]
     zi = lax.axis_index("z")
     zn = lax.axis_size("z")
     core = lax.axis_index(CA)
     copies = []
     for k, ref in enumerate(ins):
-        side, step = divmod(k, zn)
-        c = core if side == 0 else 1 - core
-        at = pl.multiple_of(rows * (zn * c + lax.rem(zi + zn - step, zn)), 8)
+        fields, rows = ref.shape[:2]
+        if k < 2:
+            first, side, step = 0, k, None
+            at = rows * (core if side == 0 else 1 - core)
+        else:
+            first = OUT - fields
+            side, step = divmod(k - 2, zn)
+            c = core if side == 0 else 1 - core
+            at = rows * (zn * c + lax.rem(zi + zn - step, zn))
+        at = pl.multiple_of(at, 8)
         copies.append(
             pltpu.make_async_copy(
                 ref, out.at[pl.ds(first, fields), pl.ds(at, rows)], sems.at[k]
@@ -524,19 +567,16 @@
     copy_all(copies)
 
 
-def place(first, pieces, shape, name, base=None):
-    hbm = pl.BlockSpec(memory_space=pltpu.HBM)
-    extra = [] if base is None else [base]
+def place(pieces, shape):
     return pl.pallas_call(
-        functools.partial(place_kernel, first),
-        in_specs=[pl.BlockSpec(memory_space=pltpu.VMEM)] * len(pieces) + [hbm] * len(extra),
-        out_specs=hbm,
+        place_kernel,
+        in_specs=[pl.BlockSpec(memory_space=pltpu.VMEM)] * len(pieces),
+        out_specs=pl.BlockSpec(memory_space=pltpu.HBM),
         out_shape=pltpu.HBM(shape, F32),
-        input_output_aliases={} if base is None else {len(pieces): 0},
         scratch_shapes=[pltpu.SemaphoreType.DMA((len(pieces),))],
         compiler_params=pltpu.CompilerParams(vmem_limit_bytes=4 * 2**20),
-        name=name,
-    )(*pieces, *extra)
+        name="place",
+    )(*pieces)
 
 
 def small_call(kernel, outs, scratch, name, *args):
@@ -571,7 +611,8 @@
         zr = send(zr, ZA, -1)
         xl = lax.ppermute(xl, GXA, up)
         xr = lax.ppermute(xr, GXA, down)
-    pad, ysl, mean, keep1, give1, dmat = base_moments(flow, dy)
+    pad, mean, keep1, give1 = base_moments(flow)
+    ysl, dmat = y_slopes(pad, dy)
     rows = lx // 2 // zn
     one_piece, two_piece = (FIRST, rows, ny), (STATE - FIRST, rows, ny)
 
@@ -579,8 +620,7 @@
         return [own, send(up, "z", 1), send(far, "z", 2), send(down, "z", -1)]
 
     def spread(done):
-        mine = [done] + [send(done, "z", k) for k in (1, 2, 3)]
-        return mine + [send(v, CA, 1) for v in mine]
+        return [done] + [send(done, "z", k) for k in (1, 2, 3)]
 
     with jax.named_scope("base_core"):
         got1 = send(give1, CA, 1)
@@ -596,12 +636,6 @@
         )
     with jax.named_scope("base_x"):
         other1 = send(part1, "xh", 1)
-        (done1,) = small_call(
-            functools.partial(last_base_kernel, 2 * zn * lz),
-            [(FIRST - 1, rows, ny)], [one_piece], "last_base", part1, other1,
-        )
-    with jax.named_scope("base_spread"):
-        out1 = place(0, spread(done1), (OUT, lx, ny), "place_base")
     keep2, give2 = edge_moments(pad, keep2, give2, ysl, xl, xr, mean, part1)
     with jax.named_scope("slope_core"):
         got2 = send(give2, CA, 1)
@@ -609,6 +643,13 @@
             functools.partial(core_slope_kernel, lz), [two_piece] * 4, [], "core_slope",
             keep1, got1, keep2, got2, dmat,
         )
+    with jax.named_scope("base_x"):
+        (done1,) = small_call(
+            functools.partial(last_base_kernel, 2 * zn * lz),
+            [(FIRST - 1, rows, ny)], [one_piece], "last_base", part1, other1, parts2[0],
+        )
+    with jax.named_scope("base_spread"):
+        spread1 = spread(done1)
     with jax.named_scope("slope_span"):
         pieces2 = along_z(*parts2)
         (part2,) = small_call(
@@ -622,8 +663,15 @@
             [(OUT - FIRST + 1, rows, ny)], [two_piece], "last_slope",
             part1, other1, part2, other2, dmat,
         )
+    with jax.named_scope("base_spread"):
+        (half1,) = small_call(
+            gather_kernel, [(FIRST - 1, lx // 2, ny)], [], "gather", done2, *spread1
+        )
+        all1 = [half1, send(half1, CA, 1)]
     with jax.named_scope("slope_spread"):
-        return place(FIRST - 1, spread(done2), (OUT, lx, ny), "place_slope", out1)
+        all2 = spread(done2)
+        all2 = all2 + [send(v, CA, 1) for v in all2]
+    return place(all1 + all2, (OUT, lx, ny))
 
 
 def solution(mesh):

time: 71.2 us -> 68.9 us (0.968)
  starting transfers between devices: 43.6 us -> 39.9 us
  waiting for transfers between devices: 2.83 us -> 4.25 us
    ppermute x26 -> x23, starting transfers between devices: 37.4 us -> 33.7 us  [send(): lax.ppermute(value, axis, [(i, (i + step) % size) for i in range(size)])]
    pallas_call x2, Pallas kernels: 1.81 us -> 4.8 us  [the longest x1 3.68 us: y_slopes(): pl.pallas_call(y_kernel, in_specs=[vm, vm], out_specs=[vm, vm], out_shape...]
    pallas_call x1, Pallas kernels: 8.75 us -> 5.88 us  [base_moments(): pl.pallas_call(base_kernel, in_specs=[pl.BlockSpec(memory_space=pltpu.HBM...]
    ppermute x26 -> x23, waiting for transfers between devices: 2.83 us -> 4.25 us  [send(): lax.ppermute(value, axis, [(i, (i + step) % size) for i in range(size)])]
  transfers between devices with their start and end apart: 28 -> 25, of which waited for: 2 -> 4; matrix products, arithmetic and copies ran while one was open for 0% -> 0% of each run, Pallas kernels for 29% -> 29%
where the time goes in v4:
time: 68.9 us; the launch traced here: 68.6 us
  starting transfers between devices  39.9 us (58%)
  Pallas kernels  24.2 us (35%)
  waiting for transfers between devices  4.25 us (6%)
    ppermute x23, starting transfers between devices, send(): lax.ppermute(value, axis, [(i, (i + step) % size) for i in range(size)])  33.7 us
    pallas_call x1, Pallas kernels, inner_moments(): pl.pallas_call(inner_kernel, in_specs=[vm] * 5 + [pl.BlockSpec(memory_spa...  9.44 us
    pallas_call x1, Pallas kernels, base_moments(): pl.pallas_call(base_kernel, in_specs=[pl.BlockSpec(memory_space=pltpu.HBM...  5.88 us
    ppermute x23, waiting for transfers between devices, send(): lax.ppermute(value, axis, [(i, (i + step) % size) for i in range(size)])  4.25 us
    pallas_call x1, Pallas kernels, y_slopes(): pl.pallas_call(y_kernel, in_specs=[vm, vm], out_specs=[vm, vm], out_shape...  3.68 us
    ppermute x1, starting transfers between devices, shards(): xl = lax.ppermute(xl, GXA, up)  3.11 us
    ppermute x1, starting transfers between devices, shards(): xr = lax.ppermute(xr, GXA, down)  3.06 us
    pallas_call x1, Pallas kernels, edge_moments(): pl.pallas_call(edge_kernel, in_specs=[vm] * 7 + [pl.BlockSpec(memory_spac...  1.66 us
  transfers between devices with their start and end apart: 25, of which 4 were waited for; matrix products, arithmetic and copies ran while one was open for 0% of the time, Pallas kernels for 29%

profile of v4, /device:TPU:9, one launch (start us, length us, event | category | flops | bytes accessed | tf_op | source)
XLA Modules:
  0.0 68.6 jit_solution(15505922506425508465)
XLA Ops:
  0.0 1.5 %rims.1 = (f32[3,64,4,128]{3,2,1,0:T(4,128)S(1)}, f32[3,64,4,128]{3,2,1,0:T(4,128)S(1)}, f32[4,4,64,128]{3,2,1,0:T(8,128)S(1)}, f32[4,4,64,128]{3,2,1,0:T(8,128)S(1)}) custom-call(f32[4,64,64,128]{3,2,1,0:T(8,128)} %flow.3), custom_call_target="tpu_custom_call" | custom-call | tf_op jit(solution)/shard_map/rims/pallas_call | solution.py:101
  1.5 2.3 %collective-permute-start.5 = (f32[3,64,4,128]{3,2,1,0:T(4,128)S(1)}, f32[3,64,4,128]{3,2,1,0:T(4,128)S(1)}, u32[]{:S(2)}, u32[]{:S(2)}) collective-permute-start(f32[3,64,4,128]{3,2,1,0:T(4,128)S(1)} %get-tuple-element.40), channel_id=1, source_target_pairs={{0,1},{1,2},{2,3},{3,4},{4,5},{5,6},{6,7},{7,8},{8,9},{9,10},{10,1... | collective-permute-start | bytes 1179656 | tf_op jit(solution)/shard_map/rim_exchange/ppermute | solution.py:598
  3.8 3.1 %collective-permute-start.7 = (f32[4,4,64,128]{3,2,1,0:T(8,128)S(1)}, f32[4,4,64,128]{3,2,1,0:T(8,128)S(1)}, u32[]{:S(2)}, u32[]{:S(2)}) collective-permute-start(f32[4,4,64,128]{3,2,1,0:T(8,128)S(1)} %get-tuple-element.46), channel_id=1, source_target_pairs={{0,16},{16,32},{32,48},{48,64},{64,80},{80,96},{96,112},{1,17},{17... | collective-permute-start | bytes 1572872 | tf_op jit(solution)/shard_map/rim_exchange/ppermute | solution.py:612
  6.9 3.1 %collective-permute-start.8 = (f32[4,4,64,128]{3,2,1,0:T(8,128)S(1)}, f32[4,4,64,128]{3,2,1,0:T(8,128)S(1)}, u32[]{:S(2)}, u32[]{:S(2)}) collective-permute-start(f32[4,4,64,128]{3,2,1,0:T(8,128)S(1)} %get-tuple-element.47), channel_id=1, source_target_pairs={{16,0},{32,16},{48,32},{64,48},{80,64},{96,80},{112,96},{17,1},{33... | collective-permute-start | bytes 1572872 | tf_op jit(solution)/shard_map/rim_exchange/ppermute | solution.py:613
  10.0 5.9 %base_moments.1 = (f32[4,72,80,128]{3,2,1,0:T(8,128)S(1)}, f32[4,64,128]{2,1,0:T(8,128)S(1)}, f32[23,32,128]{2,1,0:T(8,128)S(1)}, f32[23,32,128]{2,1,0:T(8,128)S(1)}) custom-call(f32[4,64,64,128]{3,2,1,0:T(8,128)} %flow.3), custom_call_target="tpu_custom_call" | custom-call | flops 1000 | bytes 1000 | tf_op jit(solution)/shard_map/base_moments/pallas_call | solution.py:216
  15.9 5.1 %collective-permute-start = (f32[23,32,128]{2,1,0:T(8,128)S(1)}, f32[23,32,128]{2,1,0:T(8,128)S(1)}, u32[]{:S(2)}, u32[]{:S(2)}) collective-permute-start(f32[23,32,128]{2,1,0:T(8,128)S(1)} %get-tuple-element.32), channel_id=1, source_target_pairs={{0,1},{1,0},{2,3},{3,2},{4,5},{5,4},{6,7},{7,6},{8,9},{9,8},{10,11... | collective-permute-start | bytes 1130504 | tf_op jit(solution)/shard_map/base_core/ppermute | solution.py:598
  21.0 3.7 %y_slopes.1 = (f32[4,64,64,128]{3,2,1,0:T(8,128)S(1)}, f32[128,128]{1,0:T(8,128)S(1)}) custom-call(f32[4,72,80,128]{3,2,1,0:T(8,128)S(1)} %get-tuple-element.38.pad.pad_in, f32[128,128]{1,0:T(8,128)S(1)} %copy-done), custom_call_target="tpu_custom_call" | custom-call | flops 1000 | bytes 1000 | tf_op jit(solution)/shard_map/y_slopes/pallas_call | solution.py:236
  24.7 0.1 core_base.1
  24.8 0.1 collective-permute-start.1
  24.9 0.6 collective-permute-start.2
  25.6 2.1 %collective-permute-start.3 = (f32[23,8,128]{2,1,0:T(8,128)S(1)}, f32[23,8,128]{2,1,0:T(8,128)S(1)}, u32[]{:S(2)}, u32[]{:S(2)}) collective-permute-start(f32[23,8,128]{2,1,0:T(8,128)S(1)} %get-tuple-element.36), channel_id=1, source_target_pairs={{0,6},{2,0},{4,2},{6,4},{1,7},{3,1},{5,3},{7,5},{8,14},{10,8},{12,... | collective-permute-start | bytes 282632 | tf_op jit(solution)/shard_map/base_span/ppermute | solution.py:598
  27.7 9.4 %inner_moments.1 = (f32[4,72,80,128]{3,2,1,0:T(8,128)S(1)}, f32[21,32,128]{2,1,0:T(8,128)S(1)}, f32[21,32,128]{2,1,0:T(8,128)S(1)}) custom-call(f32[4,72,80,128]{3,2,1,0:T(8,128)S(1)} %get-tuple-element.38.pad.pad_in, f32[4,64,64,128]{3,2,1,0:T(8,128)S(1)} %get-tuple-element.39.ysl, ...), custom_call_target="tpu_custom_call", output_to_operand_aliasing={{0}: (0, {})} | custom-call | flops 1500000000 | bytes 84000000 | tf_op jit(solution)/shard_map/inner_moments/pallas_call | solution.py:360
  37.1 0.0 collective-permute-done.1.one.refs_1_
  37.1 0.0 collective-permute-done.3.three.refs_3_
  37.1 0.1 span_base.1
  37.2 0.0 collective-permute-done.7.xl
  37.2 1.7 %edge_moments.1 = (f32[4,72,80,128]{3,2,1,0:T(8,128)S(1)}, f32[21,32,128]{2,1,0:T(8,128)S(1)}, f32[21,32,128]{2,1,0:T(8,128)S(1)}) custom-call(f32[4,72,80,128]{3,2,1,0:T(8,128)S(1)} %get-tuple-element.43.pad_in, f32[21,32,128]{2,1,0:T(8,128)S(1)} %get-tuple-element.44.keep_in, ...), custom_call_target="tpu_custom_call", output_to_operand_aliasing={{0}: (0, {}), {1}: (1, {}), {2}: (2, {})} | custom-call | flops 52428800 | bytes 1048576 | tf_op jit(solution)/shard_map/edge_moments/pallas_call | solution.py:430
  38.9 0.7 collective-permute-start.9
  39.5 2.1 %collective-permute-start.4 = (f32[23,8,128]{2,1,0:T(8,128)S(1)}, f32[23,8,128]{2,1,0:T(8,128)S(1)}, u32[]{:S(2)}, u32[]{:S(2)}) collective-permute-start(f32[23,8,128]{2,1,0:T(8,128)S(1)} %get-tuple-element.37.after.mine1.mine), channel_id=1, source_target_pairs={{0,8},{8,0},{1,9},{9,1},{2,10},{10,2},{3,11},{11,3},{4,12},{12,4},... | collective-permute-start | bytes 282632 | tf_op jit(solution)/shard_map/base_x/ppermute | solution.py:598
  41.6 0.2 core_slope.1
  41.9 0.6 collective-permute-start.10
  42.5 2.2 %collective-permute-start.11 = (f32[21,8,128]{2,1,0:T(8,128)S(1)}, f32[21,8,128]{2,1,0:T(8,128)S(1)}, u32[]{:S(2)}, u32[]{:S(2)}) collective-permute-start(f32[21,8,128]{2,1,0:T(8,128)S(1)} %get-tuple-element.53), channel_id=1, source_target_pairs={{0,4},{2,6},{4,0},{6,2},{1,5},{3,7},{5,1},{7,3},{8,12},{10,14},{12... | collective-permute-start | bytes 258056 | tf_op jit(solution)/shard_map/slope_span/ppermute | solution.py:598
  44.6 2.0 %collective-permute-start.12 = (f32[21,8,128]{2,1,0:T(8,128)S(1)}, f32[21,8,128]{2,1,0:T(8,128)S(1)}, u32[]{:S(2)}, u32[]{:S(2)}) collective-permute-start(f32[21,8,128]{2,1,0:T(8,128)S(1)} %get-tuple-element.54), channel_id=1, source_target_pairs={{0,6},{2,0},{4,2},{6,4},{1,7},{3,1},{5,3},{7,5},{8,14},{10,8},{12,... | collective-permute-start | bytes 258056 | tf_op jit(solution)/shard_map/slope_span/ppermute | solution.py:598
  46.6 0.0 collective-permute-done.4.other1.other
  46.6 0.1 collective-permute-start.14
  46.7 1.4 %collective-permute-start.15 = (f32[22,8,128]{2,1,0:T(8,128)S(1)}, f32[22,8,128]{2,1,0:T(8,128)S(1)}, u32[]{:S(2)}, u32[]{:S(2)}) collective-permute-start(f32[22,8,128]{2,1,0:T(8,128)S(1)} %last_base.1.refs_0_), channel_id=1, source_target_pairs={{0,4},{2,6},{4,0},{6,2},{1,5},{3,7},{5,1},{7,3},{8,12},{10,14},{12... | collective-permute-start | bytes 270344 | tf_op jit(solution)/shard_map/base_spread/ppermute | solution.py:598
  48.1 0.0 collective-permute-done.10.refs_5_
  48.1 2.0 %collective-permute-start.16 = (f32[22,8,128]{2,1,0:T(8,128)S(1)}, f32[22,8,128]{2,1,0:T(8,128)S(1)}, u32[]{:S(2)}, u32[]{:S(2)}) collective-permute-start(f32[22,8,128]{2,1,0:T(8,128)S(1)} %last_base.1.refs_0_), channel_id=1, source_target_pairs={{0,6},{2,0},{4,2},{6,4},{1,7},{3,1},{5,3},{7,5},{8,14},{10,8},{12,... | collective-permute-start | bytes 270344 | tf_op jit(solution)/shard_map/base_spread/ppermute | solution.py:598
  50.1 0.0 collective-permute-done.11.refs_6_
  50.1 0.3 span_slope.1.mine2
  50.3 2.2 %collective-permute-start.13 = (f32[21,8,128]{2,1,0:T(8,128)S(1)}, f32[21,8,128]{2,1,0:T(8,128)S(1)}, u32[]{:S(2)}, u32[]{:S(2)}) collective-permute-start(f32[21,8,128]{2,1,0:T(8,128)S(1)} %span_slope.1.mine2), channel_id=1, source_target_pairs={{0,8},{8,0},{1,9},{9,1},{2,10},{10,2},{3,11},{11,3},{4,12},{12,4},... | collective-permute-start | bytes 258056 | tf_op jit(solution)/shard_map/slope_x/ppermute | solution.py:598
  52.5 2.7 %collective-permute-done.13.other2 = f32[21,8,128]{2,1,0:T(8,128)S(1)} collective-permute-done((f32[21,8,128]{2,1,0:T(8,128)S(1)}, f32[21,8,128]{2,1,0:T(8,128)S(1)}, u32[]{:S(2)}, u32[]{:S(2)}) %collective-permute-start.13) | collective-permute-done | bytes 86048 | tf_op jit(solution)/shard_map/slope_x/ppermute | solution.py:598
  55.3 0.2 last_slope.1.after.refs_2_
  55.5 0.0 collective-permute-done.14.refs_1_
  55.5 0.1 gather.1.refs_0_
  55.6 2.9 %collective-permute-start.17 = (f32[22,32,128]{2,1,0:T(8,128)S(1)}, f32[22,32,128]{2,1,0:T(8,128)S(1)}, u32[]{:S(2)}, u32[]{:S(2)}) collective-permute-start(f32[22,32,128]{2,1,0:T(8,128)S(1)} %gather.1.refs_0_), channel_id=1, source_target_pairs={{0,1},{1,0},{2,3},{3,2},{4,5},{5,4},{6,7},{7,6},{8,9},{9,8},{10,11... | collective-permute-start | bytes 1081352 | tf_op jit(solution)/shard_map/base_spread/ppermute | solution.py:598
  58.5 0.2 collective-permute-start.18
  58.7 2.6 %collective-permute-start.19 = (f32[18,8,128]{2,1,0:T(8,128)S(1)}, f32[18,8,128]{2,1,0:T(8,128)S(1)}, u32[]{:S(2)}, u32[]{:S(2)}) collective-permute-start(f32[18,8,128]{2,1,0:T(8,128)S(1)} %last_slope.1.after.refs_2_), channel_id=1, source_target_pairs={{0,4},{2,6},{4,0},{6,2},{1,5},{3,7},{5,1},{7,3},{8,12},{10,14},{12... | collective-permute-start | bytes 221192 | tf_op jit(solution)/shard_map/slope_spread/ppermute | solution.py:598
  61.3 1.3 %collective-permute-start.20 = (f32[18,8,128]{2,1,0:T(8,128)S(1)}, f32[18,8,128]{2,1,0:T(8,128)S(1)}, u32[]{:S(2)}, u32[]{:S(2)}) collective-permute-start(f32[18,8,128]{2,1,0:T(8,128)S(1)} %last_slope.1.after.refs_2_), channel_id=1, source_target_pairs={{0,6},{2,0},{4,2},{6,4},{1,7},{3,1},{5,3},{7,5},{8,14},{10,8},{12,... | collective-permute-start | bytes 221192 | tf_op jit(solution)/shard_map/slope_spread/ppermute | solution.py:598
  62.6 0.9 %collective-permute-start.21 = (f32[18,8,128]{2,1,0:T(8,128)S(1)}, f32[18,8,128]{2,1,0:T(8,128)S(1)}, u32[]{:S(2)}, u32[]{:S(2)}) collective-permute-start(f32[18,8,128]{2,1,0:T(8,128)S(1)} %last_slope.1.after.refs_2_), channel_id=1, source_target_pairs={{0,1},{1,0},{2,3},{3,2},{4,5},{5,4},{6,7},{7,6},{8,9},{9,8},{10,11... | collective-permute-start | bytes 221192 | tf_op jit(solution)/shard_map/slope_spread/ppermute | solution.py:598
  63.5 0.0 collective-permute-done.18.refs_3_
  63.5 1.2 %collective-permute-start.22 = (f32[18,8,128]{2,1,0:T(8,128)S(1)}, f32[18,8,128]{2,1,0:T(8,128)S(1)}, u32[]{:S(2)}, u32[]{:S(2)}) collective-permute-start(f32[18,8,128]{2,1,0:T(8,128)S(1)} %collective-permute-done.18.refs_3_), channel_id=1, source_target_pairs={{0,1},{1,0},{2,3},{3,2},{4,5},{5,4},{6,7},{7,6},{8,9},{9,8},{10,11... | collective-permute-start | bytes 221192 | tf_op jit(solution)/shard_map/slope_spread/ppermute | solution.py:598
  64.7 0.5 collective-permute-done.19.refs_4_
  65.2 0.9 %collective-permute-start.23 = (f32[18,8,128]{2,1,0:T(8,128)S(1)}, f32[18,8,128]{2,1,0:T(8,128)S(1)}, u32[]{:S(2)}, u32[]{:S(2)}) collective-permute-start(f32[18,8,128]{2,1,0:T(8,128)S(1)} %collective-permute-done.19.refs_4_), channel_id=1, source_target_pairs={{0,1},{1,0},{2,3},{3,2},{4,5},{5,4},{6,7},{7,6},{8,9},{9,8},{10,11... | collective-permute-start | bytes 221192 | tf_op jit(solution)/shard_map/slope_spread/ppermute | solution.py:598
  66.1 0.5 collective-permute-start.24
  66.6 0.4 collective-permute-done.23.refs_8_
  67.0 0.5 collective-permute-done.24.refs_9_
  67.5 1.1 %place.1 = f32[40,64,128]{2,1,0:T(8,128)} custom-call(f32[22,32,128]{2,1,0:T(8,128)S(1)} %gather.1.refs_0_, f32[22,32,128]{2,1,0:T(8,128)S(1)} %collective-permute-done.17.refs_1_, f32[18,8,128]{2,1,0:T(8,128)S(1)} %last_slope.1.after.refs_2_, f32[18,8,128]{2,1,0:T(8,128)S(1)} %collective-permute-done.18.refs_3_, ...), custom_call_target="tpu_custom_call" | custom-call | tf_op jit(solution)/shard_map/place/pallas_call | solution.py:571
  (17 shorter events, 0.1 us)
Async XLA Ops:
  0.0 21.0 %copy-start = (f32[128,128]{1,0:T(8,128)S(1)}, f32[128,128]{1,0:T(8,128)}, u32[]{:S(2)}) copy-start(f32[128,128]{1,0:T(8,128)} %dy.1) | copy-start | bytes 196612
  1.5 23.4 %collective-permute-start.5 = (f32[3,64,4,128]{3,2,1,0:T(4,128)S(1)}, f32[3,64,4,128]{3,2,1,0:T(4,128)S(1)}, u32[]{:S(2)}, u32[]{:S(2)}) collective-permute-start(f32[3,64,4,128]{3,2,1,0:T(4,128)S(1)} %get-tuple-element.40), channel_id=1, source_target_pairs={{0,1},{1,2},{2,3},{3,4},{4,5},{5,6},{6,7},{7,8},{8,9},{9,10},{10,1... | collective-permute-start | bytes 1179656 | tf_op jit(solution)/shard_map/rim_exchange/ppermute | solution.py:598
  3.8 21.8 %collective-permute-start.6 = (f32[3,64,4,128]{3,2,1,0:T(4,128)S(1)}, f32[3,64,4,128]{3,2,1,0:T(4,128)S(1)}, u32[]{:S(2)}, u32[]{:S(2)}) collective-permute-start(f32[3,64,4,128]{3,2,1,0:T(4,128)S(1)} %get-tuple-element.41), channel_id=1, source_target_pairs={{0,15},{1,0},{2,1},{3,2},{4,3},{5,4},{6,5},{7,6},{8,7},{9,8},{10,9... | collective-permute-start | bytes 1179656 | tf_op jit(solution)/shard_map/rim_exchange/ppermute | solution.py:598
  3.8 33.4 %collective-permute-start.7 = (f32[4,4,64,128]{3,2,1,0:T(8,128)S(1)}, f32[4,4,64,128]{3,2,1,0:T(8,128)S(1)}, u32[]{:S(2)}, u32[]{:S(2)}) collective-permute-start(f32[4,4,64,128]{3,2,1,0:T(8,128)S(1)} %get-tuple-element.46), channel_id=1, source_target_pairs={{0,16},{16,32},{32,48},{48,64},{64,80},{80,96},{96,112},{1,17},{17... | collective-permute-start | bytes 1572872 | tf_op jit(solution)/shard_map/rim_exchange/ppermute | solution.py:612
  6.9 30.3 %collective-permute-start.8 = (f32[4,4,64,128]{3,2,1,0:T(8,128)S(1)}, f32[4,4,64,128]{3,2,1,0:T(8,128)S(1)}, u32[]{:S(2)}, u32[]{:S(2)}) collective-permute-start(f32[4,4,64,128]{3,2,1,0:T(8,128)S(1)} %get-tuple-element.47), channel_id=1, source_target_pairs={{16,0},{32,16},{48,32},{64,48},{80,64},{96,80},{112,96},{17,1},{33... | collective-permute-start | bytes 1572872 | tf_op jit(solution)/shard_map/rim_exchange/ppermute | solution.py:613
  15.9 8.8 %collective-permute-start = (f32[23,32,128]{2,1,0:T(8,128)S(1)}, f32[23,32,128]{2,1,0:T(8,128)S(1)}, u32[]{:S(2)}, u32[]{:S(2)}) collective-permute-start(f32[23,32,128]{2,1,0:T(8,128)S(1)} %get-tuple-element.32), channel_id=1, source_target_pairs={{0,1},{1,0},{2,3},{3,2},{4,5},{5,4},{6,7},{7,6},{8,9},{9,8},{10,11... | collective-permute-start | bytes 1130504 | tf_op jit(solution)/shard_map/base_core/ppermute | solution.py:598
  24.8 12.3 %collective-permute-start.1 = (f32[23,8,128]{2,1,0:T(8,128)S(1)}, f32[23,8,128]{2,1,0:T(8,128)S(1)}, u32[]{:S(2)}, u32[]{:S(2)}) collective-permute-start(f32[23,8,128]{2,1,0:T(8,128)S(1)} %get-tuple-element.34), channel_id=1, source_target_pairs={{0,2},{2,4},{4,6},{6,0},{1,3},{3,5},{5,7},{7,1},{8,10},{10,12},{12... | collective-permute-start | bytes 282632 | tf_op jit(solution)/shard_map/base_span/ppermute | solution.py:598
  24.9 12.2 %collective-permute-start.2 = (f32[23,8,128]{2,1,0:T(8,128)S(1)}, f32[23,8,128]{2,1,0:T(8,128)S(1)}, u32[]{:S(2)}, u32[]{:S(2)}) collective-permute-start(f32[23,8,128]{2,1,0:T(8,128)S(1)} %get-tuple-element.35), channel_id=1, source_target_pairs={{0,4},{2,6},{4,0},{6,2},{1,5},{3,7},{5,1},{7,3},{8,12},{10,14},{12... | collective-permute-start | bytes 282632 | tf_op jit(solution)/shard_map/base_span/ppermute | solution.py:598
  25.6 11.5 %collective-permute-start.3 = (f32[23,8,128]{2,1,0:T(8,128)S(1)}, f32[23,8,128]{2,1,0:T(8,128)S(1)}, u32[]{:S(2)}, u32[]{:S(2)}) collective-permute-start(f32[23,8,128]{2,1,0:T(8,128)S(1)} %get-tuple-element.36), channel_id=1, source_target_pairs={{0,6},{2,0},{4,2},{6,4},{1,7},{3,1},{5,3},{7,5},{8,14},{10,8},{12,... | collective-permute-start | bytes 282632 | tf_op jit(solution)/shard_map/base_span/ppermute | solution.py:598
  38.9 2.8 %collective-permute-start.9 = (f32[21,32,128]{2,1,0:T(8,128)S(1)}, f32[21,32,128]{2,1,0:T(8,128)S(1)}, u32[]{:S(2)}, u32[]{:S(2)}) collective-permute-start(f32[21,32,128]{2,1,0:T(8,128)S(1)} %get-tuple-element.49), channel_id=1, source_target_pairs={{0,1},{1,0},{2,3},{3,2},{4,5},{5,4},{6,7},{7,6},{8,9},{9,8},{10,11... | collective-permute-start | bytes 1032200 | tf_op jit(solution)/shard_map/slope_core/ppermute | solution.py:598
  39.5 7.1 %collective-permute-start.4 = (f32[23,8,128]{2,1,0:T(8,128)S(1)}, f32[23,8,128]{2,1,0:T(8,128)S(1)}, u32[]{:S(2)}, u32[]{:S(2)}) collective-permute-start(f32[23,8,128]{2,1,0:T(8,128)S(1)} %get-tuple-element.37.after.mine1.mine), channel_id=1, source_target_pairs={{0,8},{8,0},{1,9},{9,1},{2,10},{10,2},{3,11},{11,3},{4,12},{12,4},... | collective-permute-start | bytes 282632 | tf_op jit(solution)/shard_map/base_x/ppermute | solution.py:598
  41.9 6.2 %collective-permute-start.10 = (f32[21,8,128]{2,1,0:T(8,128)S(1)}, f32[21,8,128]{2,1,0:T(8,128)S(1)}, u32[]{:S(2)}, u32[]{:S(2)}) collective-permute-start(f32[21,8,128]{2,1,0:T(8,128)S(1)} %get-tuple-element.52), channel_id=1, source_target_pairs={{0,2},{2,4},{4,6},{6,0},{1,3},{3,5},{5,7},{7,1},{8,10},{10,12},{12... | collective-permute-start | bytes 258056 | tf_op jit(solution)/shard_map/slope_span/ppermute | solution.py:598
  42.5 7.6 %collective-permute-start.11 = (f32[21,8,128]{2,1,0:T(8,128)S(1)}, f32[21,8,128]{2,1,0:T(8,128)S(1)}, u32[]{:S(2)}, u32[]{:S(2)}) collective-permute-start(f32[21,8,128]{2,1,0:T(8,128)S(1)} %get-tuple-element.53), channel_id=1, source_target_pairs={{0,4},{2,6},{4,0},{6,2},{1,5},{3,7},{5,1},{7,3},{8,12},{10,14},{12... | collective-permute-start | bytes 258056 | tf_op jit(solution)/shard_map/slope_span/ppermute | solution.py:598
  44.6 5.4 %collective-permute-start.12 = (f32[21,8,128]{2,1,0:T(8,128)S(1)}, f32[21,8,128]{2,1,0:T(8,128)S(1)}, u32[]{:S(2)}, u32[]{:S(2)}) collective-permute-start(f32[21,8,128]{2,1,0:T(8,128)S(1)} %get-tuple-element.54), channel_id=1, source_target_pairs={{0,6},{2,0},{4,2},{6,4},{1,7},{3,1},{5,3},{7,5},{8,14},{10,8},{12,... | collective-permute-start | bytes 258056 | tf_op jit(solution)/shard_map/slope_span/ppermute | solution.py:598
  46.6 8.8 %collective-permute-start.14 = (f32[22,8,128]{2,1,0:T(8,128)S(1)}, f32[22,8,128]{2,1,0:T(8,128)S(1)}, u32[]{:S(2)}, u32[]{:S(2)}) collective-permute-start(f32[22,8,128]{2,1,0:T(8,128)S(1)} %last_base.1.refs_0_), channel_id=1, source_target_pairs={{0,2},{2,4},{4,6},{6,0},{1,3},{3,5},{5,7},{7,1},{8,10},{10,12},{12... | collective-permute-start | bytes 270344 | tf_op jit(solution)/shard_map/base_spread/ppermute | solution.py:598
  46.7 8.8 %collective-permute-start.15 = (f32[22,8,128]{2,1,0:T(8,128)S(1)}, f32[22,8,128]{2,1,0:T(8,128)S(1)}, u32[]{:S(2)}, u32[]{:S(2)}) collective-permute-start(f32[22,8,128]{2,1,0:T(8,128)S(1)} %last_base.1.refs_0_), channel_id=1, source_target_pairs={{0,4},{2,6},{4,0},{6,2},{1,5},{3,7},{5,1},{7,3},{8,12},{10,14},{12... | collective-permute-start | bytes 270344 | tf_op jit(solution)/shard_map/base_spread/ppermute | solution.py:598
  48.1 7.4 %collective-permute-start.16 = (f32[22,8,128]{2,1,0:T(8,128)S(1)}, f32[22,8,128]{2,1,0:T(8,128)S(1)}, u32[]{:S(2)}, u32[]{:S(2)}) collective-permute-start(f32[22,8,128]{2,1,0:T(8,128)S(1)} %last_base.1.refs_0_), channel_id=1, source_target_pairs={{0,6},{2,0},{4,2},{6,4},{1,7},{3,1},{5,3},{7,5},{8,14},{10,8},{12,... | collective-permute-start | bytes 270344 | tf_op jit(solution)/shard_map/base_spread/ppermute | solution.py:598
  50.3 4.9 %collective-permute-start.13 = (f32[21,8,128]{2,1,0:T(8,128)S(1)}, f32[21,8,128]{2,1,0:T(8,128)S(1)}, u32[]{:S(2)}, u32[]{:S(2)}) collective-permute-start(f32[21,8,128]{2,1,0:T(8,128)S(1)} %span_slope.1.mine2), channel_id=1, source_target_pairs={{0,8},{8,0},{1,9},{9,1},{2,10},{10,2},{3,11},{11,3},{4,12},{12,4},... | collective-permute-start | bytes 258056 | tf_op jit(solution)/shard_map/slope_x/ppermute | solution.py:598
  55.6 11.9 %collective-permute-start.17 = (f32[22,32,128]{2,1,0:T(8,128)S(1)}, f32[22,32,128]{2,1,0:T(8,128)S(1)}, u32[]{:S(2)}, u32[]{:S(2)}) collective-permute-start(f32[22,32,128]{2,1,0:T(8,128)S(1)} %gather.1.refs_0_), channel_id=1, source_target_pairs={{0,1},{1,0},{2,3},{3,2},{4,5},{5,4},{6,7},{7,6},{8,9},{9,8},{10,11... | collective-permute-start | bytes 1081352 | tf_op jit(solution)/shard_map/base_spread/ppermute | solution.py:598
  58.5 5.0 %collective-permute-start.18 = (f32[18,8,128]{2,1,0:T(8,128)S(1)}, f32[18,8,128]{2,1,0:T(8,128)S(1)}, u32[]{:S(2)}, u32[]{:S(2)}) collective-permute-start(f32[18,8,128]{2,1,0:T(8,128)S(1)} %last_slope.1.after.refs_2_), channel_id=1, source_target_pairs={{0,2},{2,4},{4,6},{6,0},{1,3},{3,5},{5,7},{7,1},{8,10},{10,12},{12... | collective-permute-start | bytes 221192 | tf_op jit(solution)/shard_map/slope_spread/ppermute | solution.py:598
  58.7 6.5 %collective-permute-start.19 = (f32[18,8,128]{2,1,0:T(8,128)S(1)}, f32[18,8,128]{2,1,0:T(8,128)S(1)}, u32[]{:S(2)}, u32[]{:S(2)}) collective-permute-start(f32[18,8,128]{2,1,0:T(8,128)S(1)} %last_slope.1.after.refs_2_), channel_id=1, source_target_pairs={{0,4},{2,6},{4,0},{6,2},{1,5},{3,7},{5,1},{7,3},{8,12},{10,14},{12... | collective-permute-start | bytes 221192 | tf_op jit(solution)/shard_map/slope_spread/ppermute | solution.py:598
  61.3 4.8 %collective-permute-start.20 = (f32[18,8,128]{2,1,0:T(8,128)S(1)}, f32[18,8,128]{2,1,0:T(8,128)S(1)}, u32[]{:S(2)}, u32[]{:S(2)}) collective-permute-start(f32[18,8,128]{2,1,0:T(8,128)S(1)} %last_slope.1.after.refs_2_), channel_id=1, source_target_pairs={{0,6},{2,0},{4,2},{6,4},{1,7},{3,1},{5,3},{7,5},{8,14},{10,8},{12,... | collective-permute-start | bytes 221192 | tf_op jit(solution)/shard_map/slope_spread/ppermute | solution.py:598
  62.6 4.0 %collective-permute-start.21 = (f32[18,8,128]{2,1,0:T(8,128)S(1)}, f32[18,8,128]{2,1,0:T(8,128)S(1)}, u32[]{:S(2)}, u32[]{:S(2)}) collective-permute-start(f32[18,8,128]{2,1,0:T(8,128)S(1)} %last_slope.1.after.refs_2_), channel_id=1, source_target_pairs={{0,1},{1,0},{2,3},{3,2},{4,5},{5,4},{6,7},{7,6},{8,9},{9,8},{10,11... | collective-permute-start | bytes 221192 | tf_op jit(solution)/shard_map/slope_spread/ppermute | solution.py:598
  63.5 3.0 %collective-permute-start.22 = (f32[18,8,128]{2,1,0:T(8,128)S(1)}, f32[18,8,128]{2,1,0:T(8,128)S(1)}, u32[]{:S(2)}, u32[]{:S(2)}) collective-permute-start(f32[18,8,128]{2,1,0:T(8,128)S(1)} %collective-permute-done.18.refs_3_), channel_id=1, source_target_pairs={{0,1},{1,0},{2,3},{3,2},{4,5},{5,4},{6,7},{7,6},{8,9},{9,8},{10,11... | collective-permute-start | bytes 221192 | tf_op jit(solution)/shard_map/slope_spread/ppermute | solution.py:598
  65.2 1.8 %collective-permute-start.23 = (f32[18,8,128]{2,1,0:T(8,128)S(1)}, f32[18,8,128]{2,1,0:T(8,128)S(1)}, u32[]{:S(2)}, u32[]{:S(2)}) collective-permute-start(f32[18,8,128]{2,1,0:T(8,128)S(1)} %collective-permute-done.19.refs_4_), channel_id=1, source_target_pairs={{0,1},{1,0},{2,3},{3,2},{4,5},{5,4},{6,7},{7,6},{8,9},{9,8},{10,11... | collective-permute-start | bytes 221192 | tf_op jit(solution)/shard_map/slope_spread/ppermute | solution.py:598
  66.1 1.4 %collective-permute-start.24 = (f32[18,8,128]{2,1,0:T(8,128)S(1)}, f32[18,8,128]{2,1,0:T(8,128)S(1)}, u32[]{:S(2)}, u32[]{:S(2)}) collective-permute-start(f32[18,8,128]{2,1,0:T(8,128)S(1)} %collective-permute-done.20.refs_5_), channel_id=1, source_target_pairs={{0,1},{1,0},{2,3},{3,2},{4,5},{5,4},{6,7},{7,6},{8,9},{9,8},{10,11... | collective-permute-start | bytes 221192 | tf_op jit(solution)/shard_map/slope_spread/ppermute | solution.py:598

commit v5 on v4

--- a/solution.py
+++ b/solution.py
@@ -110,24 +110,11 @@
     )(flow, *after)
 
 
-def base_kernel(flow, pad, mean, keep, send, raw, acc, sems):
+def base_kernel(raw, pad, mean, keep, send, acc):
     _, lx, ny = mean.shape
     lz = pad.shape[2] - 16
     half = lx // 2
     core = lax.axis_index(CA)
-    step = 8
-    parts = lx // step
-
-    def fetch(k):
-        return pltpu.make_async_copy(
-            flow.at[:, pl.ds(step * k, step)],
-            raw.at[:, pl.ds(step * k, step)],
-            sems.at[k],
-        )
-
-    for k in range(parts):
-        fetch(k).start()
-
     def one(x, _):
         centre = []
         for c in range(4):
@@ -155,11 +142,7 @@
             acc[pl.ds(pl.multiple_of(n * 8 * lx + 8 * x, 8), 8), :] = total[n]
         return 0
 
-    def part(k, _):
-        fetch(k).wait()
-        return lax.fori_loop(0, step, lambda r, _: one(step * k + r, _), 0, unroll=2)
-
-    lax.fori_loop(0, parts, part, 0)
+    lax.fori_loop(0, lx, one, 0, unroll=2)
     for out, side in ((send, 1 - core), (keep, core)):
         at = pl.multiple_of(half * side, 8)
         for c in range(4):
@@ -170,7 +153,7 @@
 
 def y_kernel(pad, dy, ysl, dmat, weights):
     _, lx, lz, ny = ysl.shape
-    step = 8
+    step = 16
     d = dy[...].T * (1.0 / lead)
     dmat[...] = d
     dhi = d.astype(BF16)
@@ -215,18 +198,16 @@
     shapes = [(4, lx + 8, lz + 16, ny), (4, lx, ny), half, half]
     return pl.pallas_call(
         base_kernel,
-        in_specs=[pl.BlockSpec(memory_space=pltpu.HBM)],
+        in_specs=[vm],
         out_specs=[vm] * 4,
         out_shape=[pltpu.VMEM(s, F32) for s in shapes],
         scratch_shapes=[
-            pltpu.VMEM((4, lx, lz, ny), F32),
             pltpu.VMEM((NBASE * 8 * lx, ny), F32),
-            pltpu.SemaphoreType.DMA((lx // 8,)),
         ],
         compiler_params=pltpu.CompilerParams(vmem_limit_bytes=16 * 2**20),
         cost_estimate=pl.CostEstimate(flops=1000, bytes_accessed=1000, transcendentals=0),
         name="base_moments",
-    )(pltpu.with_memory_space_constraint(flow, pltpu.HBM))
+    )(pltpu.with_memory_space_constraint(flow, pltpu.VMEM))
 
 
 def y_slopes(pad, dy):
@@ -406,7 +387,7 @@
             acc[pl.ds(pl.multiple_of(k * 64 + 8 * i, 8), 8), :] = total[k]
         return 0
 
-    lax.fori_loop(0, 8, one, 0)
+    lax.fori_loop(0, 8, one, 0, unroll=4)
 
     pressure = jnp.concatenate([mean[3, pl.ds(0, 4), :], mean[3, pl.ds(lx - 4, 4), :]], axis=0)
     fields = list(slope_fields(lambda k: row_sum(k, 8, acc), pressure))

time: 68.9 us -> 68.6 us (level)
  waiting for transfers between devices: 4.25 us -> 8.31 us
  starting transfers between devices: 39.9 us -> 36.9 us
  Pallas kernels: 24.2 us -> 22.3 us
    ppermute x23, waiting for transfers between devices: 4.25 us -> 8.3 us  [send(): lax.ppermute(value, axis, [(i, (i + step) % size) for i in range(size)])]
    ppermute x23, starting transfers between devices: 33.7 us -> 30.7 us  [send(): lax.ppermute(value, axis, [(i, (i + step) % size) for i in range(size)])]
    pallas_call x1, Pallas kernels: 5.88 us -> 4.54 us  [base_moments(): pl.pallas_call(base_kernel, in_specs=[vm], out_specs=[vm] * 4, out_shape=...]
    pallas_call x1, Pallas kernels: 3.68 us -> 2.98 us  [y_slopes(): pl.pallas_call(y_kernel, in_specs=[vm, vm], out_specs=[vm, vm], out_shape...]
  transfers between devices with their start and end apart: 25 -> 25, of which waited for: 4 -> 6; matrix products, arithmetic and copies ran while one was open for 0% -> 0% of each run, Pallas kernels for 29% -> 26%
where the time goes in v5:
time: 68.6 us; the launch traced here: 67.7 us
  starting transfers between devices  36.9 us (54%)
  Pallas kernels  22.3 us (33%)
  waiting for transfers between devices  8.31 us (12%)
    ppermute x23, starting transfers between devices, send(): lax.ppermute(value, axis, [(i, (i + step) % size) for i in range(size)])  30.7 us
    pallas_call x1, Pallas kernels, inner_moments(): pl.pallas_call(inner_kernel, in_specs=[vm] * 5 + [pl.BlockSpec(memory_spa...  9.44 us
    ppermute x23, waiting for transfers between devices, send(): lax.ppermute(value, axis, [(i, (i + step) % size) for i in range(size)])  8.3 us
    pallas_call x1, Pallas kernels, base_moments(): pl.pallas_call(base_kernel, in_specs=[vm], out_specs=[vm] * 4, out_shape=...  4.54 us
    ppermute x1, starting transfers between devices, shards(): xl = lax.ppermute(xl, GXA, up)  3.11 us
    ppermute x1, starting transfers between devices, shards(): xr = lax.ppermute(xr, GXA, down)  3.06 us
    pallas_call x1, Pallas kernels, y_slopes(): pl.pallas_call(y_kernel, in_specs=[vm, vm], out_specs=[vm, vm], out_shape...  2.98 us
    pallas_call x1, Pallas kernels, cut(): pl.pallas_call(kernel, in_specs=[pl.BlockSpec(memory_space=pltpu.HBM)] +...  1.64 us
  transfers between devices with their start and end apart: 25, of which 6 were waited for; matrix products, arithmetic and copies ran while one was open for 0% of the time, Pallas kernels for 26%

profile of v5, /device:TPU:9, one launch (start us, length us, event | category | flops | bytes accessed | tf_op | source)
XLA Modules:
  0.0 67.7 jit_solution(2173928435738017349)
XLA Ops:
  0.0 1.6 %rims.1 = (f32[3,64,4,128]{3,2,1,0:T(4,128)S(1)}, f32[3,64,4,128]{3,2,1,0:T(4,128)S(1)}, f32[4,4,64,128]{3,2,1,0:T(8,128)S(1)}, f32[4,4,64,128]{3,2,1,0:T(8,128)S(1)}) custom-call(f32[4,64,64,128]{3,2,1,0:T(8,128)} %flow.1), custom_call_target="tpu_custom_call" | custom-call | tf_op jit(solution)/shard_map/rims/pallas_call | solution.py:101
  1.7 2.3 %collective-permute-start.5 = (f32[3,64,4,128]{3,2,1,0:T(4,128)S(1)}, f32[3,64,4,128]{3,2,1,0:T(4,128)S(1)}, u32[]{:S(2)}, u32[]{:S(2)}) collective-permute-start(f32[3,64,4,128]{3,2,1,0:T(4,128)S(1)} %get-tuple-element.40), channel_id=1, source_target_pairs={{0,1},{1,2},{2,3},{3,4},{4,5},{5,6},{6,7},{7,8},{8,9},{9,10},{10,1... | collective-permute-start | bytes 1179656 | tf_op jit(solution)/shard_map/rim_exchange/ppermute | solution.py:579
  3.9 3.1 %collective-permute-start.7 = (f32[4,4,64,128]{3,2,1,0:T(8,128)S(1)}, f32[4,4,64,128]{3,2,1,0:T(8,128)S(1)}, u32[]{:S(2)}, u32[]{:S(2)}) collective-permute-start(f32[4,4,64,128]{3,2,1,0:T(8,128)S(1)} %get-tuple-element.46), channel_id=1, source_target_pairs={{0,16},{16,32},{32,48},{48,64},{64,80},{80,96},{96,112},{1,17},{17... | collective-permute-start | bytes 1572872 | tf_op jit(solution)/shard_map/rim_exchange/ppermute | solution.py:593
  7.0 3.1 %collective-permute-start.8 = (f32[4,4,64,128]{3,2,1,0:T(8,128)S(1)}, f32[4,4,64,128]{3,2,1,0:T(8,128)S(1)}, u32[]{:S(2)}, u32[]{:S(2)}) collective-permute-start(f32[4,4,64,128]{3,2,1,0:T(8,128)S(1)} %get-tuple-element.47), channel_id=1, source_target_pairs={{16,0},{32,16},{48,32},{64,48},{80,64},{96,80},{112,96},{17,1},{33... | collective-permute-start | bytes 1572872 | tf_op jit(solution)/shard_map/rim_exchange/ppermute | solution.py:594
  10.1 4.5 %base_moments.1 = (f32[4,72,80,128]{3,2,1,0:T(8,128)S(1)}, f32[4,64,128]{2,1,0:T(8,128)S(1)}, f32[23,32,128]{2,1,0:T(8,128)S(1)}, f32[23,32,128]{2,1,0:T(8,128)S(1)}) custom-call(f32[4,64,64,128]{3,2,1,0:T(8,128)S(1)} %copy-done), custom_call_target="tpu_custom_call" | custom-call | flops 1000 | bytes 1000 | tf_op jit(solution)/shard_map/base_moments/pallas_call | solution.py:199
  14.7 5.1 %collective-permute-start = (f32[23,32,128]{2,1,0:T(8,128)S(1)}, f32[23,32,128]{2,1,0:T(8,128)S(1)}, u32[]{:S(2)}, u32[]{:S(2)}) collective-permute-start(f32[23,32,128]{2,1,0:T(8,128)S(1)} %get-tuple-element.32), channel_id=1, source_target_pairs={{0,1},{1,0},{2,3},{3,2},{4,5},{5,4},{6,7},{7,6},{8,9},{9,8},{10,11... | collective-permute-start | bytes 1130504 | tf_op jit(solution)/shard_map/base_core/ppermute | solution.py:579
  19.8 3.0 %y_slopes.1 = (f32[4,64,64,128]{3,2,1,0:T(8,128)S(1)}, f32[128,128]{1,0:T(8,128)S(1)}) custom-call(f32[4,72,80,128]{3,2,1,0:T(8,128)S(1)} %get-tuple-element.38.pad.pad_in, f32[128,128]{1,0:T(8,128)S(1)} %copy-done.1), custom_call_target="tpu_custom_call" | custom-call | flops 1000 | bytes 1000 | tf_op jit(solution)/shard_map/y_slopes/pallas_call | solution.py:217
  22.8 0.1 core_base.1
  22.9 0.1 collective-permute-start.1
  23.0 0.0 collective-permute-done.5.zl
  23.0 0.7 collective-permute-start.2
  23.7 2.1 %collective-permute-start.3 = (f32[23,8,128]{2,1,0:T(8,128)S(1)}, f32[23,8,128]{2,1,0:T(8,128)S(1)}, u32[]{:S(2)}, u32[]{:S(2)}) collective-permute-start(f32[23,8,128]{2,1,0:T(8,128)S(1)} %get-tuple-element.36), channel_id=1, source_target_pairs={{0,6},{2,0},{4,2},{6,4},{1,7},{3,1},{5,3},{7,5},{8,14},{10,8},{12,... | collective-permute-start | bytes 282632 | tf_op jit(solution)/shard_map/base_span/ppermute | solution.py:579
  25.8 9.4 %inner_moments.1 = (f32[4,72,80,128]{3,2,1,0:T(8,128)S(1)}, f32[21,32,128]{2,1,0:T(8,128)S(1)}, f32[21,32,128]{2,1,0:T(8,128)S(1)}) custom-call(f32[4,72,80,128]{3,2,1,0:T(8,128)S(1)} %get-tuple-element.38.pad.pad_in, f32[4,64,64,128]{3,2,1,0:T(8,128)S(1)} %get-tuple-element.39.ysl, ...), custom_call_target="tpu_custom_call", output_to_operand_aliasing={{0}: (0, {})} | custom-call | flops 1500000000 | bytes 84000000 | tf_op jit(solution)/shard_map/inner_moments/pallas_call | solution.py:341
  35.2 0.0 collective-permute-done.2.two.refs_2_
  35.2 0.0 collective-permute-done.3.three.refs_3_
  35.2 0.1 span_base.1
  35.3 0.0 collective-permute-done.7.xl
  35.3 1.6 %edge_moments.1 = (f32[4,72,80,128]{3,2,1,0:T(8,128)S(1)}, f32[21,32,128]{2,1,0:T(8,128)S(1)}, f32[21,32,128]{2,1,0:T(8,128)S(1)}) custom-call(f32[4,72,80,128]{3,2,1,0:T(8,128)S(1)} %get-tuple-element.43.pad_in, f32[21,32,128]{2,1,0:T(8,128)S(1)} %get-tuple-element.44.keep_in, ...), custom_call_target="tpu_custom_call", output_to_operand_aliasing={{0}: (0, {}), {1}: (1, {}), {2}: (2, {})} | custom-call | flops 52428800 | bytes 1048576 | tf_op jit(solution)/shard_map/edge_moments/pallas_call | solution.py:411
  36.9 1.4 %collective-permute-start.9 = (f32[21,32,128]{2,1,0:T(8,128)S(1)}, f32[21,32,128]{2,1,0:T(8,128)S(1)}, u32[]{:S(2)}, u32[]{:S(2)}) collective-permute-start(f32[21,32,128]{2,1,0:T(8,128)S(1)} %get-tuple-element.49), channel_id=1, source_target_pairs={{0,1},{1,0},{2,3},{3,2},{4,5},{5,4},{6,7},{7,6},{8,9},{9,8},{10,11... | collective-permute-start | bytes 1032200 | tf_op jit(solution)/shard_map/slope_core/ppermute | solution.py:579
  38.3 2.8 %collective-permute-start.4 = (f32[23,8,128]{2,1,0:T(8,128)S(1)}, f32[23,8,128]{2,1,0:T(8,128)S(1)}, u32[]{:S(2)}, u32[]{:S(2)}) collective-permute-start(f32[23,8,128]{2,1,0:T(8,128)S(1)} %get-tuple-element.37.after.mine1.mine), channel_id=1, source_target_pairs={{0,8},{8,0},{1,9},{9,1},{2,10},{10,2},{3,11},{11,3},{4,12},{12,4},... | collective-permute-start | bytes 282632 | tf_op jit(solution)/shard_map/base_x/ppermute | solution.py:579
  41.1 0.0 collective-permute-done.9.got2
  41.1 0.2 core_slope.1
  41.3 0.1 collective-permute-start.10
  41.4 1.3 %collective-permute-start.11 = (f32[21,8,128]{2,1,0:T(8,128)S(1)}, f32[21,8,128]{2,1,0:T(8,128)S(1)}, u32[]{:S(2)}, u32[]{:S(2)}) collective-permute-start(f32[21,8,128]{2,1,0:T(8,128)S(1)} %get-tuple-element.53), channel_id=1, source_target_pairs={{0,4},{2,6},{4,0},{6,2},{1,5},{3,7},{5,1},{7,3},{8,12},{10,14},{12... | collective-permute-start | bytes 258056 | tf_op jit(solution)/shard_map/slope_span/ppermute | solution.py:579
  42.6 2.0 %collective-permute-start.12 = (f32[21,8,128]{2,1,0:T(8,128)S(1)}, f32[21,8,128]{2,1,0:T(8,128)S(1)}, u32[]{:S(2)}, u32[]{:S(2)}) collective-permute-start(f32[21,8,128]{2,1,0:T(8,128)S(1)} %get-tuple-element.54), channel_id=1, source_target_pairs={{0,6},{2,0},{4,2},{6,4},{1,7},{3,1},{5,3},{7,5},{8,14},{10,8},{12,... | collective-permute-start | bytes 258056 | tf_op jit(solution)/shard_map/slope_span/ppermute | solution.py:579
  44.6 0.0 collective-permute-done.4.other1.other
  44.6 0.1 collective-permute-start.14
  44.7 1.9 %collective-permute-start.15 = (f32[22,8,128]{2,1,0:T(8,128)S(1)}, f32[22,8,128]{2,1,0:T(8,128)S(1)}, u32[]{:S(2)}, u32[]{:S(2)}) collective-permute-start(f32[22,8,128]{2,1,0:T(8,128)S(1)} %last_base.1.refs_0_), channel_id=1, source_target_pairs={{0,4},{2,6},{4,0},{6,2},{1,5},{3,7},{5,1},{7,3},{8,12},{10,14},{12... | collective-permute-start | bytes 270344 | tf_op jit(solution)/shard_map/base_spread/ppermute | solution.py:579
  46.6 1.9 %collective-permute-done.10.refs_5_ = f32[21,8,128]{2,1,0:T(8,128)S(1)} collective-permute-done((f32[21,8,128]{2,1,0:T(8,128)S(1)}, f32[21,8,128]{2,1,0:T(8,128)S(1)}, u32[]{:S(2)}, u32[]{:S(2)}) %collective-permute-start.10) | collective-permute-done | bytes 86048 | tf_op jit(solution)/shard_map/slope_span/ppermute | solution.py:579
  48.5 0.1 collective-permute-start.16
  48.6 0.3 span_slope.1.mine2
  48.9 1.7 %collective-permute-start.13 = (f32[21,8,128]{2,1,0:T(8,128)S(1)}, f32[21,8,128]{2,1,0:T(8,128)S(1)}, u32[]{:S(2)}, u32[]{:S(2)}) collective-permute-start(f32[21,8,128]{2,1,0:T(8,128)S(1)} %span_slope.1.mine2), channel_id=1, source_target_pairs={{0,8},{8,0},{1,9},{9,1},{2,10},{10,2},{3,11},{11,3},{4,12},{12,4},... | collective-permute-start | bytes 258056 | tf_op jit(solution)/shard_map/slope_x/ppermute | solution.py:579
  50.6 3.2 %collective-permute-done.13.other2 = f32[21,8,128]{2,1,0:T(8,128)S(1)} collective-permute-done((f32[21,8,128]{2,1,0:T(8,128)S(1)}, f32[21,8,128]{2,1,0:T(8,128)S(1)}, u32[]{:S(2)}, u32[]{:S(2)}) %collective-permute-start.13) | collective-permute-done | bytes 86048 | tf_op jit(solution)/shard_map/slope_x/ppermute | solution.py:579
  53.8 0.2 last_slope.1.after.refs_2_
  54.0 0.1 gather.1.refs_0_
  54.1 3.3 %collective-permute-start.17 = (f32[22,32,128]{2,1,0:T(8,128)S(1)}, f32[22,32,128]{2,1,0:T(8,128)S(1)}, u32[]{:S(2)}, u32[]{:S(2)}) collective-permute-start(f32[22,32,128]{2,1,0:T(8,128)S(1)} %gather.1.refs_0_), channel_id=1, source_target_pairs={{0,1},{1,0},{2,3},{3,2},{4,5},{5,4},{6,7},{7,6},{8,9},{9,8},{10,11... | collective-permute-start | bytes 1081352 | tf_op jit(solution)/shard_map/base_spread/ppermute | solution.py:579
  57.3 1.0 %collective-permute-start.18 = (f32[18,8,128]{2,1,0:T(8,128)S(1)}, f32[18,8,128]{2,1,0:T(8,128)S(1)}, u32[]{:S(2)}, u32[]{:S(2)}) collective-permute-start(f32[18,8,128]{2,1,0:T(8,128)S(1)} %last_slope.1.after.refs_2_), channel_id=1, source_target_pairs={{0,2},{2,4},{4,6},{6,0},{1,3},{3,5},{5,7},{7,1},{8,10},{10,12},{12... | collective-permute-start | bytes 221192 | tf_op jit(solution)/shard_map/slope_spread/ppermute | solution.py:579
  58.4 2.1 %collective-permute-start.19 = (f32[18,8,128]{2,1,0:T(8,128)S(1)}, f32[18,8,128]{2,1,0:T(8,128)S(1)}, u32[]{:S(2)}, u32[]{:S(2)}) collective-permute-start(f32[18,8,128]{2,1,0:T(8,128)S(1)} %last_slope.1.after.refs_2_), channel_id=1, source_target_pairs={{0,4},{2,6},{4,0},{6,2},{1,5},{3,7},{5,1},{7,3},{8,12},{10,14},{12... | collective-permute-start | bytes 221192 | tf_op jit(solution)/shard_map/slope_spread/ppermute | solution.py:579
  60.5 0.3 collective-permute-start.20
  60.8 0.8 %collective-permute-start.21 = (f32[18,8,128]{2,1,0:T(8,128)S(1)}, f32[18,8,128]{2,1,0:T(8,128)S(1)}, u32[]{:S(2)}, u32[]{:S(2)}) collective-permute-start(f32[18,8,128]{2,1,0:T(8,128)S(1)} %last_slope.1.after.refs_2_), channel_id=1, source_target_pairs={{0,1},{1,0},{2,3},{3,2},{4,5},{5,4},{6,7},{7,6},{8,9},{9,8},{10,11... | collective-permute-start | bytes 221192 | tf_op jit(solution)/shard_map/slope_spread/ppermute | solution.py:579
  61.5 0.9 %collective-permute-done.18.refs_3_ = f32[18,8,128]{2,1,0:T(8,128)S(1)} collective-permute-done((f32[18,8,128]{2,1,0:T(8,128)S(1)}, f32[18,8,128]{2,1,0:T(8,128)S(1)}, u32[]{:S(2)}, u32[]{:S(2)}) %collective-permute-start.18) | collective-permute-done | bytes 73760 | tf_op jit(solution)/shard_map/slope_spread/ppermute | solution.py:579
  62.4 0.9 %collective-permute-start.22 = (f32[18,8,128]{2,1,0:T(8,128)S(1)}, f32[18,8,128]{2,1,0:T(8,128)S(1)}, u32[]{:S(2)}, u32[]{:S(2)}) collective-permute-start(f32[18,8,128]{2,1,0:T(8,128)S(1)} %collective-permute-done.18.refs_3_), channel_id=1, source_target_pairs={{0,1},{1,0},{2,3},{3,2},{4,5},{5,4},{6,7},{7,6},{8,9},{9,8},{10,11... | collective-permute-start | bytes 221192 | tf_op jit(solution)/shard_map/slope_spread/ppermute | solution.py:579
  63.2 1.2 %collective-permute-done.19.refs_4_ = f32[18,8,128]{2,1,0:T(8,128)S(1)} collective-permute-done((f32[18,8,128]{2,1,0:T(8,128)S(1)}, f32[18,8,128]{2,1,0:T(8,128)S(1)}, u32[]{:S(2)}, u32[]{:S(2)}) %collective-permute-start.19) | collective-permute-done | bytes 73760 | tf_op jit(solution)/shard_map/slope_spread/ppermute | solution.py:579
  64.4 0.9 %collective-permute-start.23 = (f32[18,8,128]{2,1,0:T(8,128)S(1)}, f32[18,8,128]{2,1,0:T(8,128)S(1)}, u32[]{:S(2)}, u32[]{:S(2)}) collective-permute-start(f32[18,8,128]{2,1,0:T(8,128)S(1)} %collective-permute-done.19.refs_4_), channel_id=1, source_target_pairs={{0,1},{1,0},{2,3},{3,2},{4,5},{5,4},{6,7},{7,6},{8,9},{9,8},{10,11... | collective-permute-start | bytes 221192 | tf_op jit(solution)/shard_map/slope_spread/ppermute | solution.py:579
  65.3 0.2 collective-permute-start.24
  65.5 0.7 %collective-permute-done.23.refs_8_ = f32[18,8,128]{2,1,0:T(8,128)S(1)} collective-permute-done((f32[18,8,128]{2,1,0:T(8,128)S(1)}, f32[18,8,128]{2,1,0:T(8,128)S(1)}, u32[]{:S(2)}, u32[]{:S(2)}) %collective-permute-start.23) | collective-permute-done | bytes 73760 | tf_op jit(solution)/shard_map/slope_spread/ppermute | solution.py:579
  66.2 0.4 collective-permute-done.24.refs_9_
  66.6 1.1 %place.1 = f32[40,64,128]{2,1,0:T(8,128)} custom-call(f32[22,32,128]{2,1,0:T(8,128)S(1)} %gather.1.refs_0_, f32[22,32,128]{2,1,0:T(8,128)S(1)} %collective-permute-done.17.refs_1_, f32[18,8,128]{2,1,0:T(8,128)S(1)} %last_slope.1.after.refs_2_, f32[18,8,128]{2,1,0:T(8,128)S(1)} %collective-permute-done.18.refs_3_, ...), custom_call_target="tpu_custom_call" | custom-call | tf_op jit(solution)/shard_map/place/pallas_call | solution.py:552
  (19 shorter events, 0.1 us)
Async XLA Ops:
  0.0 10.1 %copy-start = (f32[4,64,64,128]{3,2,1,0:T(8,128)S(1)}, f32[4,64,64,128]{3,2,1,0:T(8,128)}, u32[]{:S(2)}) copy-start(f32[4,64,64,128]{3,2,1,0:T(8,128)} %flow.1) | copy-start | bytes 25165828
  0.0 19.8 %copy-start.1 = (f32[128,128]{1,0:T(8,128)S(1)}, f32[128,128]{1,0:T(8,128)}, u32[]{:S(2)}) copy-start(f32[128,128]{1,0:T(8,128)} %dy.1) | copy-start | bytes 196612
  1.7 21.4 %collective-permute-start.5 = (f32[3,64,4,128]{3,2,1,0:T(4,128)S(1)}, f32[3,64,4,128]{3,2,1,0:T(4,128)S(1)}, u32[]{:S(2)}, u32[]{:S(2)}) collective-permute-start(f32[3,64,4,128]{3,2,1,0:T(4,128)S(1)} %get-tuple-element.40), channel_id=1, source_target_pairs={{0,1},{1,2},{2,3},{3,4},{4,5},{5,6},{6,7},{7,8},{8,9},{9,10},{10,1... | collective-permute-start | bytes 1179656 | tf_op jit(solution)/shard_map/rim_exchange/ppermute | solution.py:579
  3.9 19.7 %collective-permute-start.6 = (f32[3,64,4,128]{3,2,1,0:T(4,128)S(1)}, f32[3,64,4,128]{3,2,1,0:T(4,128)S(1)}, u32[]{:S(2)}, u32[]{:S(2)}) collective-permute-start(f32[3,64,4,128]{3,2,1,0:T(4,128)S(1)} %get-tuple-element.41), channel_id=1, source_target_pairs={{0,15},{1,0},{2,1},{3,2},{4,3},{5,4},{6,5},{7,6},{8,7},{9,8},{10,9... | collective-permute-start | bytes 1179656 | tf_op jit(solution)/shard_map/rim_exchange/ppermute | solution.py:579
  3.9 31.4 %collective-permute-start.7 = (f32[4,4,64,128]{3,2,1,0:T(8,128)S(1)}, f32[4,4,64,128]{3,2,1,0:T(8,128)S(1)}, u32[]{:S(2)}, u32[]{:S(2)}) collective-permute-start(f32[4,4,64,128]{3,2,1,0:T(8,128)S(1)} %get-tuple-element.46), channel_id=1, source_target_pairs={{0,16},{16,32},{32,48},{48,64},{64,80},{80,96},{96,112},{1,17},{17... | collective-permute-start | bytes 1572872 | tf_op jit(solution)/shard_map/rim_exchange/ppermute | solution.py:593
  7.0 28.3 %collective-permute-start.8 = (f32[4,4,64,128]{3,2,1,0:T(8,128)S(1)}, f32[4,4,64,128]{3,2,1,0:T(8,128)S(1)}, u32[]{:S(2)}, u32[]{:S(2)}) collective-permute-start(f32[4,4,64,128]{3,2,1,0:T(8,128)S(1)} %get-tuple-element.47), channel_id=1, source_target_pairs={{16,0},{32,16},{48,32},{64,48},{80,64},{96,80},{112,96},{17,1},{33... | collective-permute-start | bytes 1572872 | tf_op jit(solution)/shard_map/rim_exchange/ppermute | solution.py:594
  14.7 8.1 %collective-permute-start = (f32[23,32,128]{2,1,0:T(8,128)S(1)}, f32[23,32,128]{2,1,0:T(8,128)S(1)}, u32[]{:S(2)}, u32[]{:S(2)}) collective-permute-start(f32[23,32,128]{2,1,0:T(8,128)S(1)} %get-tuple-element.32), channel_id=1, source_target_pairs={{0,1},{1,0},{2,3},{3,2},{4,5},{5,4},{6,7},{7,6},{8,9},{9,8},{10,11... | collective-permute-start | bytes 1130504 | tf_op jit(solution)/shard_map/base_core/ppermute | solution.py:579
  22.9 12.3 %collective-permute-start.1 = (f32[23,8,128]{2,1,0:T(8,128)S(1)}, f32[23,8,128]{2,1,0:T(8,128)S(1)}, u32[]{:S(2)}, u32[]{:S(2)}) collective-permute-start(f32[23,8,128]{2,1,0:T(8,128)S(1)} %get-tuple-element.34), channel_id=1, source_target_pairs={{0,2},{2,4},{4,6},{6,0},{1,3},{3,5},{5,7},{7,1},{8,10},{10,12},{12... | collective-permute-start | bytes 282632 | tf_op jit(solution)/shard_map/base_span/ppermute | solution.py:579
  23.0 12.2 %collective-permute-start.2 = (f32[23,8,128]{2,1,0:T(8,128)S(1)}, f32[23,8,128]{2,1,0:T(8,128)S(1)}, u32[]{:S(2)}, u32[]{:S(2)}) collective-permute-start(f32[23,8,128]{2,1,0:T(8,128)S(1)} %get-tuple-element.35), channel_id=1, source_target_pairs={{0,4},{2,6},{4,0},{6,2},{1,5},{3,7},{5,1},{7,3},{8,12},{10,14},{12... | collective-permute-start | bytes 282632 | tf_op jit(solution)/shard_map/base_span/ppermute | solution.py:579
  23.7 11.5 %collective-permute-start.3 = (f32[23,8,128]{2,1,0:T(8,128)S(1)}, f32[23,8,128]{2,1,0:T(8,128)S(1)}, u32[]{:S(2)}, u32[]{:S(2)}) collective-permute-start(f32[23,8,128]{2,1,0:T(8,128)S(1)} %get-tuple-element.36), channel_id=1, source_target_pairs={{0,6},{2,0},{4,2},{6,4},{1,7},{3,1},{5,3},{7,5},{8,14},{10,8},{12,... | collective-permute-start | bytes 282632 | tf_op jit(solution)/shard_map/base_span/ppermute | solution.py:579
  36.9 4.1 %collective-permute-start.9 = (f32[21,32,128]{2,1,0:T(8,128)S(1)}, f32[21,32,128]{2,1,0:T(8,128)S(1)}, u32[]{:S(2)}, u32[]{:S(2)}) collective-permute-start(f32[21,32,128]{2,1,0:T(8,128)S(1)} %get-tuple-element.49), channel_id=1, source_target_pairs={{0,1},{1,0},{2,3},{3,2},{4,5},{5,4},{6,7},{7,6},{8,9},{9,8},{10,11... | collective-permute-start | bytes 1032200 | tf_op jit(solution)/shard_map/slope_core/ppermute | solution.py:579
  38.3 6.3 %collective-permute-start.4 = (f32[23,8,128]{2,1,0:T(8,128)S(1)}, f32[23,8,128]{2,1,0:T(8,128)S(1)}, u32[]{:S(2)}, u32[]{:S(2)}) collective-permute-start(f32[23,8,128]{2,1,0:T(8,128)S(1)} %get-tuple-element.37.after.mine1.mine), channel_id=1, source_target_pairs={{0,8},{8,0},{1,9},{9,1},{2,10},{10,2},{3,11},{11,3},{4,12},{12,4},... | collective-permute-start | bytes 282632 | tf_op jit(solution)/shard_map/base_x/ppermute | solution.py:579
  41.3 7.2 %collective-permute-start.10 = (f32[21,8,128]{2,1,0:T(8,128)S(1)}, f32[21,8,128]{2,1,0:T(8,128)S(1)}, u32[]{:S(2)}, u32[]{:S(2)}) collective-permute-start(f32[21,8,128]{2,1,0:T(8,128)S(1)} %get-tuple-element.52), channel_id=1, source_target_pairs={{0,2},{2,4},{4,6},{6,0},{1,3},{3,5},{5,7},{7,1},{8,10},{10,12},{12... | collective-permute-start | bytes 258056 | tf_op jit(solution)/shard_map/slope_span/ppermute | solution.py:579
  41.4 7.2 %collective-permute-start.11 = (f32[21,8,128]{2,1,0:T(8,128)S(1)}, f32[21,8,128]{2,1,0:T(8,128)S(1)}, u32[]{:S(2)}, u32[]{:S(2)}) collective-permute-start(f32[21,8,128]{2,1,0:T(8,128)S(1)} %get-tuple-element.53), channel_id=1, source_target_pairs={{0,4},{2,6},{4,0},{6,2},{1,5},{3,7},{5,1},{7,3},{8,12},{10,14},{12... | collective-permute-start | bytes 258056 | tf_op jit(solution)/shard_map/slope_span/ppermute | solution.py:579
  42.6 5.9 %collective-permute-start.12 = (f32[21,8,128]{2,1,0:T(8,128)S(1)}, f32[21,8,128]{2,1,0:T(8,128)S(1)}, u32[]{:S(2)}, u32[]{:S(2)}) collective-permute-start(f32[21,8,128]{2,1,0:T(8,128)S(1)} %get-tuple-element.54), channel_id=1, source_target_pairs={{0,6},{2,0},{4,2},{6,4},{1,7},{3,1},{5,3},{7,5},{8,14},{10,8},{12,... | collective-permute-start | bytes 258056 | tf_op jit(solution)/shard_map/slope_span/ppermute | solution.py:579
  44.6 9.3 %collective-permute-start.14 = (f32[22,8,128]{2,1,0:T(8,128)S(1)}, f32[22,8,128]{2,1,0:T(8,128)S(1)}, u32[]{:S(2)}, u32[]{:S(2)}) collective-permute-start(f32[22,8,128]{2,1,0:T(8,128)S(1)} %last_base.1.refs_0_), channel_id=1, source_target_pairs={{0,2},{2,4},{4,6},{6,0},{1,3},{3,5},{5,7},{7,1},{8,10},{10,12},{12... | collective-permute-start | bytes 270344 | tf_op jit(solution)/shard_map/base_spread/ppermute | solution.py:579
  44.7 9.2 %collective-permute-start.15 = (f32[22,8,128]{2,1,0:T(8,128)S(1)}, f32[22,8,128]{2,1,0:T(8,128)S(1)}, u32[]{:S(2)}, u32[]{:S(2)}) collective-permute-start(f32[22,8,128]{2,1,0:T(8,128)S(1)} %last_base.1.refs_0_), channel_id=1, source_target_pairs={{0,4},{2,6},{4,0},{6,2},{1,5},{3,7},{5,1},{7,3},{8,12},{10,14},{12... | collective-permute-start | bytes 270344 | tf_op jit(solution)/shard_map/base_spread/ppermute | solution.py:579
  48.5 5.5 %collective-permute-start.16 = (f32[22,8,128]{2,1,0:T(8,128)S(1)}, f32[22,8,128]{2,1,0:T(8,128)S(1)}, u32[]{:S(2)}, u32[]{:S(2)}) collective-permute-start(f32[22,8,128]{2,1,0:T(8,128)S(1)} %last_base.1.refs_0_), channel_id=1, source_target_pairs={{0,6},{2,0},{4,2},{6,4},{1,7},{3,1},{5,3},{7,5},{8,14},{10,8},{12,... | collective-permute-start | bytes 270344 | tf_op jit(solution)/shard_map/base_spread/ppermute | solution.py:579
  48.9 4.9 %collective-permute-start.13 = (f32[21,8,128]{2,1,0:T(8,128)S(1)}, f32[21,8,128]{2,1,0:T(8,128)S(1)}, u32[]{:S(2)}, u32[]{:S(2)}) collective-permute-start(f32[21,8,128]{2,1,0:T(8,128)S(1)} %span_slope.1.mine2), channel_id=1, source_target_pairs={{0,8},{8,0},{1,9},{9,1},{2,10},{10,2},{3,11},{11,3},{4,12},{12,4},... | collective-permute-start | bytes 258056 | tf_op jit(solution)/shard_map/slope_x/ppermute | solution.py:579
  54.1 12.5 %collective-permute-start.17 = (f32[22,32,128]{2,1,0:T(8,128)S(1)}, f32[22,32,128]{2,1,0:T(8,128)S(1)}, u32[]{:S(2)}, u32[]{:S(2)}) collective-permute-start(f32[22,32,128]{2,1,0:T(8,128)S(1)} %gather.1.refs_0_), channel_id=1, source_target_pairs={{0,1},{1,0},{2,3},{3,2},{4,5},{5,4},{6,7},{7,6},{8,9},{9,8},{10,11... | collective-permute-start | bytes 1081352 | tf_op jit(solution)/shard_map/base_spread/ppermute | solution.py:579
  57.3 5.0 %collective-permute-start.18 = (f32[18,8,128]{2,1,0:T(8,128)S(1)}, f32[18,8,128]{2,1,0:T(8,128)S(1)}, u32[]{:S(2)}, u32[]{:S(2)}) collective-permute-start(f32[18,8,128]{2,1,0:T(8,128)S(1)} %last_slope.1.after.refs_2_), channel_id=1, source_target_pairs={{0,2},{2,4},{4,6},{6,0},{1,3},{3,5},{5,7},{7,1},{8,10},{10,12},{12... | collective-permute-start | bytes 221192 | tf_op jit(solution)/shard_map/slope_spread/ppermute | solution.py:579
  58.4 6.1 %collective-permute-start.19 = (f32[18,8,128]{2,1,0:T(8,128)S(1)}, f32[18,8,128]{2,1,0:T(8,128)S(1)}, u32[]{:S(2)}, u32[]{:S(2)}) collective-permute-start(f32[18,8,128]{2,1,0:T(8,128)S(1)} %last_slope.1.after.refs_2_), channel_id=1, source_target_pairs={{0,4},{2,6},{4,0},{6,2},{1,5},{3,7},{5,1},{7,3},{8,12},{10,14},{12... | collective-permute-start | bytes 221192 | tf_op jit(solution)/shard_map/slope_spread/ppermute | solution.py:579
  60.5 4.8 %collective-permute-start.20 = (f32[18,8,128]{2,1,0:T(8,128)S(1)}, f32[18,8,128]{2,1,0:T(8,128)S(1)}, u32[]{:S(2)}, u32[]{:S(2)}) collective-permute-start(f32[18,8,128]{2,1,0:T(8,128)S(1)} %last_slope.1.after.refs_2_), channel_id=1, source_target_pairs={{0,6},{2,0},{4,2},{6,4},{1,7},{3,1},{5,3},{7,5},{8,14},{10,8},{12,... | collective-permute-start | bytes 221192 | tf_op jit(solution)/shard_map/slope_spread/ppermute | solution.py:579
  60.8 4.7 %collective-permute-start.21 = (f32[18,8,128]{2,1,0:T(8,128)S(1)}, f32[18,8,128]{2,1,0:T(8,128)S(1)}, u32[]{:S(2)}, u32[]{:S(2)}) collective-permute-start(f32[18,8,128]{2,1,0:T(8,128)S(1)} %last_slope.1.after.refs_2_), channel_id=1, source_target_pairs={{0,1},{1,0},{2,3},{3,2},{4,5},{5,4},{6,7},{7,6},{8,9},{9,8},{10,11... | collective-permute-start | bytes 221192 | tf_op jit(solution)/shard_map/slope_spread/ppermute | solution.py:579
  62.4 3.1 %collective-permute-start.22 = (f32[18,8,128]{2,1,0:T(8,128)S(1)}, f32[18,8,128]{2,1,0:T(8,128)S(1)}, u32[]{:S(2)}, u32[]{:S(2)}) collective-permute-start(f32[18,8,128]{2,1,0:T(8,128)S(1)} %collective-permute-done.18.refs_3_), channel_id=1, source_target_pairs={{0,1},{1,0},{2,3},{3,2},{4,5},{5,4},{6,7},{7,6},{8,9},{9,8},{10,11... | collective-permute-start | bytes 221192 | tf_op jit(solution)/shard_map/slope_spread/ppermute | solution.py:579
  64.4 1.8 %collective-permute-start.23 = (f32[18,8,128]{2,1,0:T(8,128)S(1)}, f32[18,8,128]{2,1,0:T(8,128)S(1)}, u32[]{:S(2)}, u32[]{:S(2)}) collective-permute-start(f32[18,8,128]{2,1,0:T(8,128)S(1)} %collective-permute-done.19.refs_4_), channel_id=1, source_target_pairs={{0,1},{1,0},{2,3},{3,2},{4,5},{5,4},{6,7},{7,6},{8,9},{9,8},{10,11... | collective-permute-start | bytes 221192 | tf_op jit(solution)/shard_map/slope_spread/ppermute | solution.py:579
  65.3 1.3 %collective-permute-start.24 = (f32[18,8,128]{2,1,0:T(8,128)S(1)}, f32[18,8,128]{2,1,0:T(8,128)S(1)}, u32[]{:S(2)}, u32[]{:S(2)}) collective-permute-start(f32[18,8,128]{2,1,0:T(8,128)S(1)} %collective-permute-done.20.refs_5_), channel_id=1, source_target_pairs={{0,1},{1,0},{2,3},{3,2},{4,5},{5,4},{6,7},{7,6},{8,9},{9,8},{10,11... | collective-permute-start | bytes 221192 | tf_op jit(solution)/shard_map/slope_spread/ppermute | solution.py:579

commit v6 on v5

--- a/solution.py
+++ b/solution.py
@@ -234,55 +234,73 @@
     return out
 
 
-def slope_row(pad, ysl, x):
+def slope_row(pad, ysl, x, with_x=True, rest=True):
     lz, ny = ysl.shape[2:]
     total = [None] * NSLOPE
-    row = lax.broadcasted_iota(jnp.int32, (8, ny), 0)
-    row = jnp.minimum(row, 7 - row)
-    weight = jnp.full((8, ny), sum(ratios), F32)
-    for k in range(3):
-        weight = jnp.where(row == k, sum(ratios[3 - k :]), weight)
-    for c in range(3):
-        total[c] = weight * (
-            pad[c, x + 4, pl.ds(4 + lz, 8), :] - pad[c, x + 4, pl.ds(4, 8), :]
-        )
 
     def add(k, v):
         total[k] = v if total[k] is None else total[k] + v
 
+    if rest:
+        row = lax.broadcasted_iota(jnp.int32, (8, ny), 0)
+        row = jnp.minimum(row, 7 - row)
+        weight = jnp.full((8, ny), sum(ratios), F32)
+        for k in range(3):
+            weight = jnp.where(row == k, sum(ratios[3 - k :]), weight)
+        for c in range(3):
+            total[c] = weight * (
+                pad[c, x + 4, pl.ds(4 + lz, 8), :] - pad[c, x + 4, pl.ds(4, 8), :]
+            )
     for b in range(lz // 8):
         at = 8 + 8 * b
         u = [pad[c, x + 4, pl.ds(at, 8), :] for c in range(4)]
         p = u[3]
         g = [[None] * 3 for _ in range(4)]
-        for c in range(4):
-            g[c][0] = difference(
-                lambda k: pad[c, x + 5 + k, pl.ds(at, 8), :],
-                lambda k: pad[c, x + 3 - k, pl.ds(at, 8), :],
-            )
-            g[c][1] = ysl[c, x, pl.ds(8 * b, 8), :]
-        for c in range(3):
-            g[c][2] = difference(
-                lambda k: pad[c, x + 4, pl.ds(at + 1 + k, 8), :],
-                lambda k: pad[c, x + 4, pl.ds(at - 1 - k, 8), :],
-            )
-        add(3, p * g[0][0])
-        add(4, p * (g[0][1] + g[1][0]))
-        add(5, p * g[0][2])
-        add(6, p * g[2][0])
-        add(7, p * g[1][1])
-        add(8, p * g[1][2])
-        add(9, p * g[2][1])
-        add(10, p * g[2][2])
+        if with_x:
+            for c in range(4):
+                g[c][0] = difference(
+                    lambda k: pad[c, x + 5 + k, pl.ds(at, 8), :],
+                    lambda k: pad[c, x + 3 - k, pl.ds(at, 8), :],
+                )
+        if rest:
+            for c in range(4):
+                g[c][1] = ysl[c, x, pl.ds(8 * b, 8), :]
+            for c in range(3):
+                g[c][2] = difference(
+                    lambda k: pad[c, x + 4, pl.ds(at + 1 + k, 8), :],
+                    lambda k: pad[c, x + 4, pl.ds(at - 1 - k, 8), :],
+                )
+        if with_x:
+            add(3, p * g[0][0])
+            add(6, p * g[2][0])
+            add(17, u[0] * g[3][0])
+            add(20, u[2] * g[3][0])
+        if with_x and rest:
+            add(4, p * (g[0][1] + g[1][0]))
+            add(18, u[0] * g[3][1] + u[1] * g[3][0])
+        elif with_x:
+            add(4, p * g[1][0])
+            add(18, u[1] * g[3][0])
+        else:
+            add(4, p * g[0][1])
+            add(18, u[0] * g[3][1])
+        if rest:
+            add(5, p * g[0][2])
+            add(7, p * g[1][1])
+            add(8, p * g[1][2])
+            add(9, p * g[2][1])
+            add(10, p * g[2][2])
+            add(19, u[1] * g[3][1])
+            add(21, u[2] * g[3][1])
+        dims = ((0,) if with_x else ()) + ((1, 2) if rest else ())
         for k, (i, j) in enumerate(pairs):
-            for dim in range(3):
+            for dim in dims:
                 add(11 + k, g[i][dim] * g[j][dim])
-        add(17, u[0] * g[3][0])
-        add(18, u[0] * g[3][1] + u[1] * g[3][0])
-        add(19, u[1] * g[3][1])
-        add(20, u[2] * g[3][0])
-        add(21, u[2] * g[3][1])
     return total
+
+
+def end_row(i, lx):
+    return jnp.where(i < 4, i, lx - 8 + i)
 
 
 def slope_fields(total, pressure):
@@ -323,6 +341,16 @@
         return 0
 
     lax.fori_loop(4, lx - 4, one, 0, unroll=4)
+
+    def end(i, _):
+        x = end_row(i, lx)
+        total = slope_row(pad, ysl, x, with_x=False)
+        for k in range(NSLOPE):
+            v = jnp.zeros((8, ny), F32) if total[k] is None else total[k]
+            acc[pl.ds(pl.multiple_of(k * 8 * lx + 8 * x, 8), 8), :] = v
+        return 0
+
+    lax.fori_loop(0, 8, end, 0, unroll=4)
 
     for out, side in ((send, 1 - core), (keep, core)):
         at = pl.multiple_of(half * side, 8)
@@ -381,28 +409,32 @@
             out[DXM - FIRST + c] = dxm[c, pl.ds(pl.multiple_of(half * side, 8), half), :]
 
     def one(i, _):
-        x = jnp.where(i < 4, i, lx - 8 + i)
-        total = slope_row(pad, ysl, x)
-        for k in range(NSLOPE):
+        total = slope_row(pad, ysl, end_row(i, lx), rest=False)
+        for k in used:
             acc[pl.ds(pl.multiple_of(k * 64 + 8 * i, 8), 8), :] = total[k]
         return 0
 
+    used = (3, 4, 6, 11, 12, 13, 14, 15, 16, 17, 18, 20)
     lax.fori_loop(0, 8, one, 0, unroll=4)
 
-    pressure = jnp.concatenate([mean[3, pl.ds(0, 4), :], mean[3, pl.ds(lx - 4, 4), :]], axis=0)
-    fields = list(slope_fields(lambda k: row_sum(k, 8, acc), pressure))
+    def total(k):
+        return row_sum(k, 8, acc)
+
+    fields = [(PG + 0, 2.0 * total(3)), (PG + 1, total(4)), (PG + 2, total(6))]
+    fields += [(GG + k, total(11 + k)) for k in range(6)]
+    fields += [(UG + 0, -2.0 * total(17)), (UG + 1, -total(18)), (UG + 2, -total(20))]
     for side, rows in ((0, slice(0, 4)), (1, slice(4, 8))):
-        at = 0 if side == 0 else half - 4
+        at = pl.ds(0 if side == 0 else half - 4, 4)
 
         @pl.when(core == side)
         def _():
             for f, v in fields:
-                keep[f - FIRST, pl.ds(at, 4), :] = v[rows]
+                keep[f - FIRST, at, :] = keep[f - FIRST, at, :] + v[rows]
 
         @pl.when(core != side)
         def _():
             for f, v in fields:
-                send[f - FIRST, pl.ds(at, 4), :] = v[rows]
+                send[f - FIRST, at, :] = send[f - FIRST, at, :] + v[rows]
 
 
 def edge_moments(pad, keep, send, ysl, xl, xr, mean, after):

time: 68.6 us -> 67.9 us (0.990)
  waiting for transfers between devices: 8.31 us -> 6.1 us
  starting transfers between devices: 36.9 us -> 38.2 us
    ppermute x23, waiting for transfers between devices: 8.3 us -> 6.09 us  [send(): lax.ppermute(value, axis, [(i, (i + step) % size) for i in range(size)])]
    ppermute x23, starting transfers between devices: 30.7 us -> 32.1 us  [send(): lax.ppermute(value, axis, [(i, (i + step) % size) for i in range(size)])]
    pallas_call x1, Pallas kernels: 1.6 us -> 0.89 us  [edge_moments(): pl.pallas_call(edge_kernel, in_specs=[vm] * 7 + [pl.BlockSpec(memory_spac...]
  transfers between devices with their start and end apart: 25 -> 25, of which waited for: 6 -> 6; matrix products, arithmetic and copies ran while one was open for 0% -> 0% of each run, Pallas kernels for 26% -> 28%
where the time goes in v6:
time: 67.9 us; the launch traced here: 66.8 us
  starting transfers between devices  38.2 us (56%)
  Pallas kernels  22.2 us (33%)
  waiting for transfers between devices  6.1 us (9%)
    ppermute x23, starting transfers between devices, send(): lax.ppermute(value, axis, [(i, (i + step) % size) for i in range(size)])  32.1 us
    pallas_call x1, Pallas kernels, inner_moments(): pl.pallas_call(inner_kernel, in_specs=[vm] * 5 + [pl.BlockSpec(memory_spa...  10.1 us
    ppermute x23, waiting for transfers between devices, send(): lax.ppermute(value, axis, [(i, (i + step) % size) for i in range(size)])  6.09 us
    pallas_call x1, Pallas kernels, base_moments(): pl.pallas_call(base_kernel, in_specs=[vm], out_specs=[vm] * 4, out_shape=...  4.54 us
    ppermute x1, starting transfers between devices, shards(): xl = lax.ppermute(xl, GXA, up)  3.11 us
    ppermute x1, starting transfers between devices, shards(): xr = lax.ppermute(xr, GXA, down)  3.06 us
    pallas_call x1, Pallas kernels, y_slopes(): pl.pallas_call(y_kernel, in_specs=[vm, vm], out_specs=[vm, vm], out_shape...  2.98 us
    pallas_call x1, Pallas kernels, cut(): pl.pallas_call(kernel, in_specs=[pl.BlockSpec(memory_space=pltpu.HBM)] +...  1.64 us
  transfers between devices with their start and end apart: 25, of which 6 were waited for; matrix products, arithmetic and copies ran while one was open for 0% of the time, Pallas kernels for 28%

profile of v6, /device:TPU:9, one launch (start us, length us, event | category | flops | bytes accessed | tf_op | source)
XLA Modules:
  0.0 66.8 jit_solution(166226425356553650)
XLA Ops:
  0.0 1.6 %rims.1 = (f32[3,64,4,128]{3,2,1,0:T(4,128)S(1)}, f32[3,64,4,128]{3,2,1,0:T(4,128)S(1)}, f32[4,4,64,128]{3,2,1,0:T(8,128)S(1)}, f32[4,4,64,128]{3,2,1,0:T(8,128)S(1)}) custom-call(f32[4,64,64,128]{3,2,1,0:T(8,128)} %flow.1), custom_call_target="tpu_custom_call" | custom-call | tf_op jit(solution)/shard_map/rims/pallas_call | solution.py:101
  1.7 2.3 %collective-permute-start.5 = (f32[3,64,4,128]{3,2,1,0:T(4,128)S(1)}, f32[3,64,4,128]{3,2,1,0:T(4,128)S(1)}, u32[]{:S(2)}, u32[]{:S(2)}) collective-permute-start(f32[3,64,4,128]{3,2,1,0:T(4,128)S(1)} %get-tuple-element.40), channel_id=1, source_target_pairs={{0,1},{1,2},{2,3},{3,4},{4,5},{5,6},{6,7},{7,8},{8,9},{9,10},{10,1... | collective-permute-start | bytes 1179656 | tf_op jit(solution)/shard_map/rim_exchange/ppermute | solution.py:611
  3.9 3.1 %collective-permute-start.7 = (f32[4,4,64,128]{3,2,1,0:T(8,128)S(1)}, f32[4,4,64,128]{3,2,1,0:T(8,128)S(1)}, u32[]{:S(2)}, u32[]{:S(2)}) collective-permute-start(f32[4,4,64,128]{3,2,1,0:T(8,128)S(1)} %get-tuple-element.46), channel_id=1, source_target_pairs={{0,16},{16,32},{32,48},{48,64},{64,80},{80,96},{96,112},{1,17},{17... | collective-permute-start | bytes 1572872 | tf_op jit(solution)/shard_map/rim_exchange/ppermute | solution.py:625
  7.0 3.1 %collective-permute-start.8 = (f32[4,4,64,128]{3,2,1,0:T(8,128)S(1)}, f32[4,4,64,128]{3,2,1,0:T(8,128)S(1)}, u32[]{:S(2)}, u32[]{:S(2)}) collective-permute-start(f32[4,4,64,128]{3,2,1,0:T(8,128)S(1)} %get-tuple-element.47), channel_id=1, source_target_pairs={{16,0},{32,16},{48,32},{64,48},{80,64},{96,80},{112,96},{17,1},{33... | collective-permute-start | bytes 1572872 | tf_op jit(solution)/shard_map/rim_exchange/ppermute | solution.py:626
  10.1 4.5 %base_moments.1 = (f32[4,72,80,128]{3,2,1,0:T(8,128)S(1)}, f32[4,64,128]{2,1,0:T(8,128)S(1)}, f32[23,32,128]{2,1,0:T(8,128)S(1)}, f32[23,32,128]{2,1,0:T(8,128)S(1)}) custom-call(f32[4,64,64,128]{3,2,1,0:T(8,128)S(1)} %copy-done), custom_call_target="tpu_custom_call" | custom-call | flops 1000 | bytes 1000 | tf_op jit(solution)/shard_map/base_moments/pallas_call | solution.py:199
  14.7 5.1 %collective-permute-start = (f32[23,32,128]{2,1,0:T(8,128)S(1)}, f32[23,32,128]{2,1,0:T(8,128)S(1)}, u32[]{:S(2)}, u32[]{:S(2)}) collective-permute-start(f32[23,32,128]{2,1,0:T(8,128)S(1)} %get-tuple-element.32), channel_id=1, source_target_pairs={{0,1},{1,0},{2,3},{3,2},{4,5},{5,4},{6,7},{7,6},{8,9},{9,8},{10,11... | collective-permute-start | bytes 1130504 | tf_op jit(solution)/shard_map/base_core/ppermute | solution.py:611
  19.8 3.0 %y_slopes.1 = (f32[4,64,64,128]{3,2,1,0:T(8,128)S(1)}, f32[128,128]{1,0:T(8,128)S(1)}) custom-call(f32[4,72,80,128]{3,2,1,0:T(8,128)S(1)} %get-tuple-element.38.pad.pad_in, f32[128,128]{1,0:T(8,128)S(1)} %copy-done.1), custom_call_target="tpu_custom_call" | custom-call | flops 1000 | bytes 1000 | tf_op jit(solution)/shard_map/y_slopes/pallas_call | solution.py:217
  22.8 0.0 collective-permute-done.got.got1
  22.8 0.1 core_base.1
  22.9 0.1 collective-permute-start.1
  23.0 0.0 collective-permute-done.5.zl
  23.0 0.7 collective-permute-start.2
  23.7 2.1 %collective-permute-start.3 = (f32[23,8,128]{2,1,0:T(8,128)S(1)}, f32[23,8,128]{2,1,0:T(8,128)S(1)}, u32[]{:S(2)}, u32[]{:S(2)}) collective-permute-start(f32[23,8,128]{2,1,0:T(8,128)S(1)} %get-tuple-element.36), channel_id=1, source_target_pairs={{0,6},{2,0},{4,2},{6,4},{1,7},{3,1},{5,3},{7,5},{8,14},{10,8},{12,... | collective-permute-start | bytes 282632 | tf_op jit(solution)/shard_map/base_span/ppermute | solution.py:611
  25.8 10.1 %inner_moments.1 = (f32[4,72,80,128]{3,2,1,0:T(8,128)S(1)}, f32[21,32,128]{2,1,0:T(8,128)S(1)}, f32[21,32,128]{2,1,0:T(8,128)S(1)}) custom-call(f32[4,72,80,128]{3,2,1,0:T(8,128)S(1)} %get-tuple-element.38.pad.pad_in, f32[4,64,64,128]{3,2,1,0:T(8,128)S(1)} %get-tuple-element.39.ysl, ...), custom_call_target="tpu_custom_call", output_to_operand_aliasing={{0}: (0, {})} | custom-call | flops 1500000000 | bytes 84000000 | tf_op jit(solution)/shard_map/inner_moments/pallas_call | solution.py:369
  35.9 0.0 collective-permute-done.1.one.refs_1_
  35.9 0.0 collective-permute-done.3.three.refs_3_
  35.9 0.1 span_base.1
  36.0 0.0 collective-permute-done.7.xl
  36.0 0.0 collective-permute-done.8.xr
  36.0 0.9 %edge_moments.1 = (f32[4,72,80,128]{3,2,1,0:T(8,128)S(1)}, f32[21,32,128]{2,1,0:T(8,128)S(1)}, f32[21,32,128]{2,1,0:T(8,128)S(1)}) custom-call(f32[4,72,80,128]{3,2,1,0:T(8,128)S(1)} %get-tuple-element.43.pad_in, f32[21,32,128]{2,1,0:T(8,128)S(1)} %get-tuple-element.44.keep_in, ...), custom_call_target="tpu_custom_call", output_to_operand_aliasing={{0}: (0, {}), {1}: (1, {}), {2}: (2, {})} | custom-call | flops 52428800 | bytes 1048576 | tf_op jit(solution)/shard_map/edge_moments/pallas_call | solution.py:443
  36.9 0.7 %collective-permute-start.9 = (f32[21,32,128]{2,1,0:T(8,128)S(1)}, f32[21,32,128]{2,1,0:T(8,128)S(1)}, u32[]{:S(2)}, u32[]{:S(2)}) collective-permute-start(f32[21,32,128]{2,1,0:T(8,128)S(1)} %get-tuple-element.49), channel_id=1, source_target_pairs={{0,1},{1,0},{2,3},{3,2},{4,5},{5,4},{6,7},{7,6},{8,9},{9,8},{10,11... | collective-permute-start | bytes 1032200 | tf_op jit(solution)/shard_map/slope_core/ppermute | solution.py:611
  37.6 2.8 %collective-permute-start.4 = (f32[23,8,128]{2,1,0:T(8,128)S(1)}, f32[23,8,128]{2,1,0:T(8,128)S(1)}, u32[]{:S(2)}, u32[]{:S(2)}) collective-permute-start(f32[23,8,128]{2,1,0:T(8,128)S(1)} %get-tuple-element.37.after.mine1.mine), channel_id=1, source_target_pairs={{0,8},{8,0},{1,9},{9,1},{2,10},{10,2},{3,11},{11,3},{4,12},{12,4},... | collective-permute-start | bytes 282632 | tf_op jit(solution)/shard_map/base_x/ppermute | solution.py:611
  40.3 0.2 core_slope.1
  40.6 0.1 collective-permute-start.10
  40.7 1.9 %collective-permute-start.11 = (f32[21,8,128]{2,1,0:T(8,128)S(1)}, f32[21,8,128]{2,1,0:T(8,128)S(1)}, u32[]{:S(2)}, u32[]{:S(2)}) collective-permute-start(f32[21,8,128]{2,1,0:T(8,128)S(1)} %get-tuple-element.53), channel_id=1, source_target_pairs={{0,4},{2,6},{4,0},{6,2},{1,5},{3,7},{5,1},{7,3},{8,12},{10,14},{12... | collective-permute-start | bytes 258056 | tf_op jit(solution)/shard_map/slope_span/ppermute | solution.py:611
  42.6 2.0 %collective-permute-start.12 = (f32[21,8,128]{2,1,0:T(8,128)S(1)}, f32[21,8,128]{2,1,0:T(8,128)S(1)}, u32[]{:S(2)}, u32[]{:S(2)}) collective-permute-start(f32[21,8,128]{2,1,0:T(8,128)S(1)} %get-tuple-element.54), channel_id=1, source_target_pairs={{0,6},{2,0},{4,2},{6,4},{1,7},{3,1},{5,3},{7,5},{8,14},{10,8},{12,... | collective-permute-start | bytes 258056 | tf_op jit(solution)/shard_map/slope_span/ppermute | solution.py:611
  44.6 0.1 collective-permute-start.14
  44.7 1.4 %collective-permute-start.15 = (f32[22,8,128]{2,1,0:T(8,128)S(1)}, f32[22,8,128]{2,1,0:T(8,128)S(1)}, u32[]{:S(2)}, u32[]{:S(2)}) collective-permute-start(f32[22,8,128]{2,1,0:T(8,128)S(1)} %last_base.1.refs_0_), channel_id=1, source_target_pairs={{0,4},{2,6},{4,0},{6,2},{1,5},{3,7},{5,1},{7,3},{8,12},{10,14},{12... | collective-permute-start | bytes 270344 | tf_op jit(solution)/shard_map/base_spread/ppermute | solution.py:611
  46.1 1.4 %collective-permute-done.10.refs_5_ = f32[21,8,128]{2,1,0:T(8,128)S(1)} collective-permute-done((f32[21,8,128]{2,1,0:T(8,128)S(1)}, f32[21,8,128]{2,1,0:T(8,128)S(1)}, u32[]{:S(2)}, u32[]{:S(2)}) %collective-permute-start.10) | collective-permute-done | bytes 86048 | tf_op jit(solution)/shard_map/slope_span/ppermute | solution.py:611
  47.5 0.6 collective-permute-start.16
  48.1 0.3 span_slope.1.mine2
  48.4 2.2 %collective-permute-start.13 = (f32[21,8,128]{2,1,0:T(8,128)S(1)}, f32[21,8,128]{2,1,0:T(8,128)S(1)}, u32[]{:S(2)}, u32[]{:S(2)}) collective-permute-start(f32[21,8,128]{2,1,0:T(8,128)S(1)} %span_slope.1.mine2), channel_id=1, source_target_pairs={{0,8},{8,0},{1,9},{9,1},{2,10},{10,2},{3,11},{11,3},{4,12},{12,4},... | collective-permute-start | bytes 258056 | tf_op jit(solution)/shard_map/slope_x/ppermute | solution.py:611
  50.5 2.8 %collective-permute-done.13.other2 = f32[21,8,128]{2,1,0:T(8,128)S(1)} collective-permute-done((f32[21,8,128]{2,1,0:T(8,128)S(1)}, f32[21,8,128]{2,1,0:T(8,128)S(1)}, u32[]{:S(2)}, u32[]{:S(2)}) %collective-permute-start.13) | collective-permute-done | bytes 86048 | tf_op jit(solution)/shard_map/slope_x/ppermute | solution.py:611
  53.3 0.2 last_slope.1.after.refs_2_
  53.5 0.1 gather.1.refs_0_
  53.6 3.1 %collective-permute-start.17 = (f32[22,32,128]{2,1,0:T(8,128)S(1)}, f32[22,32,128]{2,1,0:T(8,128)S(1)}, u32[]{:S(2)}, u32[]{:S(2)}) collective-permute-start(f32[22,32,128]{2,1,0:T(8,128)S(1)} %gather.1.refs_0_), channel_id=1, source_target_pairs={{0,1},{1,0},{2,3},{3,2},{4,5},{5,4},{6,7},{7,6},{8,9},{9,8},{10,11... | collective-permute-start | bytes 1081352 | tf_op jit(solution)/shard_map/base_spread/ppermute | solution.py:611
  56.6 0.7 %collective-permute-start.18 = (f32[18,8,128]{2,1,0:T(8,128)S(1)}, f32[18,8,128]{2,1,0:T(8,128)S(1)}, u32[]{:S(2)}, u32[]{:S(2)}) collective-permute-start(f32[18,8,128]{2,1,0:T(8,128)S(1)} %last_slope.1.after.refs_2_), channel_id=1, source_target_pairs={{0,2},{2,4},{4,6},{6,0},{1,3},{3,5},{5,7},{7,1},{8,10},{10,12},{12... | collective-permute-start | bytes 221192 | tf_op jit(solution)/shard_map/slope_spread/ppermute | solution.py:611
  57.4 2.2 %collective-permute-start.19 = (f32[18,8,128]{2,1,0:T(8,128)S(1)}, f32[18,8,128]{2,1,0:T(8,128)S(1)}, u32[]{:S(2)}, u32[]{:S(2)}) collective-permute-start(f32[18,8,128]{2,1,0:T(8,128)S(1)} %last_slope.1.after.refs_2_), channel_id=1, source_target_pairs={{0,4},{2,6},{4,0},{6,2},{1,5},{3,7},{5,1},{7,3},{8,12},{10,14},{12... | collective-permute-start | bytes 221192 | tf_op jit(solution)/shard_map/slope_spread/ppermute | solution.py:611
  59.6 1.0 %collective-permute-start.20 = (f32[18,8,128]{2,1,0:T(8,128)S(1)}, f32[18,8,128]{2,1,0:T(8,128)S(1)}, u32[]{:S(2)}, u32[]{:S(2)}) collective-permute-start(f32[18,8,128]{2,1,0:T(8,128)S(1)} %last_slope.1.after.refs_2_), channel_id=1, source_target_pairs={{0,6},{2,0},{4,2},{6,4},{1,7},{3,1},{5,3},{7,5},{8,14},{10,8},{12,... | collective-permute-start | bytes 221192 | tf_op jit(solution)/shard_map/slope_spread/ppermute | solution.py:611
  60.6 0.9 %collective-permute-start.21 = (f32[18,8,128]{2,1,0:T(8,128)S(1)}, f32[18,8,128]{2,1,0:T(8,128)S(1)}, u32[]{:S(2)}, u32[]{:S(2)}) collective-permute-start(f32[18,8,128]{2,1,0:T(8,128)S(1)} %last_slope.1.after.refs_2_), channel_id=1, source_target_pairs={{0,1},{1,0},{2,3},{3,2},{4,5},{5,4},{6,7},{7,6},{8,9},{9,8},{10,11... | collective-permute-start | bytes 221192 | tf_op jit(solution)/shard_map/slope_spread/ppermute | solution.py:611
  61.5 0.2 collective-permute-done.18.refs_3_
  61.7 1.1 %collective-permute-start.22 = (f32[18,8,128]{2,1,0:T(8,128)S(1)}, f32[18,8,128]{2,1,0:T(8,128)S(1)}, u32[]{:S(2)}, u32[]{:S(2)}) collective-permute-start(f32[18,8,128]{2,1,0:T(8,128)S(1)} %collective-permute-done.18.refs_3_), channel_id=1, source_target_pairs={{0,1},{1,0},{2,3},{3,2},{4,5},{5,4},{6,7},{7,6},{8,9},{9,8},{10,11... | collective-permute-start | bytes 221192 | tf_op jit(solution)/shard_map/slope_spread/ppermute | solution.py:611
  62.7 0.8 %collective-permute-done.19.refs_4_ = f32[18,8,128]{2,1,0:T(8,128)S(1)} collective-permute-done((f32[18,8,128]{2,1,0:T(8,128)S(1)}, f32[18,8,128]{2,1,0:T(8,128)S(1)}, u32[]{:S(2)}, u32[]{:S(2)}) %collective-permute-start.19) | collective-permute-done | bytes 73760 | tf_op jit(solution)/shard_map/slope_spread/ppermute | solution.py:611
  63.5 0.9 %collective-permute-start.23 = (f32[18,8,128]{2,1,0:T(8,128)S(1)}, f32[18,8,128]{2,1,0:T(8,128)S(1)}, u32[]{:S(2)}, u32[]{:S(2)}) collective-permute-start(f32[18,8,128]{2,1,0:T(8,128)S(1)} %collective-permute-done.19.refs_4_), channel_id=1, source_target_pairs={{0,1},{1,0},{2,3},{3,2},{4,5},{5,4},{6,7},{7,6},{8,9},{9,8},{10,11... | collective-permute-start | bytes 221192 | tf_op jit(solution)/shard_map/slope_spread/ppermute | solution.py:611
  64.4 0.3 collective-permute-start.24
  64.7 0.6 collective-permute-done.23.refs_8_
  65.3 0.4 collective-permute-done.24.refs_9_
  65.7 1.1 %place.1 = f32[40,64,128]{2,1,0:T(8,128)} custom-call(f32[22,32,128]{2,1,0:T(8,128)S(1)} %gather.1.refs_0_, f32[22,32,128]{2,1,0:T(8,128)S(1)} %collective-permute-done.17.refs_1_, f32[18,8,128]{2,1,0:T(8,128)S(1)} %last_slope.1.after.refs_2_, f32[18,8,128]{2,1,0:T(8,128)S(1)} %collective-permute-done.18.refs_3_, ...), custom_call_target="tpu_custom_call" | custom-call | tf_op jit(solution)/shard_map/place/pallas_call | solution.py:584
  (19 shorter events, 0.1 us)
Async XLA Ops:
  0.0 10.1 %copy-start = (f32[4,64,64,128]{3,2,1,0:T(8,128)S(1)}, f32[4,64,64,128]{3,2,1,0:T(8,128)}, u32[]{:S(2)}) copy-start(f32[4,64,64,128]{3,2,1,0:T(8,128)} %flow.1) | copy-start | bytes 25165828
  0.0 19.8 %copy-start.1 = (f32[128,128]{1,0:T(8,128)S(1)}, f32[128,128]{1,0:T(8,128)}, u32[]{:S(2)}) copy-start(f32[128,128]{1,0:T(8,128)} %dy.1) | copy-start | bytes 196612
  1.7 21.4 %collective-permute-start.5 = (f32[3,64,4,128]{3,2,1,0:T(4,128)S(1)}, f32[3,64,4,128]{3,2,1,0:T(4,128)S(1)}, u32[]{:S(2)}, u32[]{:S(2)}) collective-permute-start(f32[3,64,4,128]{3,2,1,0:T(4,128)S(1)} %get-tuple-element.40), channel_id=1, source_target_pairs={{0,1},{1,2},{2,3},{3,4},{4,5},{5,6},{6,7},{7,8},{8,9},{9,10},{10,1... | collective-permute-start | bytes 1179656 | tf_op jit(solution)/shard_map/rim_exchange/ppermute | solution.py:611
  3.9 19.7 %collective-permute-start.6 = (f32[3,64,4,128]{3,2,1,0:T(4,128)S(1)}, f32[3,64,4,128]{3,2,1,0:T(4,128)S(1)}, u32[]{:S(2)}, u32[]{:S(2)}) collective-permute-start(f32[3,64,4,128]{3,2,1,0:T(4,128)S(1)} %get-tuple-element.41), channel_id=1, source_target_pairs={{0,15},{1,0},{2,1},{3,2},{4,3},{5,4},{6,5},{7,6},{8,7},{9,8},{10,9... | collective-permute-start | bytes 1179656 | tf_op jit(solution)/shard_map/rim_exchange/ppermute | solution.py:611
  3.9 32.0 %collective-permute-start.7 = (f32[4,4,64,128]{3,2,1,0:T(8,128)S(1)}, f32[4,4,64,128]{3,2,1,0:T(8,128)S(1)}, u32[]{:S(2)}, u32[]{:S(2)}) collective-permute-start(f32[4,4,64,128]{3,2,1,0:T(8,128)S(1)} %get-tuple-element.46), channel_id=1, source_target_pairs={{0,16},{16,32},{32,48},{48,64},{64,80},{80,96},{96,112},{1,17},{17... | collective-permute-start | bytes 1572872 | tf_op jit(solution)/shard_map/rim_exchange/ppermute | solution.py:625
  7.0 28.9 %collective-permute-start.8 = (f32[4,4,64,128]{3,2,1,0:T(8,128)S(1)}, f32[4,4,64,128]{3,2,1,0:T(8,128)S(1)}, u32[]{:S(2)}, u32[]{:S(2)}) collective-permute-start(f32[4,4,64,128]{3,2,1,0:T(8,128)S(1)} %get-tuple-element.47), channel_id=1, source_target_pairs={{16,0},{32,16},{48,32},{64,48},{80,64},{96,80},{112,96},{17,1},{33... | collective-permute-start | bytes 1572872 | tf_op jit(solution)/shard_map/rim_exchange/ppermute | solution.py:626
  14.7 8.1 %collective-permute-start = (f32[23,32,128]{2,1,0:T(8,128)S(1)}, f32[23,32,128]{2,1,0:T(8,128)S(1)}, u32[]{:S(2)}, u32[]{:S(2)}) collective-permute-start(f32[23,32,128]{2,1,0:T(8,128)S(1)} %get-tuple-element.32), channel_id=1, source_target_pairs={{0,1},{1,0},{2,3},{3,2},{4,5},{5,4},{6,7},{7,6},{8,9},{9,8},{10,11... | collective-permute-start | bytes 1130504 | tf_op jit(solution)/shard_map/base_core/ppermute | solution.py:611
  22.9 12.9 %collective-permute-start.1 = (f32[23,8,128]{2,1,0:T(8,128)S(1)}, f32[23,8,128]{2,1,0:T(8,128)S(1)}, u32[]{:S(2)}, u32[]{:S(2)}) collective-permute-start(f32[23,8,128]{2,1,0:T(8,128)S(1)} %get-tuple-element.34), channel_id=1, source_target_pairs={{0,2},{2,4},{4,6},{6,0},{1,3},{3,5},{5,7},{7,1},{8,10},{10,12},{12... | collective-permute-start | bytes 282632 | tf_op jit(solution)/shard_map/base_span/ppermute | solution.py:611
  23.0 12.9 %collective-permute-start.2 = (f32[23,8,128]{2,1,0:T(8,128)S(1)}, f32[23,8,128]{2,1,0:T(8,128)S(1)}, u32[]{:S(2)}, u32[]{:S(2)}) collective-permute-start(f32[23,8,128]{2,1,0:T(8,128)S(1)} %get-tuple-element.35), channel_id=1, source_target_pairs={{0,4},{2,6},{4,0},{6,2},{1,5},{3,7},{5,1},{7,3},{8,12},{10,14},{12... | collective-permute-start | bytes 282632 | tf_op jit(solution)/shard_map/base_span/ppermute | solution.py:611
  23.7 12.2 %collective-permute-start.3 = (f32[23,8,128]{2,1,0:T(8,128)S(1)}, f32[23,8,128]{2,1,0:T(8,128)S(1)}, u32[]{:S(2)}, u32[]{:S(2)}) collective-permute-start(f32[23,8,128]{2,1,0:T(8,128)S(1)} %get-tuple-element.36), channel_id=1, source_target_pairs={{0,6},{2,0},{4,2},{6,4},{1,7},{3,1},{5,3},{7,5},{8,14},{10,8},{12,... | collective-permute-start | bytes 282632 | tf_op jit(solution)/shard_map/base_span/ppermute | solution.py:611
  36.9 3.5 %collective-permute-start.9 = (f32[21,32,128]{2,1,0:T(8,128)S(1)}, f32[21,32,128]{2,1,0:T(8,128)S(1)}, u32[]{:S(2)}, u32[]{:S(2)}) collective-permute-start(f32[21,32,128]{2,1,0:T(8,128)S(1)} %get-tuple-element.49), channel_id=1, source_target_pairs={{0,1},{1,0},{2,3},{3,2},{4,5},{5,4},{6,7},{7,6},{8,9},{9,8},{10,11... | collective-permute-start | bytes 1032200 | tf_op jit(solution)/shard_map/slope_core/ppermute | solution.py:611
  37.6 7.0 %collective-permute-start.4 = (f32[23,8,128]{2,1,0:T(8,128)S(1)}, f32[23,8,128]{2,1,0:T(8,128)S(1)}, u32[]{:S(2)}, u32[]{:S(2)}) collective-permute-start(f32[23,8,128]{2,1,0:T(8,128)S(1)} %get-tuple-element.37.after.mine1.mine), channel_id=1, source_target_pairs={{0,8},{8,0},{1,9},{9,1},{2,10},{10,2},{3,11},{11,3},{4,12},{12,4},... | collective-permute-start | bytes 282632 | tf_op jit(solution)/shard_map/base_x/ppermute | solution.py:611
  40.6 6.9 %collective-permute-start.10 = (f32[21,8,128]{2,1,0:T(8,128)S(1)}, f32[21,8,128]{2,1,0:T(8,128)S(1)}, u32[]{:S(2)}, u32[]{:S(2)}) collective-permute-start(f32[21,8,128]{2,1,0:T(8,128)S(1)} %get-tuple-element.52), channel_id=1, source_target_pairs={{0,2},{2,4},{4,6},{6,0},{1,3},{3,5},{5,7},{7,1},{8,10},{10,12},{12... | collective-permute-start | bytes 258056 | tf_op jit(solution)/shard_map/slope_span/ppermute | solution.py:611
  40.7 7.4 %collective-permute-start.11 = (f32[21,8,128]{2,1,0:T(8,128)S(1)}, f32[21,8,128]{2,1,0:T(8,128)S(1)}, u32[]{:S(2)}, u32[]{:S(2)}) collective-permute-start(f32[21,8,128]{2,1,0:T(8,128)S(1)} %get-tuple-element.53), channel_id=1, source_target_pairs={{0,4},{2,6},{4,0},{6,2},{1,5},{3,7},{5,1},{7,3},{8,12},{10,14},{12... | collective-permute-start | bytes 258056 | tf_op jit(solution)/shard_map/slope_span/ppermute | solution.py:611
  42.6 5.5 %collective-permute-start.12 = (f32[21,8,128]{2,1,0:T(8,128)S(1)}, f32[21,8,128]{2,1,0:T(8,128)S(1)}, u32[]{:S(2)}, u32[]{:S(2)}) collective-permute-start(f32[21,8,128]{2,1,0:T(8,128)S(1)} %get-tuple-element.54), channel_id=1, source_target_pairs={{0,6},{2,0},{4,2},{6,4},{1,7},{3,1},{5,3},{7,5},{8,14},{10,8},{12,... | collective-permute-start | bytes 258056 | tf_op jit(solution)/shard_map/slope_span/ppermute | solution.py:611
  44.6 8.8 %collective-permute-start.14 = (f32[22,8,128]{2,1,0:T(8,128)S(1)}, f32[22,8,128]{2,1,0:T(8,128)S(1)}, u32[]{:S(2)}, u32[]{:S(2)}) collective-permute-start(f32[22,8,128]{2,1,0:T(8,128)S(1)} %last_base.1.refs_0_), channel_id=1, source_target_pairs={{0,2},{2,4},{4,6},{6,0},{1,3},{3,5},{5,7},{7,1},{8,10},{10,12},{12... | collective-permute-start | bytes 270344 | tf_op jit(solution)/shard_map/base_spread/ppermute | solution.py:611
  44.7 8.8 %collective-permute-start.15 = (f32[22,8,128]{2,1,0:T(8,128)S(1)}, f32[22,8,128]{2,1,0:T(8,128)S(1)}, u32[]{:S(2)}, u32[]{:S(2)}) collective-permute-start(f32[22,8,128]{2,1,0:T(8,128)S(1)} %last_base.1.refs_0_), channel_id=1, source_target_pairs={{0,4},{2,6},{4,0},{6,2},{1,5},{3,7},{5,1},{7,3},{8,12},{10,14},{12... | collective-permute-start | bytes 270344 | tf_op jit(solution)/shard_map/base_spread/ppermute | solution.py:611
  47.5 6.0 %collective-permute-start.16 = (f32[22,8,128]{2,1,0:T(8,128)S(1)}, f32[22,8,128]{2,1,0:T(8,128)S(1)}, u32[]{:S(2)}, u32[]{:S(2)}) collective-permute-start(f32[22,8,128]{2,1,0:T(8,128)S(1)} %last_base.1.refs_0_), channel_id=1, source_target_pairs={{0,6},{2,0},{4,2},{6,4},{1,7},{3,1},{5,3},{7,5},{8,14},{10,8},{12,... | collective-permute-start | bytes 270344 | tf_op jit(solution)/shard_map/base_spread/ppermute | solution.py:611
  48.4 4.9 %collective-permute-start.13 = (f32[21,8,128]{2,1,0:T(8,128)S(1)}, f32[21,8,128]{2,1,0:T(8,128)S(1)}, u32[]{:S(2)}, u32[]{:S(2)}) collective-permute-start(f32[21,8,128]{2,1,0:T(8,128)S(1)} %span_slope.1.mine2), channel_id=1, source_target_pairs={{0,8},{8,0},{1,9},{9,1},{2,10},{10,2},{3,11},{11,3},{4,12},{12,4},... | collective-permute-start | bytes 258056 | tf_op jit(solution)/shard_map/slope_x/ppermute | solution.py:611
  53.6 12.1 %collective-permute-start.17 = (f32[22,32,128]{2,1,0:T(8,128)S(1)}, f32[22,32,128]{2,1,0:T(8,128)S(1)}, u32[]{:S(2)}, u32[]{:S(2)}) collective-permute-start(f32[22,32,128]{2,1,0:T(8,128)S(1)} %gather.1.refs_0_), channel_id=1, source_target_pairs={{0,1},{1,0},{2,3},{3,2},{4,5},{5,4},{6,7},{7,6},{8,9},{9,8},{10,11... | collective-permute-start | bytes 1081352 | tf_op jit(solution)/shard_map/base_spread/ppermute | solution.py:611
  56.6 5.0 %collective-permute-start.18 = (f32[18,8,128]{2,1,0:T(8,128)S(1)}, f32[18,8,128]{2,1,0:T(8,128)S(1)}, u32[]{:S(2)}, u32[]{:S(2)}) collective-permute-start(f32[18,8,128]{2,1,0:T(8,128)S(1)} %last_slope.1.after.refs_2_), channel_id=1, source_target_pairs={{0,2},{2,4},{4,6},{6,0},{1,3},{3,5},{5,7},{7,1},{8,10},{10,12},{12... | collective-permute-start | bytes 221192 | tf_op jit(solution)/shard_map/slope_spread/ppermute | solution.py:611
  57.4 6.1 %collective-permute-start.19 = (f32[18,8,128]{2,1,0:T(8,128)S(1)}, f32[18,8,128]{2,1,0:T(8,128)S(1)}, u32[]{:S(2)}, u32[]{:S(2)}) collective-permute-start(f32[18,8,128]{2,1,0:T(8,128)S(1)} %last_slope.1.after.refs_2_), channel_id=1, source_target_pairs={{0,4},{2,6},{4,0},{6,2},{1,5},{3,7},{5,1},{7,3},{8,12},{10,14},{12... | collective-permute-start | bytes 221192 | tf_op jit(solution)/shard_map/slope_spread/ppermute | solution.py:611
  59.6 4.8 %collective-permute-start.20 = (f32[18,8,128]{2,1,0:T(8,128)S(1)}, f32[18,8,128]{2,1,0:T(8,128)S(1)}, u32[]{:S(2)}, u32[]{:S(2)}) collective-permute-start(f32[18,8,128]{2,1,0:T(8,128)S(1)} %last_slope.1.after.refs_2_), channel_id=1, source_target_pairs={{0,6},{2,0},{4,2},{6,4},{1,7},{3,1},{5,3},{7,5},{8,14},{10,8},{12,... | collective-permute-start | bytes 221192 | tf_op jit(solution)/shard_map/slope_spread/ppermute | solution.py:611
  60.6 4.1 %collective-permute-start.21 = (f32[18,8,128]{2,1,0:T(8,128)S(1)}, f32[18,8,128]{2,1,0:T(8,128)S(1)}, u32[]{:S(2)}, u32[]{:S(2)}) collective-permute-start(f32[18,8,128]{2,1,0:T(8,128)S(1)} %last_slope.1.after.refs_2_), channel_id=1, source_target_pairs={{0,1},{1,0},{2,3},{3,2},{4,5},{5,4},{6,7},{7,6},{8,9},{9,8},{10,11... | collective-permute-start | bytes 221192 | tf_op jit(solution)/shard_map/slope_spread/ppermute | solution.py:611
  61.7 3.0 %collective-permute-start.22 = (f32[18,8,128]{2,1,0:T(8,128)S(1)}, f32[18,8,128]{2,1,0:T(8,128)S(1)}, u32[]{:S(2)}, u32[]{:S(2)}) collective-permute-start(f32[18,8,128]{2,1,0:T(8,128)S(1)} %collective-permute-done.18.refs_3_), channel_id=1, source_target_pairs={{0,1},{1,0},{2,3},{3,2},{4,5},{5,4},{6,7},{7,6},{8,9},{9,8},{10,11... | collective-permute-start | bytes 221192 | tf_op jit(solution)/shard_map/slope_spread/ppermute | solution.py:611
  63.5 1.8 %collective-permute-start.23 = (f32[18,8,128]{2,1,0:T(8,128)S(1)}, f32[18,8,128]{2,1,0:T(8,128)S(1)}, u32[]{:S(2)}, u32[]{:S(2)}) collective-permute-start(f32[18,8,128]{2,1,0:T(8,128)S(1)} %collective-permute-done.19.refs_4_), channel_id=1, source_target_pairs={{0,1},{1,0},{2,3},{3,2},{4,5},{5,4},{6,7},{7,6},{8,9},{9,8},{10,11... | collective-permute-start | bytes 221192 | tf_op jit(solution)/shard_map/slope_spread/ppermute | solution.py:611
  64.4 1.3 %collective-permute-start.24 = (f32[18,8,128]{2,1,0:T(8,128)S(1)}, f32[18,8,128]{2,1,0:T(8,128)S(1)}, u32[]{:S(2)}, u32[]{:S(2)}) collective-permute-start(f32[18,8,128]{2,1,0:T(8,128)S(1)} %collective-permute-done.20.refs_5_), channel_id=1, source_target_pairs={{0,1},{1,0},{2,3},{3,2},{4,5},{5,4},{6,7},{7,6},{8,9},{9,8},{10,11... | collective-permute-start | bytes 221192 | tf_op jit(solution)/shard_map/slope_spread/ppermute | solution.py:611

commit v7 on v6

--- a/solution.py
+++ b/solution.py
@@ -21,6 +21,7 @@
 STATE = 44
 OUT = 40
 NBASE = 19
+z_order = (0, 2, 1, 3)
 NSLOPE = 22
 GXA, ZA, CA = "gx", ("xh", "z", "c"), "c"
 
@@ -570,7 +571,7 @@
             first = OUT - fields
             side, step = divmod(k - 2, zn)
             c = core if side == 0 else 1 - core
-            at = rows * (zn * c + lax.rem(zi + zn - step, zn))
+            at = rows * (zn * c + lax.rem(zi + zn - z_order[step], zn))
         at = pl.multiple_of(at, 8)
         copies.append(
             pltpu.make_async_copy(
@@ -682,7 +683,7 @@
         )
         all1 = [half1, send(half1, CA, 1)]
     with jax.named_scope("slope_spread"):
-        all2 = spread(done2)
+        all2 = [done2] + [send(done2, "z", k) for k in z_order[1:]]
         all2 = all2 + [send(v, CA, 1) for v in all2]
     return place(all1 + all2, (OUT, lx, ny))
 

time: 67.9 us -> 67.9 us (level)
  transfers between devices with their start and end apart: 25 -> 25, of which waited for: 6 -> 5; matrix products, arithmetic and copies ran while one was open for 0% -> 0% of each run, Pallas kernels for 28% -> 28%
where the time goes in v7:
time: 67.9 us; the launch traced here: 67 us
  starting transfers between devices  38.6 us (57%)
  Pallas kernels  22.2 us (33%)
  waiting for transfers between devices  5.84 us (9%)
    ppermute x23, starting transfers between devices, send(): lax.ppermute(value, axis, [(i, (i + step) % size) for i in range(size)])  32.5 us
    pallas_call x1, Pallas kernels, inner_moments(): pl.pallas_call(inner_kernel, in_specs=[vm] * 5 + [pl.BlockSpec(memory_spa...  10.1 us
    ppermute x23, waiting for transfers between devices, send(): lax.ppermute(value, axis, [(i, (i + step) % size) for i in range(size)])  5.84 us
    pallas_call x1, Pallas kernels, base_moments(): pl.pallas_call(base_kernel, in_specs=[vm], out_specs=[vm] * 4, out_shape=...  4.54 us
    ppermute x1, starting transfers between devices, shards(): xl = lax.ppermute(xl, GXA, up)  3.11 us
    ppermute x1, starting transfers between devices, shards(): xr = lax.ppermute(xr, GXA, down)  3.06 us
    pallas_call x1, Pallas kernels, y_slopes(): pl.pallas_call(y_kernel, in_specs=[vm, vm], out_specs=[vm, vm], out_shape...  2.98 us
    pallas_call x1, Pallas kernels, cut(): pl.pallas_call(kernel, in_specs=[pl.BlockSpec(memory_space=pltpu.HBM)] +...  1.64 us
  transfers between devices with their start and end apart: 25, of which 5 were waited for; matrix products, arithmetic and copies ran while one was open for 0% of the time, Pallas kernels for 28%

profile of v7, /device:TPU:9, one launch (start us, length us, event | category | flops | bytes accessed | tf_op | source)
XLA Modules:
  0.0 67.0 jit_solution(2370934314412125348)
XLA Ops:
  0.0 1.6 %rims.1 = (f32[3,64,4,128]{3,2,1,0:T(4,128)S(1)}, f32[3,64,4,128]{3,2,1,0:T(4,128)S(1)}, f32[4,4,64,128]{3,2,1,0:T(8,128)S(1)}, f32[4,4,64,128]{3,2,1,0:T(8,128)S(1)}) custom-call(f32[4,64,64,128]{3,2,1,0:T(8,128)} %flow.1), custom_call_target="tpu_custom_call" | custom-call | tf_op jit(solution)/shard_map/rims/pallas_call | solution.py:102
  1.7 2.3 %collective-permute-start.5 = (f32[3,64,4,128]{3,2,1,0:T(4,128)S(1)}, f32[3,64,4,128]{3,2,1,0:T(4,128)S(1)}, u32[]{:S(2)}, u32[]{:S(2)}) collective-permute-start(f32[3,64,4,128]{3,2,1,0:T(4,128)S(1)} %get-tuple-element.40), channel_id=1, source_target_pairs={{0,1},{1,2},{2,3},{3,4},{4,5},{5,6},{6,7},{7,8},{8,9},{9,10},{10,1... | collective-permute-start | bytes 1179656 | tf_op jit(solution)/shard_map/rim_exchange/ppermute | solution.py:612
  3.9 3.1 %collective-permute-start.7 = (f32[4,4,64,128]{3,2,1,0:T(8,128)S(1)}, f32[4,4,64,128]{3,2,1,0:T(8,128)S(1)}, u32[]{:S(2)}, u32[]{:S(2)}) collective-permute-start(f32[4,4,64,128]{3,2,1,0:T(8,128)S(1)} %get-tuple-element.46), channel_id=1, source_target_pairs={{0,16},{16,32},{32,48},{48,64},{64,80},{80,96},{96,112},{1,17},{17... | collective-permute-start | bytes 1572872 | tf_op jit(solution)/shard_map/rim_exchange/ppermute | solution.py:626
  7.0 3.1 %collective-permute-start.8 = (f32[4,4,64,128]{3,2,1,0:T(8,128)S(1)}, f32[4,4,64,128]{3,2,1,0:T(8,128)S(1)}, u32[]{:S(2)}, u32[]{:S(2)}) collective-permute-start(f32[4,4,64,128]{3,2,1,0:T(8,128)S(1)} %get-tuple-element.47), channel_id=1, source_target_pairs={{16,0},{32,16},{48,32},{64,48},{80,64},{96,80},{112,96},{17,1},{33... | collective-permute-start | bytes 1572872 | tf_op jit(solution)/shard_map/rim_exchange/ppermute | solution.py:627
  10.1 4.5 %base_moments.1 = (f32[4,72,80,128]{3,2,1,0:T(8,128)S(1)}, f32[4,64,128]{2,1,0:T(8,128)S(1)}, f32[23,32,128]{2,1,0:T(8,128)S(1)}, f32[23,32,128]{2,1,0:T(8,128)S(1)}) custom-call(f32[4,64,64,128]{3,2,1,0:T(8,128)S(1)} %copy-done), custom_call_target="tpu_custom_call" | custom-call | flops 1000 | bytes 1000 | tf_op jit(solution)/shard_map/base_moments/pallas_call | solution.py:200
  14.7 5.1 %collective-permute-start = (f32[23,32,128]{2,1,0:T(8,128)S(1)}, f32[23,32,128]{2,1,0:T(8,128)S(1)}, u32[]{:S(2)}, u32[]{:S(2)}) collective-permute-start(f32[23,32,128]{2,1,0:T(8,128)S(1)} %get-tuple-element.32), channel_id=1, source_target_pairs={{0,1},{1,0},{2,3},{3,2},{4,5},{5,4},{6,7},{7,6},{8,9},{9,8},{10,11... | collective-permute-start | bytes 1130504 | tf_op jit(solution)/shard_map/base_core/ppermute | solution.py:612
  19.8 3.0 %y_slopes.1 = (f32[4,64,64,128]{3,2,1,0:T(8,128)S(1)}, f32[128,128]{1,0:T(8,128)S(1)}) custom-call(f32[4,72,80,128]{3,2,1,0:T(8,128)S(1)} %get-tuple-element.38.pad.pad_in, f32[128,128]{1,0:T(8,128)S(1)} %copy-done.1), custom_call_target="tpu_custom_call" | custom-call | flops 1000 | bytes 1000 | tf_op jit(solution)/shard_map/y_slopes/pallas_call | solution.py:218
  22.8 0.0 collective-permute-done.got.got1
  22.8 0.1 core_base.1
  22.9 0.1 collective-permute-start.1
  23.0 0.0 collective-permute-done.5.zl
  23.0 0.7 collective-permute-start.2
  23.7 2.1 %collective-permute-start.3 = (f32[23,8,128]{2,1,0:T(8,128)S(1)}, f32[23,8,128]{2,1,0:T(8,128)S(1)}, u32[]{:S(2)}, u32[]{:S(2)}) collective-permute-start(f32[23,8,128]{2,1,0:T(8,128)S(1)} %get-tuple-element.36), channel_id=1, source_target_pairs={{0,6},{2,0},{4,2},{6,4},{1,7},{3,1},{5,3},{7,5},{8,14},{10,8},{12,... | collective-permute-start | bytes 282632 | tf_op jit(solution)/shard_map/base_span/ppermute | solution.py:612
  25.8 10.1 %inner_moments.1 = (f32[4,72,80,128]{3,2,1,0:T(8,128)S(1)}, f32[21,32,128]{2,1,0:T(8,128)S(1)}, f32[21,32,128]{2,1,0:T(8,128)S(1)}) custom-call(f32[4,72,80,128]{3,2,1,0:T(8,128)S(1)} %get-tuple-element.38.pad.pad_in, f32[4,64,64,128]{3,2,1,0:T(8,128)S(1)} %get-tuple-element.39.ysl, ...), custom_call_target="tpu_custom_call", output_to_operand_aliasing={{0}: (0, {})} | custom-call | flops 1500000000 | bytes 84000000 | tf_op jit(solution)/shard_map/inner_moments/pallas_call | solution.py:370
  35.9 0.0 collective-permute-done.1.one.refs_1_
  35.9 0.0 collective-permute-done.3.three.refs_3_
  35.9 0.1 span_base.1
  36.0 0.0 collective-permute-done.8.xr
  36.0 0.9 %edge_moments.1 = (f32[4,72,80,128]{3,2,1,0:T(8,128)S(1)}, f32[21,32,128]{2,1,0:T(8,128)S(1)}, f32[21,32,128]{2,1,0:T(8,128)S(1)}) custom-call(f32[4,72,80,128]{3,2,1,0:T(8,128)S(1)} %get-tuple-element.43.pad_in, f32[21,32,128]{2,1,0:T(8,128)S(1)} %get-tuple-element.44.keep_in, ...), custom_call_target="tpu_custom_call", output_to_operand_aliasing={{0}: (0, {}), {1}: (1, {}), {2}: (2, {})} | custom-call | flops 52428800 | bytes 1048576 | tf_op jit(solution)/shard_map/edge_moments/pallas_call | solution.py:444
  36.9 0.7 %collective-permute-start.9 = (f32[21,32,128]{2,1,0:T(8,128)S(1)}, f32[21,32,128]{2,1,0:T(8,128)S(1)}, u32[]{:S(2)}, u32[]{:S(2)}) collective-permute-start(f32[21,32,128]{2,1,0:T(8,128)S(1)} %get-tuple-element.49), channel_id=1, source_target_pairs={{0,1},{1,0},{2,3},{3,2},{4,5},{5,4},{6,7},{7,6},{8,9},{9,8},{10,11... | collective-permute-start | bytes 1032200 | tf_op jit(solution)/shard_map/slope_core/ppermute | solution.py:612
  37.6 2.8 %collective-permute-start.4 = (f32[23,8,128]{2,1,0:T(8,128)S(1)}, f32[23,8,128]{2,1,0:T(8,128)S(1)}, u32[]{:S(2)}, u32[]{:S(2)}) collective-permute-start(f32[23,8,128]{2,1,0:T(8,128)S(1)} %get-tuple-element.37.after.mine1.mine), channel_id=1, source_target_pairs={{0,8},{8,0},{1,9},{9,1},{2,10},{10,2},{3,11},{11,3},{4,12},{12,4},... | collective-permute-start | bytes 282632 | tf_op jit(solution)/shard_map/base_x/ppermute | solution.py:612
  40.3 0.2 core_slope.1
  40.6 0.1 collective-permute-start.10
  40.7 1.9 %collective-permute-start.11 = (f32[21,8,128]{2,1,0:T(8,128)S(1)}, f32[21,8,128]{2,1,0:T(8,128)S(1)}, u32[]{:S(2)}, u32[]{:S(2)}) collective-permute-start(f32[21,8,128]{2,1,0:T(8,128)S(1)} %get-tuple-element.53), channel_id=1, source_target_pairs={{0,4},{2,6},{4,0},{6,2},{1,5},{3,7},{5,1},{7,3},{8,12},{10,14},{12... | collective-permute-start | bytes 258056 | tf_op jit(solution)/shard_map/slope_span/ppermute | solution.py:612
  42.6 2.0 %collective-permute-start.12 = (f32[21,8,128]{2,1,0:T(8,128)S(1)}, f32[21,8,128]{2,1,0:T(8,128)S(1)}, u32[]{:S(2)}, u32[]{:S(2)}) collective-permute-start(f32[21,8,128]{2,1,0:T(8,128)S(1)} %get-tuple-element.54), channel_id=1, source_target_pairs={{0,6},{2,0},{4,2},{6,4},{1,7},{3,1},{5,3},{7,5},{8,14},{10,8},{12,... | collective-permute-start | bytes 258056 | tf_op jit(solution)/shard_map/slope_span/ppermute | solution.py:612
  44.6 0.1 collective-permute-start.14
  44.7 1.4 %collective-permute-start.15 = (f32[22,8,128]{2,1,0:T(8,128)S(1)}, f32[22,8,128]{2,1,0:T(8,128)S(1)}, u32[]{:S(2)}, u32[]{:S(2)}) collective-permute-start(f32[22,8,128]{2,1,0:T(8,128)S(1)} %last_base.1.refs_0_), channel_id=1, source_target_pairs={{0,4},{2,6},{4,0},{6,2},{1,5},{3,7},{5,1},{7,3},{8,12},{10,14},{12... | collective-permute-start | bytes 270344 | tf_op jit(solution)/shard_map/base_spread/ppermute | solution.py:612
  46.1 1.4 %collective-permute-done.10.refs_5_ = f32[21,8,128]{2,1,0:T(8,128)S(1)} collective-permute-done((f32[21,8,128]{2,1,0:T(8,128)S(1)}, f32[21,8,128]{2,1,0:T(8,128)S(1)}, u32[]{:S(2)}, u32[]{:S(2)}) %collective-permute-start.10) | collective-permute-done | bytes 86048 | tf_op jit(solution)/shard_map/slope_span/ppermute | solution.py:612
  47.5 0.6 collective-permute-start.16
  48.1 0.3 span_slope.1.mine2
  48.4 2.2 %collective-permute-start.13 = (f32[21,8,128]{2,1,0:T(8,128)S(1)}, f32[21,8,128]{2,1,0:T(8,128)S(1)}, u32[]{:S(2)}, u32[]{:S(2)}) collective-permute-start(f32[21,8,128]{2,1,0:T(8,128)S(1)} %span_slope.1.mine2), channel_id=1, source_target_pairs={{0,8},{8,0},{1,9},{9,1},{2,10},{10,2},{3,11},{11,3},{4,12},{12,4},... | collective-permute-start | bytes 258056 | tf_op jit(solution)/shard_map/slope_x/ppermute | solution.py:612
  50.5 2.8 %collective-permute-done.13.other2 = f32[21,8,128]{2,1,0:T(8,128)S(1)} collective-permute-done((f32[21,8,128]{2,1,0:T(8,128)S(1)}, f32[21,8,128]{2,1,0:T(8,128)S(1)}, u32[]{:S(2)}, u32[]{:S(2)}) %collective-permute-start.13) | collective-permute-done | bytes 86048 | tf_op jit(solution)/shard_map/slope_x/ppermute | solution.py:612
  53.3 0.2 last_slope.1.after.refs_2_
  53.5 0.0 collective-permute-done.16.refs_3_
  53.5 0.1 gather.1.refs_0_
  53.6 3.1 %collective-permute-start.17 = (f32[22,32,128]{2,1,0:T(8,128)S(1)}, f32[22,32,128]{2,1,0:T(8,128)S(1)}, u32[]{:S(2)}, u32[]{:S(2)}) collective-permute-start(f32[22,32,128]{2,1,0:T(8,128)S(1)} %gather.1.refs_0_), channel_id=1, source_target_pairs={{0,1},{1,0},{2,3},{3,2},{4,5},{5,4},{6,7},{7,6},{8,9},{9,8},{10,11... | collective-permute-start | bytes 1081352 | tf_op jit(solution)/shard_map/base_spread/ppermute | solution.py:612
  56.6 1.9 %collective-permute-start.18 = (f32[18,8,128]{2,1,0:T(8,128)S(1)}, f32[18,8,128]{2,1,0:T(8,128)S(1)}, u32[]{:S(2)}, u32[]{:S(2)}) collective-permute-start(f32[18,8,128]{2,1,0:T(8,128)S(1)} %last_slope.1.after.refs_2_), channel_id=1, source_target_pairs={{0,4},{2,6},{4,0},{6,2},{1,5},{3,7},{5,1},{7,3},{8,12},{10,14},{12... | collective-permute-start | bytes 221192 | tf_op jit(solution)/shard_map/slope_spread/ppermute | solution.py:612
  58.5 0.5 collective-permute-start.19
  59.0 2.2 %collective-permute-start.20 = (f32[18,8,128]{2,1,0:T(8,128)S(1)}, f32[18,8,128]{2,1,0:T(8,128)S(1)}, u32[]{:S(2)}, u32[]{:S(2)}) collective-permute-start(f32[18,8,128]{2,1,0:T(8,128)S(1)} %last_slope.1.after.refs_2_), channel_id=1, source_target_pairs={{0,6},{2,0},{4,2},{6,4},{1,7},{3,1},{5,3},{7,5},{8,14},{10,8},{12,... | collective-permute-start | bytes 221192 | tf_op jit(solution)/shard_map/slope_spread/ppermute | solution.py:612
  61.2 0.9 %collective-permute-start.21 = (f32[18,8,128]{2,1,0:T(8,128)S(1)}, f32[18,8,128]{2,1,0:T(8,128)S(1)}, u32[]{:S(2)}, u32[]{:S(2)}) collective-permute-start(f32[18,8,128]{2,1,0:T(8,128)S(1)} %last_slope.1.after.refs_2_), channel_id=1, source_target_pairs={{0,1},{1,0},{2,3},{3,2},{4,5},{5,4},{6,7},{7,6},{8,9},{9,8},{10,11... | collective-permute-start | bytes 221192 | tf_op jit(solution)/shard_map/slope_spread/ppermute | solution.py:612
  62.1 0.0 collective-permute-done.18.refs_3_
  62.1 1.0 %collective-permute-start.22 = (f32[18,8,128]{2,1,0:T(8,128)S(1)}, f32[18,8,128]{2,1,0:T(8,128)S(1)}, u32[]{:S(2)}, u32[]{:S(2)}) collective-permute-start(f32[18,8,128]{2,1,0:T(8,128)S(1)} %collective-permute-done.18.refs_3_), channel_id=1, source_target_pairs={{0,1},{1,0},{2,3},{3,2},{4,5},{5,4},{6,7},{7,6},{8,9},{9,8},{10,11... | collective-permute-start | bytes 221192 | tf_op jit(solution)/shard_map/slope_spread/ppermute | solution.py:612
  63.1 0.4 collective-permute-done.19.refs_4_
  63.5 1.0 %collective-permute-start.23 = (f32[18,8,128]{2,1,0:T(8,128)S(1)}, f32[18,8,128]{2,1,0:T(8,128)S(1)}, u32[]{:S(2)}, u32[]{:S(2)}) collective-permute-start(f32[18,8,128]{2,1,0:T(8,128)S(1)} %collective-permute-done.19.refs_4_), channel_id=1, source_target_pairs={{0,1},{1,0},{2,3},{3,2},{4,5},{5,4},{6,7},{7,6},{8,9},{9,8},{10,11... | collective-permute-start | bytes 221192 | tf_op jit(solution)/shard_map/slope_spread/ppermute | solution.py:612
  64.6 0.0 collective-permute-start.24
  64.6 0.9 %collective-permute-done.23.refs_8_ = f32[18,8,128]{2,1,0:T(8,128)S(1)} collective-permute-done((f32[18,8,128]{2,1,0:T(8,128)S(1)}, f32[18,8,128]{2,1,0:T(8,128)S(1)}, u32[]{:S(2)}, u32[]{:S(2)}) %collective-permute-start.23) | collective-permute-done | bytes 73760 | tf_op jit(solution)/shard_map/slope_spread/ppermute | solution.py:612
  65.5 0.4 collective-permute-done.24.refs_9_
  65.8 1.1 %place.1 = f32[40,64,128]{2,1,0:T(8,128)} custom-call(f32[22,32,128]{2,1,0:T(8,128)S(1)} %gather.1.refs_0_, f32[22,32,128]{2,1,0:T(8,128)S(1)} %collective-permute-done.17.refs_1_, f32[18,8,128]{2,1,0:T(8,128)S(1)} %last_slope.1.after.refs_2_, f32[18,8,128]{2,1,0:T(8,128)S(1)} %collective-permute-done.18.refs_3_, ...), custom_call_target="tpu_custom_call" | custom-call | tf_op jit(solution)/shard_map/place/pallas_call | solution.py:585
  (19 shorter events, 0.1 us)
Async XLA Ops:
  0.0 10.1 %copy-start = (f32[4,64,64,128]{3,2,1,0:T(8,128)S(1)}, f32[4,64,64,128]{3,2,1,0:T(8,128)}, u32[]{:S(2)}) copy-start(f32[4,64,64,128]{3,2,1,0:T(8,128)} %flow.1) | copy-start | bytes 25165828
  0.0 19.8 %copy-start.1 = (f32[128,128]{1,0:T(8,128)S(1)}, f32[128,128]{1,0:T(8,128)}, u32[]{:S(2)}) copy-start(f32[128,128]{1,0:T(8,128)} %dy.1) | copy-start | bytes 196612
  1.7 21.4 %collective-permute-start.5 = (f32[3,64,4,128]{3,2,1,0:T(4,128)S(1)}, f32[3,64,4,128]{3,2,1,0:T(4,128)S(1)}, u32[]{:S(2)}, u32[]{:S(2)}) collective-permute-start(f32[3,64,4,128]{3,2,1,0:T(4,128)S(1)} %get-tuple-element.40), channel_id=1, source_target_pairs={{0,1},{1,2},{2,3},{3,4},{4,5},{5,6},{6,7},{7,8},{8,9},{9,10},{10,1... | collective-permute-start | bytes 1179656 | tf_op jit(solution)/shard_map/rim_exchange/ppermute | solution.py:612
  3.9 19.7 %collective-permute-start.6 = (f32[3,64,4,128]{3,2,1,0:T(4,128)S(1)}, f32[3,64,4,128]{3,2,1,0:T(4,128)S(1)}, u32[]{:S(2)}, u32[]{:S(2)}) collective-permute-start(f32[3,64,4,128]{3,2,1,0:T(4,128)S(1)} %get-tuple-element.41), channel_id=1, source_target_pairs={{0,15},{1,0},{2,1},{3,2},{4,3},{5,4},{6,5},{7,6},{8,7},{9,8},{10,9... | collective-permute-start | bytes 1179656 | tf_op jit(solution)/shard_map/rim_exchange/ppermute | solution.py:612
  3.9 32.0 %collective-permute-start.7 = (f32[4,4,64,128]{3,2,1,0:T(8,128)S(1)}, f32[4,4,64,128]{3,2,1,0:T(8,128)S(1)}, u32[]{:S(2)}, u32[]{:S(2)}) collective-permute-start(f32[4,4,64,128]{3,2,1,0:T(8,128)S(1)} %get-tuple-element.46), channel_id=1, source_target_pairs={{0,16},{16,32},{32,48},{48,64},{64,80},{80,96},{96,112},{1,17},{17... | collective-permute-start | bytes 1572872 | tf_op jit(solution)/shard_map/rim_exchange/ppermute | solution.py:626
  7.0 28.9 %collective-permute-start.8 = (f32[4,4,64,128]{3,2,1,0:T(8,128)S(1)}, f32[4,4,64,128]{3,2,1,0:T(8,128)S(1)}, u32[]{:S(2)}, u32[]{:S(2)}) collective-permute-start(f32[4,4,64,128]{3,2,1,0:T(8,128)S(1)} %get-tuple-element.47), channel_id=1, source_target_pairs={{16,0},{32,16},{48,32},{64,48},{80,64},{96,80},{112,96},{17,1},{33... | collective-permute-start | bytes 1572872 | tf_op jit(solution)/shard_map/rim_exchange/ppermute | solution.py:627
  14.7 8.1 %collective-permute-start = (f32[23,32,128]{2,1,0:T(8,128)S(1)}, f32[23,32,128]{2,1,0:T(8,128)S(1)}, u32[]{:S(2)}, u32[]{:S(2)}) collective-permute-start(f32[23,32,128]{2,1,0:T(8,128)S(1)} %get-tuple-element.32), channel_id=1, source_target_pairs={{0,1},{1,0},{2,3},{3,2},{4,5},{5,4},{6,7},{7,6},{8,9},{9,8},{10,11... | collective-permute-start | bytes 1130504 | tf_op jit(solution)/shard_map/base_core/ppermute | solution.py:612
  22.9 12.9 %collective-permute-start.1 = (f32[23,8,128]{2,1,0:T(8,128)S(1)}, f32[23,8,128]{2,1,0:T(8,128)S(1)}, u32[]{:S(2)}, u32[]{:S(2)}) collective-permute-start(f32[23,8,128]{2,1,0:T(8,128)S(1)} %get-tuple-element.34), channel_id=1, source_target_pairs={{0,2},{2,4},{4,6},{6,0},{1,3},{3,5},{5,7},{7,1},{8,10},{10,12},{12... | collective-permute-start | bytes 282632 | tf_op jit(solution)/shard_map/base_span/ppermute | solution.py:612
  23.0 12.9 %collective-permute-start.2 = (f32[23,8,128]{2,1,0:T(8,128)S(1)}, f32[23,8,128]{2,1,0:T(8,128)S(1)}, u32[]{:S(2)}, u32[]{:S(2)}) collective-permute-start(f32[23,8,128]{2,1,0:T(8,128)S(1)} %get-tuple-element.35), channel_id=1, source_target_pairs={{0,4},{2,6},{4,0},{6,2},{1,5},{3,7},{5,1},{7,3},{8,12},{10,14},{12... | collective-permute-start | bytes 282632 | tf_op jit(solution)/shard_map/base_span/ppermute | solution.py:612
  23.7 12.2 %collective-permute-start.3 = (f32[23,8,128]{2,1,0:T(8,128)S(1)}, f32[23,8,128]{2,1,0:T(8,128)S(1)}, u32[]{:S(2)}, u32[]{:S(2)}) collective-permute-start(f32[23,8,128]{2,1,0:T(8,128)S(1)} %get-tuple-element.36), channel_id=1, source_target_pairs={{0,6},{2,0},{4,2},{6,4},{1,7},{3,1},{5,3},{7,5},{8,14},{10,8},{12,... | collective-permute-start | bytes 282632 | tf_op jit(solution)/shard_map/base_span/ppermute | solution.py:612
  36.9 3.5 %collective-permute-start.9 = (f32[21,32,128]{2,1,0:T(8,128)S(1)}, f32[21,32,128]{2,1,0:T(8,128)S(1)}, u32[]{:S(2)}, u32[]{:S(2)}) collective-permute-start(f32[21,32,128]{2,1,0:T(8,128)S(1)} %get-tuple-element.49), channel_id=1, source_target_pairs={{0,1},{1,0},{2,3},{3,2},{4,5},{5,4},{6,7},{7,6},{8,9},{9,8},{10,11... | collective-permute-start | bytes 1032200 | tf_op jit(solution)/shard_map/slope_core/ppermute | solution.py:612
  37.6 7.0 %collective-permute-start.4 = (f32[23,8,128]{2,1,0:T(8,128)S(1)}, f32[23,8,128]{2,1,0:T(8,128)S(1)}, u32[]{:S(2)}, u32[]{:S(2)}) collective-permute-start(f32[23,8,128]{2,1,0:T(8,128)S(1)} %get-tuple-element.37.after.mine1.mine), channel_id=1, source_target_pairs={{0,8},{8,0},{1,9},{9,1},{2,10},{10,2},{3,11},{11,3},{4,12},{12,4},... | collective-permute-start | bytes 282632 | tf_op jit(solution)/shard_map/base_x/ppermute | solution.py:612
  40.6 6.9 %collective-permute-start.10 = (f32[21,8,128]{2,1,0:T(8,128)S(1)}, f32[21,8,128]{2,1,0:T(8,128)S(1)}, u32[]{:S(2)}, u32[]{:S(2)}) collective-permute-start(f32[21,8,128]{2,1,0:T(8,128)S(1)} %get-tuple-element.52), channel_id=1, source_target_pairs={{0,2},{2,4},{4,6},{6,0},{1,3},{3,5},{5,7},{7,1},{8,10},{10,12},{12... | collective-permute-start | bytes 258056 | tf_op jit(solution)/shard_map/slope_span/ppermute | solution.py:612
  40.7 7.4 %collective-permute-start.11 = (f32[21,8,128]{2,1,0:T(8,128)S(1)}, f32[21,8,128]{2,1,0:T(8,128)S(1)}, u32[]{:S(2)}, u32[]{:S(2)}) collective-permute-start(f32[21,8,128]{2,1,0:T(8,128)S(1)} %get-tuple-element.53), channel_id=1, source_target_pairs={{0,4},{2,6},{4,0},{6,2},{1,5},{3,7},{5,1},{7,3},{8,12},{10,14},{12... | collective-permute-start | bytes 258056 | tf_op jit(solution)/shard_map/slope_span/ppermute | solution.py:612
  42.6 5.5 %collective-permute-start.12 = (f32[21,8,128]{2,1,0:T(8,128)S(1)}, f32[21,8,128]{2,1,0:T(8,128)S(1)}, u32[]{:S(2)}, u32[]{:S(2)}) collective-permute-start(f32[21,8,128]{2,1,0:T(8,128)S(1)} %get-tuple-element.54), channel_id=1, source_target_pairs={{0,6},{2,0},{4,2},{6,4},{1,7},{3,1},{5,3},{7,5},{8,14},{10,8},{12,... | collective-permute-start | bytes 258056 | tf_op jit(solution)/shard_map/slope_span/ppermute | solution.py:612
  44.6 8.8 %collective-permute-start.14 = (f32[22,8,128]{2,1,0:T(8,128)S(1)}, f32[22,8,128]{2,1,0:T(8,128)S(1)}, u32[]{:S(2)}, u32[]{:S(2)}) collective-permute-start(f32[22,8,128]{2,1,0:T(8,128)S(1)} %last_base.1.refs_0_), channel_id=1, source_target_pairs={{0,2},{2,4},{4,6},{6,0},{1,3},{3,5},{5,7},{7,1},{8,10},{10,12},{12... | collective-permute-start | bytes 270344 | tf_op jit(solution)/shard_map/base_spread/ppermute | solution.py:612
  44.7 8.8 %collective-permute-start.15 = (f32[22,8,128]{2,1,0:T(8,128)S(1)}, f32[22,8,128]{2,1,0:T(8,128)S(1)}, u32[]{:S(2)}, u32[]{:S(2)}) collective-permute-start(f32[22,8,128]{2,1,0:T(8,128)S(1)} %last_base.1.refs_0_), channel_id=1, source_target_pairs={{0,4},{2,6},{4,0},{6,2},{1,5},{3,7},{5,1},{7,3},{8,12},{10,14},{12... | collective-permute-start | bytes 270344 | tf_op jit(solution)/shard_map/base_spread/ppermute | solution.py:612
  47.5 6.0 %collective-permute-start.16 = (f32[22,8,128]{2,1,0:T(8,128)S(1)}, f32[22,8,128]{2,1,0:T(8,128)S(1)}, u32[]{:S(2)}, u32[]{:S(2)}) collective-permute-start(f32[22,8,128]{2,1,0:T(8,128)S(1)} %last_base.1.refs_0_), channel_id=1, source_target_pairs={{0,6},{2,0},{4,2},{6,4},{1,7},{3,1},{5,3},{7,5},{8,14},{10,8},{12,... | collective-permute-start | bytes 270344 | tf_op jit(solution)/shard_map/base_spread/ppermute | solution.py:612
  48.4 4.9 %collective-permute-start.13 = (f32[21,8,128]{2,1,0:T(8,128)S(1)}, f32[21,8,128]{2,1,0:T(8,128)S(1)}, u32[]{:S(2)}, u32[]{:S(2)}) collective-permute-start(f32[21,8,128]{2,1,0:T(8,128)S(1)} %span_slope.1.mine2), channel_id=1, source_target_pairs={{0,8},{8,0},{1,9},{9,1},{2,10},{10,2},{3,11},{11,3},{4,12},{12,4},... | collective-permute-start | bytes 258056 | tf_op jit(solution)/shard_map/slope_x/ppermute | solution.py:612
  53.6 12.3 %collective-permute-start.17 = (f32[22,32,128]{2,1,0:T(8,128)S(1)}, f32[22,32,128]{2,1,0:T(8,128)S(1)}, u32[]{:S(2)}, u32[]{:S(2)}) collective-permute-start(f32[22,32,128]{2,1,0:T(8,128)S(1)} %gather.1.refs_0_), channel_id=1, source_target_pairs={{0,1},{1,0},{2,3},{3,2},{4,5},{5,4},{6,7},{7,6},{8,9},{9,8},{10,11... | collective-permute-start | bytes 1081352 | tf_op jit(solution)/shard_map/base_spread/ppermute | solution.py:612
  56.6 5.5 %collective-permute-start.18 = (f32[18,8,128]{2,1,0:T(8,128)S(1)}, f32[18,8,128]{2,1,0:T(8,128)S(1)}, u32[]{:S(2)}, u32[]{:S(2)}) collective-permute-start(f32[18,8,128]{2,1,0:T(8,128)S(1)} %last_slope.1.after.refs_2_), channel_id=1, source_target_pairs={{0,4},{2,6},{4,0},{6,2},{1,5},{3,7},{5,1},{7,3},{8,12},{10,14},{12... | collective-permute-start | bytes 221192 | tf_op jit(solution)/shard_map/slope_spread/ppermute | solution.py:612
  58.5 5.0 %collective-permute-start.19 = (f32[18,8,128]{2,1,0:T(8,128)S(1)}, f32[18,8,128]{2,1,0:T(8,128)S(1)}, u32[]{:S(2)}, u32[]{:S(2)}) collective-permute-start(f32[18,8,128]{2,1,0:T(8,128)S(1)} %last_slope.1.after.refs_2_), channel_id=1, source_target_pairs={{0,2},{2,4},{4,6},{6,0},{1,3},{3,5},{5,7},{7,1},{8,10},{10,12},{12... | collective-permute-start | bytes 221192 | tf_op jit(solution)/shard_map/slope_spread/ppermute | solution.py:612
  59.0 5.6 %collective-permute-start.20 = (f32[18,8,128]{2,1,0:T(8,128)S(1)}, f32[18,8,128]{2,1,0:T(8,128)S(1)}, u32[]{:S(2)}, u32[]{:S(2)}) collective-permute-start(f32[18,8,128]{2,1,0:T(8,128)S(1)} %last_slope.1.after.refs_2_), channel_id=1, source_target_pairs={{0,6},{2,0},{4,2},{6,4},{1,7},{3,1},{5,3},{7,5},{8,14},{10,8},{12,... | collective-permute-start | bytes 221192 | tf_op jit(solution)/shard_map/slope_spread/ppermute | solution.py:612
  61.2 3.4 %collective-permute-start.21 = (f32[18,8,128]{2,1,0:T(8,128)S(1)}, f32[18,8,128]{2,1,0:T(8,128)S(1)}, u32[]{:S(2)}, u32[]{:S(2)}) collective-permute-start(f32[18,8,128]{2,1,0:T(8,128)S(1)} %last_slope.1.after.refs_2_), channel_id=1, source_target_pairs={{0,1},{1,0},{2,3},{3,2},{4,5},{5,4},{6,7},{7,6},{8,9},{9,8},{10,11... | collective-permute-start | bytes 221192 | tf_op jit(solution)/shard_map/slope_spread/ppermute | solution.py:612
  62.1 2.5 %collective-permute-start.22 = (f32[18,8,128]{2,1,0:T(8,128)S(1)}, f32[18,8,128]{2,1,0:T(8,128)S(1)}, u32[]{:S(2)}, u32[]{:S(2)}) collective-permute-start(f32[18,8,128]{2,1,0:T(8,128)S(1)} %collective-permute-done.18.refs_3_), channel_id=1, source_target_pairs={{0,1},{1,0},{2,3},{3,2},{4,5},{5,4},{6,7},{7,6},{8,9},{9,8},{10,11... | collective-permute-start | bytes 221192 | tf_op jit(solution)/shard_map/slope_spread/ppermute | solution.py:612
  63.5 2.0 %collective-permute-start.23 = (f32[18,8,128]{2,1,0:T(8,128)S(1)}, f32[18,8,128]{2,1,0:T(8,128)S(1)}, u32[]{:S(2)}, u32[]{:S(2)}) collective-permute-start(f32[18,8,128]{2,1,0:T(8,128)S(1)} %collective-permute-done.19.refs_4_), channel_id=1, source_target_pairs={{0,1},{1,0},{2,3},{3,2},{4,5},{5,4},{6,7},{7,6},{8,9},{9,8},{10,11... | collective-permute-start | bytes 221192 | tf_op jit(solution)/shard_map/slope_spread/ppermute | solution.py:612
  64.6 1.3 %collective-permute-start.24 = (f32[18,8,128]{2,1,0:T(8,128)S(1)}, f32[18,8,128]{2,1,0:T(8,128)S(1)}, u32[]{:S(2)}, u32[]{:S(2)}) collective-permute-start(f32[18,8,128]{2,1,0:T(8,128)S(1)} %collective-permute-done.20.refs_5_), channel_id=1, source_target_pairs={{0,1},{1,0},{2,3},{3,2},{4,5},{5,4},{6,7},{7,6},{8,9},{9,8},{10,11... | collective-permute-start | bytes 221192 | tf_op jit(solution)/shard_map/slope_spread/ppermute | solution.py:612

commit v8 on v7

--- a/solution.py
+++ b/solution.py
@@ -631,7 +631,7 @@
     one_piece, two_piece = (FIRST, rows, ny), (STATE - FIRST, rows, ny)
 
     def along_z(own, up, down, far):
-        return [own, send(up, "z", 1), send(far, "z", 2), send(down, "z", -1)]
+        return [own, send(far, "z", 2), send(up, "z", 1), send(down, "z", -1)]
 
     def spread(done):
         return [done] + [send(done, "z", k) for k in (1, 2, 3)]

time: 67.9 us -> 67.2 us (0.990)
  no operation moved by 1% of the time
where the time goes in v8:
time: 67.2 us; the launch traced here: 66.9 us
  starting transfers between devices  38.9 us (58%)
  Pallas kernels  22.2 us (33%)
  waiting for transfers between devices  5.45 us (8%)
    ppermute x23, starting transfers between devices, send(): lax.ppermute(value, axis, [(i, (i + step) % size) for i in range(size)])  32.8 us
    pallas_call x1, Pallas kernels, inner_moments(): pl.pallas_call(inner_kernel, in_specs=[vm] * 5 + [pl.BlockSpec(memory_spa...  10.1 us
    ppermute x23, waiting for transfers between devices, send(): lax.ppermute(value, axis, [(i, (i + step) % size) for i in range(size)])  5.45 us
    pallas_call x1, Pallas kernels, base_moments(): pl.pallas_call(base_kernel, in_specs=[vm], out_specs=[vm] * 4, out_shape=...  4.54 us
    ppermute x1, starting transfers between devices, shards(): xl = lax.ppermute(xl, GXA, up)  3.11 us
    ppermute x1, starting transfers between devices, shards(): xr = lax.ppermute(xr, GXA, down)  3.06 us
    pallas_call x1, Pallas kernels, y_slopes(): pl.pallas_call(y_kernel, in_specs=[vm, vm], out_specs=[vm, vm], out_shape...  2.98 us
    pallas_call x1, Pallas kernels, cut(): pl.pallas_call(kernel, in_specs=[pl.BlockSpec(memory_space=pltpu.HBM)] +...  1.64 us
  transfers between devices with their start and end apart: 25, of which 5 were waited for; matrix products, arithmetic and copies ran while one was open for 0% of the time, Pallas kernels for 28%

profile of v8, /device:TPU:9, one launch (start us, length us, event | category | flops | bytes accessed | tf_op | source)
XLA Modules:
  0.0 66.9 jit_solution(14751356878558537095)
XLA Ops:
  0.0 1.6 %rims.1 = (f32[3,64,4,128]{3,2,1,0:T(4,128)S(1)}, f32[3,64,4,128]{3,2,1,0:T(4,128)S(1)}, f32[4,4,64,128]{3,2,1,0:T(8,128)S(1)}, f32[4,4,64,128]{3,2,1,0:T(8,128)S(1)}) custom-call(f32[4,64,64,128]{3,2,1,0:T(8,128)} %flow.1), custom_call_target="tpu_custom_call" | custom-call | tf_op jit(solution)/shard_map/rims/pallas_call | solution.py:102
  1.7 2.3 %collective-permute-start.5 = (f32[3,64,4,128]{3,2,1,0:T(4,128)S(1)}, f32[3,64,4,128]{3,2,1,0:T(4,128)S(1)}, u32[]{:S(2)}, u32[]{:S(2)}) collective-permute-start(f32[3,64,4,128]{3,2,1,0:T(4,128)S(1)} %get-tuple-element.40), channel_id=1, source_target_pairs={{0,1},{1,2},{2,3},{3,4},{4,5},{5,6},{6,7},{7,8},{8,9},{9,10},{10,1... | collective-permute-start | bytes 1179656 | tf_op jit(solution)/shard_map/rim_exchange/ppermute | solution.py:612
  3.9 0.0 collective-permute-start.6
  3.9 3.1 %collective-permute-start.7 = (f32[4,4,64,128]{3,2,1,0:T(8,128)S(1)}, f32[4,4,64,128]{3,2,1,0:T(8,128)S(1)}, u32[]{:S(2)}, u32[]{:S(2)}) collective-permute-start(f32[4,4,64,128]{3,2,1,0:T(8,128)S(1)} %get-tuple-element.46), channel_id=1, source_target_pairs={{0,16},{16,32},{32,48},{48,64},{64,80},{80,96},{96,112},{1,17},{17... | collective-permute-start | bytes 1572872 | tf_op jit(solution)/shard_map/rim_exchange/ppermute | solution.py:626
  7.0 3.1 %collective-permute-start.8 = (f32[4,4,64,128]{3,2,1,0:T(8,128)S(1)}, f32[4,4,64,128]{3,2,1,0:T(8,128)S(1)}, u32[]{:S(2)}, u32[]{:S(2)}) collective-permute-start(f32[4,4,64,128]{3,2,1,0:T(8,128)S(1)} %get-tuple-element.47), channel_id=1, source_target_pairs={{16,0},{32,16},{48,32},{64,48},{80,64},{96,80},{112,96},{17,1},{33... | collective-permute-start | bytes 1572872 | tf_op jit(solution)/shard_map/rim_exchange/ppermute | solution.py:627
  10.1 4.5 %base_moments.1 = (f32[4,72,80,128]{3,2,1,0:T(8,128)S(1)}, f32[4,64,128]{2,1,0:T(8,128)S(1)}, f32[23,32,128]{2,1,0:T(8,128)S(1)}, f32[23,32,128]{2,1,0:T(8,128)S(1)}) custom-call(f32[4,64,64,128]{3,2,1,0:T(8,128)S(1)} %copy-done), custom_call_target="tpu_custom_call" | custom-call | flops 1000 | bytes 1000 | tf_op jit(solution)/shard_map/base_moments/pallas_call | solution.py:200
  14.7 5.1 %collective-permute-start = (f32[23,32,128]{2,1,0:T(8,128)S(1)}, f32[23,32,128]{2,1,0:T(8,128)S(1)}, u32[]{:S(2)}, u32[]{:S(2)}) collective-permute-start(f32[23,32,128]{2,1,0:T(8,128)S(1)} %get-tuple-element.32), channel_id=1, source_target_pairs={{0,1},{1,0},{2,3},{3,2},{4,5},{5,4},{6,7},{7,6},{8,9},{9,8},{10,11... | collective-permute-start | bytes 1130504 | tf_op jit(solution)/shard_map/base_core/ppermute | solution.py:612
  19.8 3.0 %y_slopes.1 = (f32[4,64,64,128]{3,2,1,0:T(8,128)S(1)}, f32[128,128]{1,0:T(8,128)S(1)}) custom-call(f32[4,72,80,128]{3,2,1,0:T(8,128)S(1)} %get-tuple-element.38.pad.pad_in, f32[128,128]{1,0:T(8,128)S(1)} %copy-done.1), custom_call_target="tpu_custom_call" | custom-call | flops 1000 | bytes 1000 | tf_op jit(solution)/shard_map/y_slopes/pallas_call | solution.py:218
  22.8 0.1 core_base.1
  22.9 0.1 collective-permute-start.1
  23.0 0.0 collective-permute-done.5.zl
  23.0 0.1 collective-permute-start.2
  23.1 2.7 %collective-permute-start.3 = (f32[23,8,128]{2,1,0:T(8,128)S(1)}, f32[23,8,128]{2,1,0:T(8,128)S(1)}, u32[]{:S(2)}, u32[]{:S(2)}) collective-permute-start(f32[23,8,128]{2,1,0:T(8,128)S(1)} %get-tuple-element.36), channel_id=1, source_target_pairs={{0,6},{2,0},{4,2},{6,4},{1,7},{3,1},{5,3},{7,5},{8,14},{10,8},{12,... | collective-permute-start | bytes 282632 | tf_op jit(solution)/shard_map/base_span/ppermute | solution.py:612
  25.8 10.1 %inner_moments.1 = (f32[4,72,80,128]{3,2,1,0:T(8,128)S(1)}, f32[21,32,128]{2,1,0:T(8,128)S(1)}, f32[21,32,128]{2,1,0:T(8,128)S(1)}) custom-call(f32[4,72,80,128]{3,2,1,0:T(8,128)S(1)} %get-tuple-element.38.pad.pad_in, f32[4,64,64,128]{3,2,1,0:T(8,128)S(1)} %get-tuple-element.39.ysl, ...), custom_call_target="tpu_custom_call", output_to_operand_aliasing={{0}: (0, {})} | custom-call | flops 1500000000 | bytes 84000000 | tf_op jit(solution)/shard_map/inner_moments/pallas_call | solution.py:370
  35.9 0.0 collective-permute-done.2.two.refs_2_
  35.9 0.0 collective-permute-done.3.three.refs_3_
  35.9 0.1 span_base.1
  36.0 0.0 collective-permute-done.7.xl
  36.0 0.0 collective-permute-done.8.xr
  36.0 0.9 %edge_moments.1 = (f32[4,72,80,128]{3,2,1,0:T(8,128)S(1)}, f32[21,32,128]{2,1,0:T(8,128)S(1)}, f32[21,32,128]{2,1,0:T(8,128)S(1)}) custom-call(f32[4,72,80,128]{3,2,1,0:T(8,128)S(1)} %get-tuple-element.43.pad_in, f32[21,32,128]{2,1,0:T(8,128)S(1)} %get-tuple-element.44.keep_in, ...), custom_call_target="tpu_custom_call", output_to_operand_aliasing={{0}: (0, {}), {1}: (1, {}), {2}: (2, {})} | custom-call | flops 52428800 | bytes 1048576 | tf_op jit(solution)/shard_map/edge_moments/pallas_call | solution.py:444
  36.9 0.7 %collective-permute-start.9 = (f32[21,32,128]{2,1,0:T(8,128)S(1)}, f32[21,32,128]{2,1,0:T(8,128)S(1)}, u32[]{:S(2)}, u32[]{:S(2)}) collective-permute-start(f32[21,32,128]{2,1,0:T(8,128)S(1)} %get-tuple-element.49), channel_id=1, source_target_pairs={{0,1},{1,0},{2,3},{3,2},{4,5},{5,4},{6,7},{7,6},{8,9},{9,8},{10,11... | collective-permute-start | bytes 1032200 | tf_op jit(solution)/shard_map/slope_core/ppermute | solution.py:612
  37.6 2.8 %collective-permute-start.4 = (f32[23,8,128]{2,1,0:T(8,128)S(1)}, f32[23,8,128]{2,1,0:T(8,128)S(1)}, u32[]{:S(2)}, u32[]{:S(2)}) collective-permute-start(f32[23,8,128]{2,1,0:T(8,128)S(1)} %get-tuple-element.37.after.mine1.mine), channel_id=1, source_target_pairs={{0,8},{8,0},{1,9},{9,1},{2,10},{10,2},{3,11},{11,3},{4,12},{12,4},... | collective-permute-start | bytes 282632 | tf_op jit(solution)/shard_map/base_x/ppermute | solution.py:612
  40.3 0.2 core_slope.1
  40.6 1.4 %collective-permute-start.10 = (f32[21,8,128]{2,1,0:T(8,128)S(1)}, f32[21,8,128]{2,1,0:T(8,128)S(1)}, u32[]{:S(2)}, u32[]{:S(2)}) collective-permute-start(f32[21,8,128]{2,1,0:T(8,128)S(1)} %get-tuple-element.52), channel_id=1, source_target_pairs={{0,4},{2,6},{4,0},{6,2},{1,5},{3,7},{5,1},{7,3},{8,12},{10,14},{12... | collective-permute-start | bytes 258056 | tf_op jit(solution)/shard_map/slope_span/ppermute | solution.py:612
  41.9 0.0 collective-permute-start.11
  41.9 2.7 %collective-permute-start.12 = (f32[21,8,128]{2,1,0:T(8,128)S(1)}, f32[21,8,128]{2,1,0:T(8,128)S(1)}, u32[]{:S(2)}, u32[]{:S(2)}) collective-permute-start(f32[21,8,128]{2,1,0:T(8,128)S(1)} %get-tuple-element.54), channel_id=1, source_target_pairs={{0,6},{2,0},{4,2},{6,4},{1,7},{3,1},{5,3},{7,5},{8,14},{10,8},{12,... | collective-permute-start | bytes 258056 | tf_op jit(solution)/shard_map/slope_span/ppermute | solution.py:612
  44.6 0.1 collective-permute-start.14
  44.7 1.2 %collective-permute-start.15 = (f32[22,8,128]{2,1,0:T(8,128)S(1)}, f32[22,8,128]{2,1,0:T(8,128)S(1)}, u32[]{:S(2)}, u32[]{:S(2)}) collective-permute-start(f32[22,8,128]{2,1,0:T(8,128)S(1)} %last_base.1.refs_0_), channel_id=1, source_target_pairs={{0,4},{2,6},{4,0},{6,2},{1,5},{3,7},{5,1},{7,3},{8,12},{10,14},{12... | collective-permute-start | bytes 270344 | tf_op jit(solution)/shard_map/base_spread/ppermute | solution.py:612
  45.9 0.0 collective-permute-done.10.refs_5_
  45.9 1.5 %collective-permute-start.16 = (f32[22,8,128]{2,1,0:T(8,128)S(1)}, f32[22,8,128]{2,1,0:T(8,128)S(1)}, u32[]{:S(2)}, u32[]{:S(2)}) collective-permute-start(f32[22,8,128]{2,1,0:T(8,128)S(1)} %last_base.1.refs_0_), channel_id=1, source_target_pairs={{0,6},{2,0},{4,2},{6,4},{1,7},{3,1},{5,3},{7,5},{8,14},{10,8},{12,... | collective-permute-start | bytes 270344 | tf_op jit(solution)/shard_map/base_spread/ppermute | solution.py:612
  47.5 0.6 collective-permute-done.11.refs_6_
  48.0 0.0 collective-permute-done.12.refs_7_
  48.0 0.3 span_slope.1.mine2
  48.3 1.6 %collective-permute-start.13 = (f32[21,8,128]{2,1,0:T(8,128)S(1)}, f32[21,8,128]{2,1,0:T(8,128)S(1)}, u32[]{:S(2)}, u32[]{:S(2)}) collective-permute-start(f32[21,8,128]{2,1,0:T(8,128)S(1)} %span_slope.1.mine2), channel_id=1, source_target_pairs={{0,8},{8,0},{1,9},{9,1},{2,10},{10,2},{3,11},{11,3},{4,12},{12,4},... | collective-permute-start | bytes 258056 | tf_op jit(solution)/shard_map/slope_x/ppermute | solution.py:612
  49.9 3.3 %collective-permute-done.13.other2 = f32[21,8,128]{2,1,0:T(8,128)S(1)} collective-permute-done((f32[21,8,128]{2,1,0:T(8,128)S(1)}, f32[21,8,128]{2,1,0:T(8,128)S(1)}, u32[]{:S(2)}, u32[]{:S(2)}) %collective-permute-start.13) | collective-permute-done | bytes 86048 | tf_op jit(solution)/shard_map/slope_x/ppermute | solution.py:612
  53.2 0.2 last_slope.1.after.refs_2_
  53.5 0.1 gather.1.refs_0_
  53.5 2.5 %collective-permute-start.17 = (f32[22,32,128]{2,1,0:T(8,128)S(1)}, f32[22,32,128]{2,1,0:T(8,128)S(1)}, u32[]{:S(2)}, u32[]{:S(2)}) collective-permute-start(f32[22,32,128]{2,1,0:T(8,128)S(1)} %gather.1.refs_0_), channel_id=1, source_target_pairs={{0,1},{1,0},{2,3},{3,2},{4,5},{5,4},{6,7},{7,6},{8,9},{9,8},{10,11... | collective-permute-start | bytes 1081352 | tf_op jit(solution)/shard_map/base_spread/ppermute | solution.py:612
  56.0 2.5 %collective-permute-start.18 = (f32[18,8,128]{2,1,0:T(8,128)S(1)}, f32[18,8,128]{2,1,0:T(8,128)S(1)}, u32[]{:S(2)}, u32[]{:S(2)}) collective-permute-start(f32[18,8,128]{2,1,0:T(8,128)S(1)} %last_slope.1.after.refs_2_), channel_id=1, source_target_pairs={{0,4},{2,6},{4,0},{6,2},{1,5},{3,7},{5,1},{7,3},{8,12},{10,14},{12... | collective-permute-start | bytes 221192 | tf_op jit(solution)/shard_map/slope_spread/ppermute | solution.py:612
  58.5 2.7 %collective-permute-start.20 = (f32[18,8,128]{2,1,0:T(8,128)S(1)}, f32[18,8,128]{2,1,0:T(8,128)S(1)}, u32[]{:S(2)}, u32[]{:S(2)}) collective-permute-start(f32[18,8,128]{2,1,0:T(8,128)S(1)} %last_slope.1.after.refs_2_), channel_id=1, source_target_pairs={{0,6},{2,0},{4,2},{6,4},{1,7},{3,1},{5,3},{7,5},{8,14},{10,8},{12,... | collective-permute-start | bytes 221192 | tf_op jit(solution)/shard_map/slope_spread/ppermute | solution.py:612
  61.2 0.9 %collective-permute-start.21 = (f32[18,8,128]{2,1,0:T(8,128)S(1)}, f32[18,8,128]{2,1,0:T(8,128)S(1)}, u32[]{:S(2)}, u32[]{:S(2)}) collective-permute-start(f32[18,8,128]{2,1,0:T(8,128)S(1)} %last_slope.1.after.refs_2_), channel_id=1, source_target_pairs={{0,1},{1,0},{2,3},{3,2},{4,5},{5,4},{6,7},{7,6},{8,9},{9,8},{10,11... | collective-permute-start | bytes 221192 | tf_op jit(solution)/shard_map/slope_spread/ppermute | solution.py:612
  62.1 0.6 collective-permute-start.22
  62.7 0.2 collective-permute-done.19.refs_4_
  63.0 1.5 %collective-permute-start.23 = (f32[18,8,128]{2,1,0:T(8,128)S(1)}, f32[18,8,128]{2,1,0:T(8,128)S(1)}, u32[]{:S(2)}, u32[]{:S(2)}) collective-permute-start(f32[18,8,128]{2,1,0:T(8,128)S(1)} %collective-permute-done.19.refs_4_), channel_id=1, source_target_pairs={{0,1},{1,0},{2,3},{3,2},{4,5},{5,4},{6,7},{7,6},{8,9},{9,8},{10,11... | collective-permute-start | bytes 221192 | tf_op jit(solution)/shard_map/slope_spread/ppermute | solution.py:612
  64.5 0.0 collective-permute-start.24
  64.5 0.9 %collective-permute-done.23.refs_8_ = f32[18,8,128]{2,1,0:T(8,128)S(1)} collective-permute-done((f32[18,8,128]{2,1,0:T(8,128)S(1)}, f32[18,8,128]{2,1,0:T(8,128)S(1)}, u32[]{:S(2)}, u32[]{:S(2)}) %collective-permute-start.23) | collective-permute-done | bytes 73760 | tf_op jit(solution)/shard_map/slope_spread/ppermute | solution.py:612
  65.4 0.4 collective-permute-done.24.refs_9_
  65.7 1.1 %place.1 = f32[40,64,128]{2,1,0:T(8,128)} custom-call(f32[22,32,128]{2,1,0:T(8,128)S(1)} %gather.1.refs_0_, f32[22,32,128]{2,1,0:T(8,128)S(1)} %collective-permute-done.17.refs_1_, f32[18,8,128]{2,1,0:T(8,128)S(1)} %last_slope.1.after.refs_2_, f32[18,8,128]{2,1,0:T(8,128)S(1)} %collective-permute-done.18.refs_3_, ...), custom_call_target="tpu_custom_call" | custom-call | tf_op jit(solution)/shard_map/place/pallas_call | solution.py:585
  (19 shorter events, 0.1 us)
Async XLA Ops:
  0.0 10.1 %copy-start = (f32[4,64,64,128]{3,2,1,0:T(8,128)S(1)}, f32[4,64,64,128]{3,2,1,0:T(8,128)}, u32[]{:S(2)}) copy-start(f32[4,64,64,128]{3,2,1,0:T(8,128)} %flow.1) | copy-start | bytes 25165828
  0.0 19.8 %copy-start.1 = (f32[128,128]{1,0:T(8,128)S(1)}, f32[128,128]{1,0:T(8,128)}, u32[]{:S(2)}) copy-start(f32[128,128]{1,0:T(8,128)} %dy.1) | copy-start | bytes 196612
  1.7 21.4 %collective-permute-start.5 = (f32[3,64,4,128]{3,2,1,0:T(4,128)S(1)}, f32[3,64,4,128]{3,2,1,0:T(4,128)S(1)}, u32[]{:S(2)}, u32[]{:S(2)}) collective-permute-start(f32[3,64,4,128]{3,2,1,0:T(4,128)S(1)} %get-tuple-element.40), channel_id=1, source_target_pairs={{0,1},{1,2},{2,3},{3,4},{4,5},{5,6},{6,7},{7,8},{8,9},{9,10},{10,1... | collective-permute-start | bytes 1179656 | tf_op jit(solution)/shard_map/rim_exchange/ppermute | solution.py:612
  3.9 19.2 %collective-permute-start.6 = (f32[3,64,4,128]{3,2,1,0:T(4,128)S(1)}, f32[3,64,4,128]{3,2,1,0:T(4,128)S(1)}, u32[]{:S(2)}, u32[]{:S(2)}) collective-permute-start(f32[3,64,4,128]{3,2,1,0:T(4,128)S(1)} %get-tuple-element.41), channel_id=1, source_target_pairs={{0,15},{1,0},{2,1},{3,2},{4,3},{5,4},{6,5},{7,6},{8,7},{9,8},{10,9... | collective-permute-start | bytes 1179656 | tf_op jit(solution)/shard_map/rim_exchange/ppermute | solution.py:612
  3.9 32.1 %collective-permute-start.7 = (f32[4,4,64,128]{3,2,1,0:T(8,128)S(1)}, f32[4,4,64,128]{3,2,1,0:T(8,128)S(1)}, u32[]{:S(2)}, u32[]{:S(2)}) collective-permute-start(f32[4,4,64,128]{3,2,1,0:T(8,128)S(1)} %get-tuple-element.46), channel_id=1, source_target_pairs={{0,16},{16,32},{32,48},{48,64},{64,80},{80,96},{96,112},{1,17},{17... | collective-permute-start | bytes 1572872 | tf_op jit(solution)/shard_map/rim_exchange/ppermute | solution.py:626
  7.0 29.0 %collective-permute-start.8 = (f32[4,4,64,128]{3,2,1,0:T(8,128)S(1)}, f32[4,4,64,128]{3,2,1,0:T(8,128)S(1)}, u32[]{:S(2)}, u32[]{:S(2)}) collective-permute-start(f32[4,4,64,128]{3,2,1,0:T(8,128)S(1)} %get-tuple-element.47), channel_id=1, source_target_pairs={{16,0},{32,16},{48,32},{64,48},{80,64},{96,80},{112,96},{17,1},{33... | collective-permute-start | bytes 1572872 | tf_op jit(solution)/shard_map/rim_exchange/ppermute | solution.py:627
  14.7 8.1 %collective-permute-start = (f32[23,32,128]{2,1,0:T(8,128)S(1)}, f32[23,32,128]{2,1,0:T(8,128)S(1)}, u32[]{:S(2)}, u32[]{:S(2)}) collective-permute-start(f32[23,32,128]{2,1,0:T(8,128)S(1)} %get-tuple-element.32), channel_id=1, source_target_pairs={{0,1},{1,0},{2,3},{3,2},{4,5},{5,4},{6,7},{7,6},{8,9},{9,8},{10,11... | collective-permute-start | bytes 1130504 | tf_op jit(solution)/shard_map/base_core/ppermute | solution.py:612
  22.9 13.0 %collective-permute-start.1 = (f32[23,8,128]{2,1,0:T(8,128)S(1)}, f32[23,8,128]{2,1,0:T(8,128)S(1)}, u32[]{:S(2)}, u32[]{:S(2)}) collective-permute-start(f32[23,8,128]{2,1,0:T(8,128)S(1)} %get-tuple-element.34), channel_id=1, source_target_pairs={{0,4},{2,6},{4,0},{6,2},{1,5},{3,7},{5,1},{7,3},{8,12},{10,14},{12... | collective-permute-start | bytes 282632 | tf_op jit(solution)/shard_map/base_span/ppermute | solution.py:612
  23.0 12.9 %collective-permute-start.2 = (f32[23,8,128]{2,1,0:T(8,128)S(1)}, f32[23,8,128]{2,1,0:T(8,128)S(1)}, u32[]{:S(2)}, u32[]{:S(2)}) collective-permute-start(f32[23,8,128]{2,1,0:T(8,128)S(1)} %get-tuple-element.35), channel_id=1, source_target_pairs={{0,2},{2,4},{4,6},{6,0},{1,3},{3,5},{5,7},{7,1},{8,10},{10,12},{12... | collective-permute-start | bytes 282632 | tf_op jit(solution)/shard_map/base_span/ppermute | solution.py:612
  23.1 12.8 %collective-permute-start.3 = (f32[23,8,128]{2,1,0:T(8,128)S(1)}, f32[23,8,128]{2,1,0:T(8,128)S(1)}, u32[]{:S(2)}, u32[]{:S(2)}) collective-permute-start(f32[23,8,128]{2,1,0:T(8,128)S(1)} %get-tuple-element.36), channel_id=1, source_target_pairs={{0,6},{2,0},{4,2},{6,4},{1,7},{3,1},{5,3},{7,5},{8,14},{10,8},{12,... | collective-permute-start | bytes 282632 | tf_op jit(solution)/shard_map/base_span/ppermute | solution.py:612
  36.9 3.4 %collective-permute-start.9 = (f32[21,32,128]{2,1,0:T(8,128)S(1)}, f32[21,32,128]{2,1,0:T(8,128)S(1)}, u32[]{:S(2)}, u32[]{:S(2)}) collective-permute-start(f32[21,32,128]{2,1,0:T(8,128)S(1)} %get-tuple-element.49), channel_id=1, source_target_pairs={{0,1},{1,0},{2,3},{3,2},{4,5},{5,4},{6,7},{7,6},{8,9},{9,8},{10,11... | collective-permute-start | bytes 1032200 | tf_op jit(solution)/shard_map/slope_core/ppermute | solution.py:612
  37.6 7.0 %collective-permute-start.4 = (f32[23,8,128]{2,1,0:T(8,128)S(1)}, f32[23,8,128]{2,1,0:T(8,128)S(1)}, u32[]{:S(2)}, u32[]{:S(2)}) collective-permute-start(f32[23,8,128]{2,1,0:T(8,128)S(1)} %get-tuple-element.37.after.mine1.mine), channel_id=1, source_target_pairs={{0,8},{8,0},{1,9},{9,1},{2,10},{10,2},{3,11},{11,3},{4,12},{12,4},... | collective-permute-start | bytes 282632 | tf_op jit(solution)/shard_map/base_x/ppermute | solution.py:612
  40.6 5.3 %collective-permute-start.10 = (f32[21,8,128]{2,1,0:T(8,128)S(1)}, f32[21,8,128]{2,1,0:T(8,128)S(1)}, u32[]{:S(2)}, u32[]{:S(2)}) collective-permute-start(f32[21,8,128]{2,1,0:T(8,128)S(1)} %get-tuple-element.52), channel_id=1, source_target_pairs={{0,4},{2,6},{4,0},{6,2},{1,5},{3,7},{5,1},{7,3},{8,12},{10,14},{12... | collective-permute-start | bytes 258056 | tf_op jit(solution)/shard_map/slope_span/ppermute | solution.py:612
  41.9 6.1 %collective-permute-start.11 = (f32[21,8,128]{2,1,0:T(8,128)S(1)}, f32[21,8,128]{2,1,0:T(8,128)S(1)}, u32[]{:S(2)}, u32[]{:S(2)}) collective-permute-start(f32[21,8,128]{2,1,0:T(8,128)S(1)} %get-tuple-element.53), channel_id=1, source_target_pairs={{0,2},{2,4},{4,6},{6,0},{1,3},{3,5},{5,7},{7,1},{8,10},{10,12},{12... | collective-permute-start | bytes 258056 | tf_op jit(solution)/shard_map/slope_span/ppermute | solution.py:612
  41.9 6.1 %collective-permute-start.12 = (f32[21,8,128]{2,1,0:T(8,128)S(1)}, f32[21,8,128]{2,1,0:T(8,128)S(1)}, u32[]{:S(2)}, u32[]{:S(2)}) collective-permute-start(f32[21,8,128]{2,1,0:T(8,128)S(1)} %get-tuple-element.54), channel_id=1, source_target_pairs={{0,6},{2,0},{4,2},{6,4},{1,7},{3,1},{5,3},{7,5},{8,14},{10,8},{12,... | collective-permute-start | bytes 258056 | tf_op jit(solution)/shard_map/slope_span/ppermute | solution.py:612
  44.6 8.8 %collective-permute-start.14 = (f32[22,8,128]{2,1,0:T(8,128)S(1)}, f32[22,8,128]{2,1,0:T(8,128)S(1)}, u32[]{:S(2)}, u32[]{:S(2)}) collective-permute-start(f32[22,8,128]{2,1,0:T(8,128)S(1)} %last_base.1.refs_0_), channel_id=1, source_target_pairs={{0,2},{2,4},{4,6},{6,0},{1,3},{3,5},{5,7},{7,1},{8,10},{10,12},{12... | collective-permute-start | bytes 270344 | tf_op jit(solution)/shard_map/base_spread/ppermute | solution.py:612
  44.7 8.7 %collective-permute-start.15 = (f32[22,8,128]{2,1,0:T(8,128)S(1)}, f32[22,8,128]{2,1,0:T(8,128)S(1)}, u32[]{:S(2)}, u32[]{:S(2)}) collective-permute-start(f32[22,8,128]{2,1,0:T(8,128)S(1)} %last_base.1.refs_0_), channel_id=1, source_target_pairs={{0,4},{2,6},{4,0},{6,2},{1,5},{3,7},{5,1},{7,3},{8,12},{10,14},{12... | collective-permute-start | bytes 270344 | tf_op jit(solution)/shard_map/base_spread/ppermute | solution.py:612
  45.9 7.5 %collective-permute-start.16 = (f32[22,8,128]{2,1,0:T(8,128)S(1)}, f32[22,8,128]{2,1,0:T(8,128)S(1)}, u32[]{:S(2)}, u32[]{:S(2)}) collective-permute-start(f32[22,8,128]{2,1,0:T(8,128)S(1)} %last_base.1.refs_0_), channel_id=1, source_target_pairs={{0,6},{2,0},{4,2},{6,4},{1,7},{3,1},{5,3},{7,5},{8,14},{10,8},{12,... | collective-permute-start | bytes 270344 | tf_op jit(solution)/shard_map/base_spread/ppermute | solution.py:612
  48.3 4.9 %collective-permute-start.13 = (f32[21,8,128]{2,1,0:T(8,128)S(1)}, f32[21,8,128]{2,1,0:T(8,128)S(1)}, u32[]{:S(2)}, u32[]{:S(2)}) collective-permute-start(f32[21,8,128]{2,1,0:T(8,128)S(1)} %span_slope.1.mine2), channel_id=1, source_target_pairs={{0,8},{8,0},{1,9},{9,1},{2,10},{10,2},{3,11},{11,3},{4,12},{12,4},... | collective-permute-start | bytes 258056 | tf_op jit(solution)/shard_map/slope_x/ppermute | solution.py:612
  53.5 12.2 %collective-permute-start.17 = (f32[22,32,128]{2,1,0:T(8,128)S(1)}, f32[22,32,128]{2,1,0:T(8,128)S(1)}, u32[]{:S(2)}, u32[]{:S(2)}) collective-permute-start(f32[22,32,128]{2,1,0:T(8,128)S(1)} %gather.1.refs_0_), channel_id=1, source_target_pairs={{0,1},{1,0},{2,3},{3,2},{4,5},{5,4},{6,7},{7,6},{8,9},{9,8},{10,11... | collective-permute-start | bytes 1081352 | tf_op jit(solution)/shard_map/base_spread/ppermute | solution.py:612
  56.0 6.1 %collective-permute-start.18 = (f32[18,8,128]{2,1,0:T(8,128)S(1)}, f32[18,8,128]{2,1,0:T(8,128)S(1)}, u32[]{:S(2)}, u32[]{:S(2)}) collective-permute-start(f32[18,8,128]{2,1,0:T(8,128)S(1)} %last_slope.1.after.refs_2_), channel_id=1, source_target_pairs={{0,4},{2,6},{4,0},{6,2},{1,5},{3,7},{5,1},{7,3},{8,12},{10,14},{12... | collective-permute-start | bytes 221192 | tf_op jit(solution)/shard_map/slope_spread/ppermute | solution.py:612
  58.5 4.4 %collective-permute-start.19 = (f32[18,8,128]{2,1,0:T(8,128)S(1)}, f32[18,8,128]{2,1,0:T(8,128)S(1)}, u32[]{:S(2)}, u32[]{:S(2)}) collective-permute-start(f32[18,8,128]{2,1,0:T(8,128)S(1)} %last_slope.1.after.refs_2_), channel_id=1, source_target_pairs={{0,2},{2,4},{4,6},{6,0},{1,3},{3,5},{5,7},{7,1},{8,10},{10,12},{12... | collective-permute-start | bytes 221192 | tf_op jit(solution)/shard_map/slope_spread/ppermute | solution.py:612
  58.5 5.9 %collective-permute-start.20 = (f32[18,8,128]{2,1,0:T(8,128)S(1)}, f32[18,8,128]{2,1,0:T(8,128)S(1)}, u32[]{:S(2)}, u32[]{:S(2)}) collective-permute-start(f32[18,8,128]{2,1,0:T(8,128)S(1)} %last_slope.1.after.refs_2_), channel_id=1, source_target_pairs={{0,6},{2,0},{4,2},{6,4},{1,7},{3,1},{5,3},{7,5},{8,14},{10,8},{12,... | collective-permute-start | bytes 221192 | tf_op jit(solution)/shard_map/slope_spread/ppermute | solution.py:612
  61.2 3.3 %collective-permute-start.21 = (f32[18,8,128]{2,1,0:T(8,128)S(1)}, f32[18,8,128]{2,1,0:T(8,128)S(1)}, u32[]{:S(2)}, u32[]{:S(2)}) collective-permute-start(f32[18,8,128]{2,1,0:T(8,128)S(1)} %last_slope.1.after.refs_2_), channel_id=1, source_target_pairs={{0,1},{1,0},{2,3},{3,2},{4,5},{5,4},{6,7},{7,6},{8,9},{9,8},{10,11... | collective-permute-start | bytes 221192 | tf_op jit(solution)/shard_map/slope_spread/ppermute | solution.py:612
  62.1 2.3 %collective-permute-start.22 = (f32[18,8,128]{2,1,0:T(8,128)S(1)}, f32[18,8,128]{2,1,0:T(8,128)S(1)}, u32[]{:S(2)}, u32[]{:S(2)}) collective-permute-start(f32[18,8,128]{2,1,0:T(8,128)S(1)} %collective-permute-done.18.refs_3_), channel_id=1, source_target_pairs={{0,1},{1,0},{2,3},{3,2},{4,5},{5,4},{6,7},{7,6},{8,9},{9,8},{10,11... | collective-permute-start | bytes 221192 | tf_op jit(solution)/shard_map/slope_spread/ppermute | solution.py:612
  63.0 2.4 %collective-permute-start.23 = (f32[18,8,128]{2,1,0:T(8,128)S(1)}, f32[18,8,128]{2,1,0:T(8,128)S(1)}, u32[]{:S(2)}, u32[]{:S(2)}) collective-permute-start(f32[18,8,128]{2,1,0:T(8,128)S(1)} %collective-permute-done.19.refs_4_), channel_id=1, source_target_pairs={{0,1},{1,0},{2,3},{3,2},{4,5},{5,4},{6,7},{7,6},{8,9},{9,8},{10,11... | collective-permute-start | bytes 221192 | tf_op jit(solution)/shard_map/slope_spread/ppermute | solution.py:612
  64.5 1.3 %collective-permute-start.24 = (f32[18,8,128]{2,1,0:T(8,128)S(1)}, f32[18,8,128]{2,1,0:T(8,128)S(1)}, u32[]{:S(2)}, u32[]{:S(2)}) collective-permute-start(f32[18,8,128]{2,1,0:T(8,128)S(1)} %collective-permute-done.20.refs_5_), channel_id=1, source_target_pairs={{0,1},{1,0},{2,3},{3,2},{4,5},{5,4},{6,7},{7,6},{8,9},{9,8},{10,11... | collective-permute-start | bytes 221192 | tf_op jit(solution)/shard_map/slope_spread/ppermute | solution.py:612
